TPU v7x, 32 devices: a whole 2x2x4 slice. The times are simulated.
32 devices in a mesh: replica: 16 (over z, y, core), fsdp: 2 (over x).
Axes of the slice: x: 2, y: 2, z: 4, core: 2. Of those that a mesh axis runs over, the one named last changes fastest.
Arguments:
- tokens: bfloat16 [12288, 8192], P(('replica', 'fsdp')), may hold values from -6 to 6
- inner_weight: bfloat16 [16, 8192, 512], P('replica', 'fsdp'), may hold values from -0.0625 to 0.0625
- cotangent: bfloat16 [12288, 512], P(('replica', 'fsdp')), may hold values from -0.059814453 to 0.059814453
- local_weights: bfloat16 [16, 2, 8192, 896], P('replica', None, 'fsdp'), may hold values from -3 to 3
- anchor: bfloat16 [2, 2, 4096, 896], P(None, 'fsdp', 'replica'), may hold values from -1.5 to 1.5
- momentum: float32 [2, 2, 4096, 896], P(None, 'fsdp', 'replica'), may hold values from -1.5 to 1.5
Outputs:
- keys: bfloat16 [12288, 512], P(('replica', 'fsdp'))
- weight_grad: bfloat16 [16, 8192, 512], P('replica', 'fsdp')
- new_weights: bfloat16 [2, 8192, 896], P(None, 'fsdp')
- new_momentum: float32 [2, 2, 4096, 896], P(None, 'fsdp', 'replica')
All inputs are finite; a program needn't handle non-finite values.
Results may differ from a plain program's by a relative error of at most 0.017.
Values may be sent and summed in bfloat16 or wider, within the bound.
No kernel may reach another device: no remote copies, remote signals or barrier semaphores. Data moves between devices by JAX's collectives and lax.ppermute only.
A program may use at most 128 MiB of HBM per device.

v0:
```python
import jax
import jax.numpy as jnp
from jax import lax
from jax.sharding import PartitionSpec as P

outer_rate = 0.7
momentum_decay = 0.9


def outer_step(local_weights, anchor, momentum):
    workers = lax.axis_size("replica")
    local_slab = local_weights[0].astype(jnp.float32)
    summed = lax.psum_scatter(local_slab, "replica", scatter_dimension=1, tiled=True)
    average = summed / workers
    anchor_now = anchor[:, 0].astype(jnp.float32)
    pseudo_grad = anchor_now - average
    momentum_new = momentum_decay * momentum[:, 0] + pseudo_grad
    new_piece = (anchor_now - outer_rate * (pseudo_grad + momentum_decay * momentum_new)).astype(
        jnp.bfloat16
    )
    gathered = lax.all_gather(new_piece, "replica", axis=1, tiled=True)
    return (gathered, momentum_new[:, None])


def inner_pass(tokens, inner_weight, cotangent):
    weight = inner_weight[0]
    columns = tokens
    key_rows = jnp.dot(
        columns,
        lax.all_gather(weight, "fsdp", axis=0, tiled=True),
        preferred_element_type=jnp.float32,
    ).astype(jnp.bfloat16)
    columns = tokens
    grad_sum = lax.psum_scatter(
        lax.dot_general(
            columns, cotangent, (((0,), (0,)), ((), ())), preferred_element_type=jnp.float32
        ).astype(jnp.bfloat16),
        "fsdp",
        scatter_dimension=0,
        tiled=True,
    )
    return (key_rows, grad_sum[None])


def shards(tokens, inner_weight, cotangent, local_weights, anchor, momentum):
    new_weights, new_momentum = outer_step(local_weights, anchor, momentum)
    keys, weight_grad = inner_pass(tokens, inner_weight, cotangent)
    return (keys, weight_grad, new_weights, new_momentum)


def solution(mesh):
    return jax.shard_map(
        shards,
        mesh=mesh,
        in_specs=(
            P(("replica", "fsdp"), None),
            P("replica", "fsdp", None),
            P(("replica", "fsdp"), None),
            P("replica", None, "fsdp", None),
            P(None, "fsdp", "replica", None),
            P(None, "fsdp", "replica", None),
        ),
        out_specs=(
            P(("replica", "fsdp"), None),
            P("replica", "fsdp", None),
            P(None, "fsdp", None),
            P(None, "fsdp", "replica", None),
        ),
        check_vma=False,
    )
```

profile of v0, /device:TPU:0, one launch (start us, length us, event | category | flops | bytes accessed | tf_op | source)
XLA Modules:
  0.0 542.2 jit_solution(15271169910842426486)
XLA Ops:
  8.0 0.0 copy-start
  8.0 0.0 reduce-scatter.5.cloned.1.call-start
  8.1 16.4 %bitcast_convert_fusion = f32[2,4096,896]{2,1,0:T(8,128)} fusion(bf16[1,2,4096,896]{3,2,1,0:T(8,128)(2,1)} %param.9), kind=kLoop, calls=%fused_computation | loop fusion | flops 7340032 | bytes 44040192 | tf_op jit(solution)/shard_map/convert_element_type | solution.py:12
  24.4 0.0 copy-start.2
  24.4 0.0 copy-start.3
  24.4 0.0 reduce-scatter.5.cloned.1.call-update
  24.5 0.0 all-gather.6.cloned.1.call-start
  24.5 0.5 all-gather.6.cloned.1.call-update
  25.1 0.0 all-gather.4.cloned.1.call-start
  25.1 279.9 %reduce-scatter.5.cloned.1.call-done = f32[2,256,896]{2,1,0:T(8,128)} async-done(((f32[2,4096,896]{2,1,0:T(8,128)}), f32[2,256,896]{2,1,0:T(8,128)}) %reduce-scatter.5.cloned.1.call-update) | async-done | bytes 1835024 | tf_op jit(solution)/shard_map/reduce_scatter | solution.py:13
  305.0 0.0 copy-done.2
  305.0 0.0 copy-done.3
  305.1 3.7 fusion.3
  308.7 0.0 all-gather.4.cloned.1.call-update
  308.7 0.0 reduce-scatter.3.cloned.1.call-start
  308.8 0.0 copy-done
  308.8 9.6 %convolution_convert_fusion = bf16[8192,512]{1,0:T(8,128)(2,1)} fusion(bf16[384,8192]{1,0:T(8,128)(2,1)} %param.6, bf16[384,512]{1,0:T(8,128)(2,1)S(1)} %copy-done), kind=kOutput, calls=%fused_computation.1 | convolution fusion | flops 3225419776 | bytes 15073280 | tf_op jit(solution)/shard_map/dot_general | solution.py:35
  318.4 0.0 reduce-scatter.3.cloned.1.call-update
  318.4 0.0 all-gather.6.cloned.1.call-done
  318.5 9.4 %fusion.4 = bf16[384,512]{1,0:T(8,128)(2,1)} fusion(bf16[384,8192]{1,0:T(8,128)(2,1)} %param.6, bf16[1,8192,512]{2,1,0:T(8,128)(2,1)} %all-gather.6.cloned.1.call-done), kind=kOutput, calls=%fused_computation.10 | convolution fusion | flops 3221422080 | bytes 15073280 | tf_op jit(solution)/shard_map/dot_general | solution.py:28
  327.8 93.5 %all-gather.4.cloned.1.call-done = bf16[2,4096,896]{2,1,0:T(8,128)(2,1)} async-done(((bf16[2,256,896]{2,1,0:T(8,128)(2,1)}), bf16[2,4096,896]{2,1,0:T(8,128)(2,1)}) %all-gather.4.cloned.1.call-update) | async-done | bytes 14680080 | tf_op jit(solution)/shard_map/all_gather | solution.py:21
  421.4 100.1 %reduce-scatter.3.cloned.1.call-done = bf16[4096,512]{1,0:T(8,128)(2,1)} async-done(((bf16[8192,512]{1,0:T(8,128)(2,1)}), bf16[4096,512]{1,0:T(8,128)(2,1)}) %reduce-scatter.3.cloned.1.call-update) | async-done | bytes 4194320 | tf_op jit(solution)/shard_map/reduce_scatter | solution.py:34
  521.4 0.0 copy-start.1
  521.4 13.2 %copy.13 = bf16[2,4096,896]{2,1,0:T(8,128)(2,1)} copy(bf16[2,4096,896]{2,1,0:T(8,128)(2,1)} %all-gather.4.cloned.1.call-done) | data formatting | bytes 29360128
  534.6 0.0 copy-done.1
Async XLA Ops:
  8.0 300.8 %copy-start = (bf16[384,512]{1,0:T(8,128)(2,1)S(1)}, bf16[384,512]{1,0:T(8,128)(2,1)}, u32[]{:S(2)}) copy-start(bf16[384,512]{1,0:T(8,128)(2,1)} %param.8) | copy-start | bytes 1179652
  8.0 297.0 %reduce-scatter.5.cloned.1.call-start = ((), (), s32[]{:S(2)}) async-start(), calls=%async_computation.3 | async-start | bytes 31195136 | tf_op jit(solution)/shard_map/reduce_scatter | solution.py:13
  24.4 280.6 %copy-start.2 = (f32[2,1,256,896]{3,2,1,0:T(8,128)S(1)}, f32[2,1,256,896]{3,2,1,0:T(8,128)}, u32[]{:S(2)}) copy-start(f32[2,1,256,896]{3,2,1,0:T(8,128)} %param.11) | copy-start | bytes 5505028
  24.4 280.6 %copy-start.3 = (bf16[2,1,256,896]{3,2,1,0:T(8,128)(2,1)S(1)}, bf16[2,1,256,896]{3,2,1,0:T(8,128)(2,1)}, u32[]{:S(2)}) copy-start(bf16[2,1,256,896]{3,2,1,0:T(8,128)(2,1)} %param.10) | copy-start | bytes 2752516
  24.5 294.0 %all-gather.6.cloned.1.call-start = ((), (), s32[]{:S(2)}) async-start(), calls=%async_computation.5 | async-start | bytes 12582912 | tf_op jit(solution)/shard_map/all_gather | solution.py:30
  25.1 396.3 %all-gather.4.cloned.1.call-start = ((), (), s32[]{:S(2)}) async-start(), calls=%async_computation.4 | async-start | bytes 15597568 | tf_op jit(solution)/shard_map/all_gather | solution.py:21
  308.7 212.7 %reduce-scatter.3.cloned.1.call-start = ((), (), s32[]{:S(2)}) async-start(), calls=%async_computation.2 | async-start | bytes 12582912 | tf_op jit(solution)/shard_map/reduce_scatter | solution.py:34
  521.4 13.2 %copy-start.1 = (bf16[384,512]{1,0:T(8,128)(2,1)S(1)}, bf16[384,512]{1,0:T(8,128)(2,1)}, u32[]{:S(2)}) copy-start(bf16[384,512]{1,0:T(8,128)(2,1)} %param.8) | copy-start | bytes 1179652
Sparse Core Ops, SparseCore 0:
  24.6 280.4 reduce-scatter.4
Sparse Core Ops, SparseCore 1:
  26.5 106.5 all-gather.5
  308.8 112.5 all-gather.3
  424.1 97.3 reduce-scatter.2
where the time goes:
time: 543 us; the launch traced here: 542 us
  waiting for transfers between devices  474 us (87%)
  other arithmetic  20 us (4%)
  matrix products  19 us (3%)
  between operations  15.7 us (3%)
  local copies, waits for them, and re-layouts  13.2 us (2%)
    reduce_scatter x1, waiting for transfers between devices, outer_step(): lax.psum_scatter(local_slab, 'replica', scatter_dimension=1, tiled=True)  280 us
    reduce_scatter x1, waiting for transfers between devices, inner_pass(): lax.psum_scatter(lax.dot_general(columns, cotangent, (((0,), (0,)), ((),...  100 us
    all_gather x1, waiting for transfers between devices, outer_step(): gathered = lax.all_gather(new_piece, 'replica', axis=1, tiled=True)  93.5 us
    convert_element_type x1, other arithmetic, outer_step(): local_slab = local_weights[0].astype(jnp.float32)  16.4 us
    unnamed x9, local copies, waits for them, and re-layouts  13.2 us
  transfers between devices with their start and end apart: 4, of which 3 were waited for; matrix products, arithmetic and copies ran while one was open for 4% of the time, Pallas kernels for 0%

commit v1 on v0

v1 whole, which is shorter than its diff:
```python
import jax
import jax.numpy as jnp
from jax import lax
from jax.sharding import PartitionSpec as P

outer_rate = 0.7
momentum_decay = 0.9
f32 = jnp.float32
bf16 = jnp.bfloat16


def ring_chip(pos, chips):
    return jnp.where(pos < chips // 2, 2 * pos, 2 * (chips - 1 - pos) + 1)


def ring_pos(chip, chips):
    return jnp.where(chip % 2 == 0, chip // 2, chips - 1 - chip // 2)


def ring_perms(n):
    chips = n // 2
    order = [2 * p if p < chips // 2 else 2 * (chips - 1 - p) + 1 for p in range(chips)]
    fwd = [(2 * order[p] + c, 2 * order[(p + 1) % chips] + c) for p in range(chips) for c in range(2)]
    bwd = [(b, a) for a, b in fwd]
    swap = [(r, r ^ 1) for r in range(n)]
    return fwd, bwd, swap


def outer_step(local_weights, anchor, momentum):
    n = lax.axis_size("replica")
    chips = n // 2
    half = chips // 2
    rows, cols = anchor.shape[2], anchor.shape[3]
    fwd, bwd, swap = ring_perms(n)
    me = lax.axis_index("replica")
    core = me % 2
    pos = ring_pos(me // 2, chips)
    chip_at = {d: ring_chip((pos + d + chips) % chips, chips) for d in range(-half + 1, half + 1)}

    def send(x, perm):
        return lax.ppermute(x, "replica", perm)

    shards = local_weights[0].reshape(2, chips, 2, rows, cols)

    def piece(m, d, c):
        return lax.dynamic_slice(shards, (m, chip_at[d], c, 0, 0), (1, 1, 1, rows, cols)).reshape(rows, cols)

    def both(d, c):
        return lax.dynamic_slice(shards, (0, chip_at[d], c, 0, 0), (2, 1, 1, rows, cols)).reshape(2, rows, cols)

    order = [half] + [s * d for d in range(half - 1, 0, -1) for s in (1, -1)] + [0]
    theirs = {d: send(both(d, 1 - core), swap) for d in order}

    def pair(m, d):
        return piece(m, d, core).astype(f32) + theirs[d][m].astype(f32)

    state = {}
    for k in range(half):
        for first in (0, 1):
            for sign, perm in ((1, fwd), (-1, bwd)):
                lead = 0 if sign == 1 else 1
                m = lead if first == 1 else 1 - lead
                if k == 0 and m != lead:
                    continue
                d = half if k == 0 else sign * (half - k)
                total = pair(m, d)
                if (sign, m) in state:
                    total = total + state[sign, m].astype(f32)
                state[sign, m] = send(total.astype(bf16), perm)

    pieces = []
    momentum_out = []
    for m in range(2):
        summed = pair(m, 0) + state[1, m].astype(f32) + state[-1, m].astype(f32)
        average = summed / n
        anchor_now = anchor[m, 0].astype(f32)
        pseudo_grad = anchor_now - average
        momentum_new = momentum_decay * momentum[m, 0] + pseudo_grad
        pieces.append((anchor_now - outer_rate * (pseudo_grad + momentum_decay * momentum_new)).astype(bf16))
        momentum_out.append(momentum_new)

    gathered = jnp.zeros((2, chips, 2, rows, cols), bf16)

    def put(gathered, value, m, d, c):
        return lax.dynamic_update_slice(gathered, value.reshape(1, 1, 1, rows, cols), (m, chip_at[d], c, 0, 0))

    have = {(s, m): pieces[m] for s in (1, -1) for m in range(2)}
    arrived = [(m, 0, pieces[m]) for m in range(2)]
    for k in range(half):
        for first in (0, 1):
            for sign, perm in ((1, fwd), (-1, bwd)):
                lead = 0 if sign == 1 else 1
                m = lead if first == 0 else 1 - lead
                if k == half - 1 and m != lead:
                    continue
                have[sign, m] = send(have[sign, m], perm)
                d = -sign * (k + 1)
                arrived.append((m, half if d == -half else d, have[sign, m]))
    for m, d, value in arrived:
        gathered = put(gathered, value, m, d, core)
        gathered = put(gathered, send(value, swap), m, d, 1 - core)
    return gathered.reshape(2, n * rows, cols), jnp.stack(momentum_out)[:, None]


def inner_pass(tokens, inner_weight, cotangent):
    parts = lax.axis_size("fsdp")
    mine = lax.axis_index("fsdp")
    weight = inner_weight[0]
    depth = weight.shape[0]

    def columns(owner):
        return lax.dynamic_slice(tokens, (0, owner * depth), (tokens.shape[0], depth))

    def shift(x, s):
        return lax.ppermute(x, "fsdp", [(k, (k + s) % parts) for k in range(parts)])

    own = columns(mine)
    keys = jnp.dot(own, weight, preferred_element_type=f32)

    def outer_product(a, b):
        return lax.dot_general(a, b, (((0,), (0,)), ((), ())), preferred_element_type=f32)

    grad = outer_product(own, cotangent)
    for s in range(1, parts):
        other = shift(columns((mine + s) % parts), s)
        other_cotangent = shift(cotangent, s)
        partial = jnp.dot(other, weight, preferred_element_type=f32).astype(bf16)
        keys = keys + shift(partial, parts - s).astype(f32)
        grad = grad + outer_product(other, other_cotangent)
    return keys.astype(bf16), grad.astype(bf16)[None]


def shards(tokens, inner_weight, cotangent, local_weights, anchor, momentum):
    keys, weight_grad = inner_pass(tokens, inner_weight, cotangent)
    new_weights, new_momentum = outer_step(local_weights, anchor, momentum)
    return (keys, weight_grad, new_weights, new_momentum)


def solution(mesh):
    return jax.shard_map(
        shards,
        mesh=mesh,
        in_specs=(
            P(("replica", "fsdp"), None),
            P("replica", "fsdp", None),
            P(("replica", "fsdp"), None),
            P("replica", None, "fsdp", None),
            P(None, "fsdp", "replica", None),
            P(None, "fsdp", "replica", None),
        ),
        out_specs=(
            P(("replica", "fsdp"), None),
            P("replica", "fsdp", None),
            P(None, "fsdp", None),
            P(None, "fsdp", "replica", None),
        ),
        check_vma=False,
    )
```

time: 543 us -> 242 us (0.45)
  waiting for transfers between devices: 474 us -> 125 us
  starting transfers between devices: 0.17 us -> 42.3 us
  between operations: 15.7 us -> 1.33 us
  local copies, waits for them, and re-layouts: 13.2 us -> 23.9 us
    reduce_scatter x2 -> x0, waiting for transfers between devices: 380 us -> none  [the longest x1 280 us: outer_step(): lax.psum_scatter(local_slab, 'replica', scatter_dimension=1, tiled=True)]
    ppermute x0 -> x55, waiting for transfers between devices: none -> 125 us  [the longest x52 125 us: send(): return lax.ppermute(x, 'replica', perm)]
    all_gather x2 -> x0, waiting for transfers between devices: 93.5 us -> none  [the longest x1 93.5 us: outer_step(): gathered = lax.all_gather(new_piece, 'replica', axis=1, tiled=True)]
    ppermute x0 -> x55, starting transfers between devices: none -> 42.3 us  [the longest x52 39 us: send(): return lax.ppermute(x, 'replica', perm)]
    unnamed x9 -> x22, local copies, waits for them, and re-layouts: 13.2 us -> 5.51 us
    broadcast_in_dim x0 -> x1, local copies, waits for them, and re-layouts: none -> 7.56 us  [outer_step(): gathered = jnp.zeros((2, chips, 2, rows, cols), bf16)]
    dot_general x2 -> x4, matrix products: 19 us -> 24.3 us  [the longest x2 15.8 us: outer_product(): lax.dot_general(a, b, (((0,), (0,)), ((), ())), preferred_element_type=f32)]
    convert_element_type x1 -> x7, other arithmetic: 16.4 us -> 15 us  [the longest x6 14.2 us: outer_step(): state[sign, m] = send(total.astype(bf16), perm)]
  transfers between devices with their start and end apart: 4 -> 55, of which waited for: 3 -> 24; matrix products, arithmetic and copies ran while one was open for 4% -> 25% of each run, Pallas kernels for 0% -> 0%
where the time goes in v1:
time: 242 us; the launch traced here: 241 us
  waiting for transfers between devices  125 us (52%)
  starting transfers between devices  42.3 us (17%)
  matrix products  24.3 us (10%)
  other arithmetic  24 us (10%)
  local copies, waits for them, and re-layouts  23.9 us (10%)
    ppermute x52, waiting for transfers between devices, send(): return lax.ppermute(x, 'replica', perm)  125 us
    ppermute x52, starting transfers between devices, send(): return lax.ppermute(x, 'replica', perm)  39 us
    dot_general x2, matrix products, outer_product(): lax.dot_general(a, b, (((0,), (0,)), ((), ())), preferred_element_type=f32)  15.8 us
    convert_element_type x6, other arithmetic, outer_step(): state[sign, m] = send(total.astype(bf16), perm)  14.2 us
    broadcast_in_dim x1, local copies, waits for them, and re-layouts, outer_step(): gathered = jnp.zeros((2, chips, 2, rows, cols), bf16)  7.56 us
    dot_general x1, matrix products, inner_pass(): keys = jnp.dot(own, weight, preferred_element_type=f32)  5.85 us
    unnamed x22, local copies, waits for them, and re-layouts  5.51 us
    reshape x1, local copies, waits for them, and re-layouts, both(): lax.dynamic_slice(shards, (0, chip_at[d], c, 0, 0), (2, 1, 1, rows, cols))  5.41 us
  transfers between devices with their start and end apart: 55, of which 24 were waited for; matrix products, arithmetic and copies ran while one was open for 25% of the time, Pallas kernels for 0%

profile of v1, /device:TPU:0, one launch (start us, length us, event | category | flops | bytes accessed | tf_op | source)
XLA Modules:
  0.0 241.1 jit_solution(15528567357940871302)
XLA Ops:
  0.9 5.4 %dynamic-slice_bitcast_fusion.7 = (bf16[2,256,896]{2,1,0:T(8,128)(2,1)}, bf16[2,256,896]{2,1,0:T(8,128)(2,1)}, bf16[2,256,896]{2,1,0:T(8,128)(2,1)}, bf16[2,256,...) fusion(bf16[2,8,2,256,896]{4,3,2,1,0:T(8,128)(2,1)} %bitcast.28, ...), kind=kLoop, calls=%fused_computation.72 | loop fusion | bytes 14680100 | tf_op jit(solution)/shard_map/reshape | solution.py:49
  6.8 2.2 collective-permute-done.7
  9.0 2.4 %fusion.13 = (bf16[256,896]{1,0:T(8,128)(2,1)}, bf16[256,896]{1,0:T(8,128)(2,1)S(1)}) fusion(bf16[2,256,896]{2,1,0:T(8,128)(2,1)} %collective-permute-done.7, bf16[2,8,2,256,896]{4,3,2,1,0:T(8,128)(2,1)} %bitcast.282, s32[]{:T(128)S(6)} %select_n.244, s32[]{:T(128)S(6)} %select_n.117), kind=kLoop, calls=%fused_computation.18 | loop fusion | flops 1835008 | bytes 2752520 | tf_op jit(solution)/shard_map/convert_element_type | solution.py:69
  11.4 2.9 %collective-permute-start.8 = (bf16[256,896]{1,0:T(8,128)(2,1)S(1)}, bf16[256,896]{1,0:T(8,128)(2,1)S(1)}, u32[]{:S(2)}, u32[]{:S(2)}) collective-permute-start(bf16[256,896]{1,0:T(8,128)(2,1)S(1)} %get-tuple-element.23), channel_id=1, source_target_pairs={{0,8},{2,10},{8,16},{10,18},{16,24},{18,26},{24,28},{26,30},{28,20... | collective-permute-start | bytes 1376264 | tf_op jit(solution)/shard_map/ppermute | solution.py:41
  14.9 10.2 %collective-permute-done.8 = bf16[256,896]{1,0:T(8,128)(2,1)S(1)} collective-permute-done((bf16[256,896]{1,0:T(8,128)(2,1)S(1)}, bf16[256,896]{1,0:T(8,128)(2,1)S(1)}, u32[]{:S(2)}, u32[]{:S(2)}) %collective-permute-start.8) | collective-permute-done | bytes 458784 | tf_op jit(solution)/shard_map/ppermute | solution.py:41
  30.3 3.9 %constant_dynamic-slice_fusion = bf16[384,4096]{1,0:T(8,128)(2,1)} fusion(bf16[384,8192]{1,0:T(8,128)(2,1)} %param.6, s32[]{:T(128)S(6)} %select_n.108), kind=kLoop, calls=%fused_computation.125 | loop fusion | bytes 6291460 | tf_op jit(solution)/shard_map/dynamic_slice | solution.py:112
  35.7 4.7 %collective-permute-done.19 = bf16[256,896]{1,0:T(8,128)(2,1)S(1)} collective-permute-done((bf16[256,896]{1,0:T(8,128)(2,1)S(1)}, bf16[256,896]{1,0:T(8,128)(2,1)S(1)}, u32[]{:S(2)}, u32[]{:S(2)}) %collective-permute-start.19) | collective-permute-done | bytes 458784 | tf_op jit(solution)/shard_map/ppermute | solution.py:41
  42.1 6.7 %collective-permute-done.9 = bf16[256,896]{1,0:T(8,128)(2,1)S(1)} collective-permute-done((bf16[256,896]{1,0:T(8,128)(2,1)S(1)}, bf16[256,896]{1,0:T(8,128)(2,1)S(1)}, u32[]{:S(2)}, u32[]{:S(2)}) %collective-permute-start.9) | collective-permute-done | bytes 458784 | tf_op jit(solution)/shard_map/ppermute | solution.py:41
  53.7 10.4 %collective-permute-done.10 = bf16[256,896]{1,0:T(8,128)(2,1)S(1)} collective-permute-done((bf16[256,896]{1,0:T(8,128)(2,1)S(1)}, bf16[256,896]{1,0:T(8,128)(2,1)S(1)}, u32[]{:S(2)}, u32[]{:S(2)}) %collective-permute-start.10) | collective-permute-done | bytes 458784 | tf_op jit(solution)/shard_map/ppermute | solution.py:41
  64.1 7.5 %collective-permute-done.20 = bf16[256,896]{1,0:T(8,128)(2,1)S(1)} collective-permute-done((bf16[256,896]{1,0:T(8,128)(2,1)S(1)}, bf16[256,896]{1,0:T(8,128)(2,1)S(1)}, u32[]{:S(2)}, u32[]{:S(2)}) %collective-permute-start.20) | collective-permute-done | bytes 458784 | tf_op jit(solution)/shard_map/ppermute | solution.py:41
  71.6 3.7 %fusion.24 = (bf16[256,896]{1,0:T(8,128)(2,1)}, bf16[256,896]{1,0:T(8,128)(2,1)}, bf16[256,896]{1,0:T(8,128)(2,1)}, bf16[256,896]{1,0:T(8,128)(2,1)}) fusion(bf16[256,896]{1,0:T(8,128)(2,1)S(1)} %collective-permute-done.20, bf16[2,256,896]{2,1,0:T(8,128)(2,1)} %collective-permute-done.4, bf16[2,8,2,256,896]{4,3,2,1,0:T(8,128)(2,1)} %bitcast.285, ...), kind=kLoop, calls=%fused_computation.35 | loop fusion | flops 5046272 | bytes 6881292 | tf_op jit(solution)/shard_map/convert_element_type | solution.py:69
  78.4 10.6 %collective-permute-done.15 = bf16[256,896]{1,0:T(8,128)(2,1)} collective-permute-done((bf16[256,896]{1,0:T(8,128)(2,1)}, bf16[256,896]{1,0:T(8,128)(2,1)}, u32[]{:S(2)}, u32[]{:S(2)}) %collective-permute-start.15) | collective-permute-done | bytes 458784 | tf_op jit(solution)/shard_map/ppermute | solution.py:41
  89.0 6.6 %collective-permute-done.23 = bf16[256,896]{1,0:T(8,128)(2,1)} collective-permute-done((bf16[256,896]{1,0:T(8,128)(2,1)}, bf16[256,896]{1,0:T(8,128)(2,1)}, u32[]{:S(2)}, u32[]{:S(2)}) %collective-permute-start.23) | collective-permute-done | bytes 458784 | tf_op jit(solution)/shard_map/ppermute | solution.py:41
  100.1 5.9 %fusion.3 = f32[384,512]{1,0:T(8,128)} fusion(bf16[1,4096,512]{2,1,0:T(8,128)(2,1)} %param.7, bf16[384,8192]{1,0:T(8,128)(2,1)} %param.6, s32[]{:T(128)S(6)} %select_n.106), kind=kOutput, calls=%fused_computation.4 | convolution fusion | flops 1610612736 | bytes 8126468 | tf_op jit(solution)/shard_map/dot_general | solution.py:118
  105.9 7.7 %fusion.5 = f32[4096,512]{1,0:T(8,128)} fusion(bf16[384,512]{1,0:T(8,128)(2,1)} %param.8, bf16[384,8192]{1,0:T(8,128)(2,1)} %param.6, s32[]{:T(128)S(6)} %select_n.106), kind=kOutput, calls=%fused_computation.6 | convolution fusion | flops 1610612736 | bytes 11927556 | tf_op jit(solution)/shard_map/dot_general | solution.py:121
  117.4 2.5 %fusion.19 = (bf16[256,896]{1,0:T(8,128)(2,1)}, bf16[256,896]{1,0:T(8,128)(2,1)S(1)}) fusion(bf16[256,896]{1,0:T(8,128)(2,1)S(1)} %collective-permute-done.24, bf16[2,256,896]{2,1,0:T(8,128)(2,1)} %collective-permute-done.12, bf16[2,8,2,256,896]{4,3,2,1,0:T(8,128)(2,1)} %bitcast.287, s32[]{:T(128)S(6)} %select_n.247, s32[]{:T(128)S(6)} %select_n.117, ...), kind=kLoop, calls=%fused_computation.27 | loop fusion | flops 2752512 | bytes 3670024 | tf_op jit(solution)/shard_map/convert_element_type | solution.py:69
  121.4 2.6 %fusion.8 = bf16[384,512]{1,0:T(8,128)(2,1)} fusion(bf16[384,4096]{1,0:T(8,128)(2,1)S(1)} %collective-permute-done, bf16[1,4096,512]{2,1,0:T(8,128)(2,1)S(1)} %copy-done.6), kind=kOutput, calls=%fused_computation.10 | convolution fusion | flops 1610809344 | bytes 7733248 | tf_op jit(solution)/shard_map/dot_general | solution.py:127
  124.4 3.8 %collective-permute-done.11 = bf16[256,896]{1,0:T(8,128)(2,1)} collective-permute-done((bf16[256,896]{1,0:T(8,128)(2,1)S(1)}, bf16[256,896]{1,0:T(8,128)(2,1)}, u32[]{:S(2)}, u32[]{:S(2)}) %collective-permute-start.11) | collective-permute-done | bytes 458784 | tf_op jit(solution)/shard_map/ppermute | solution.py:41
  128.5 7.6 %broadcast_in_dim.10 = bf16[2,8,2,256,896]{4,3,2,1,0:T(8,128)(2,1)} broadcast(bf16[]{:T(256)} %constant.109.clone.1), dimensions={} | broadcast | bytes 14680066 | tf_op jit(solution)/shard_map/broadcast_in_dim | solution.py:82
  136.0 3.2 %bitcast_dynamic-update-slice_fusion.31 = (bf16[2,8,2,256,896]{4,3,2,1,0:T(8,128)(2,1)}, bf16[256,896]{1,0:T(8,128)(2,1)S(1)}) fusion(bf16[2,8,2,256,896]{4,3,2,1,0:T(8,128)(2,1)} %broadcast_in_dim.10, s32[]{:T(128)S(6)} %select_n.115, s32[]{:T(128)S(6)} %select_n.117, f32[2,1,256,896]{3,2,1,0:T(8,128)} %param.11, ...), kind=kLoop, calls=%fused_computation.123 | loop fusion | flops 3899392 | bytes 4128776 | tf_op jit(solution)/shard_map/dynamic_update_slice | solution.py:85
  139.4 8.2 %fusion = bf16[1,4096,512]{2,1,0:T(8,128)(2,1)} fusion(f32[4096,512]{1,0:T(8,128)} %fusion.5, bf16[384,4096]{1,0:T(8,128)(2,1)S(1)} %collective-permute-done, bf16[384,512]{1,0:T(8,128)(2,1)} %collective-permute-done.2), kind=kOutput, calls=%fused_computation.1 | convolution fusion | flops 1614807040 | bytes 16121856 | tf_op jit(solution)/shard_map/dot_general | solution.py:121
  152.1 8.8 %collective-permute-done.25 = bf16[256,896]{1,0:T(8,128)(2,1)S(1)} collective-permute-done((bf16[256,896]{1,0:T(8,128)(2,1)S(1)}, bf16[256,896]{1,0:T(8,128)(2,1)S(1)}, u32[]{:S(2)}, u32[]{:S(2)}) %collective-permute-start.25) | collective-permute-done | bytes 458784 | tf_op jit(solution)/shard_map/ppermute | solution.py:41
  162.8 2.6 %fusion.43 = (f32[1,256,896]{2,1,0:T(8,128)S(1)}, f32[1,256,896]{2,1,0:T(8,128)S(1)}) fusion(f32[2,1,256,896]{3,2,1,0:T(8,128)S(1)} %copy-done.1, bf16[256,896]{1,0:T(8,128)(2,1)} %collective-permute-done.17, bf16[256,896]{1,0:T(8,128)(2,1)} %collective-permute-done.11, bf16[2,256,896]{2,1,0:T(8,128)(2,1)} %collective-permute-done.3, ...), kind=kLoop, calls=%fused_computation.74 | loop fusion | flops 5505024 | bytes 8257544 | tf_op jit(solution)/shard_map/stack | solution.py:102
  172.4 7.7 %collective-permute-done.29 = bf16[256,896]{1,0:T(8,128)(2,1)S(1)} collective-permute-done((bf16[256,896]{1,0:T(8,128)(2,1)S(1)}, bf16[256,896]{1,0:T(8,128)(2,1)S(1)}, u32[]{:S(2)}, u32[]{:S(2)}) %collective-permute-start.29) | collective-permute-done | bytes 458784 | tf_op jit(solution)/shard_map/ppermute | solution.py:41
  183.2 7.6 %collective-permute-done.35 = bf16[256,896]{1,0:T(8,128)(2,1)S(1)} collective-permute-done((bf16[256,896]{1,0:T(8,128)(2,1)S(1)}, bf16[256,896]{1,0:T(8,128)(2,1)S(1)}, u32[]{:S(2)}, u32[]{:S(2)}) %collective-permute-start.35) | collective-permute-done | bytes 458784 | tf_op jit(solution)/shard_map/ppermute | solution.py:41
  194.6 5.2 %collective-permute-done.37 = bf16[256,896]{1,0:T(8,128)(2,1)S(1)} collective-permute-done((bf16[256,896]{1,0:T(8,128)(2,1)S(1)}, bf16[256,896]{1,0:T(8,128)(2,1)S(1)}, u32[]{:S(2)}, u32[]{:S(2)}) %collective-permute-start.37) | collective-permute-done | bytes 458784 | tf_op jit(solution)/shard_map/ppermute | solution.py:41
  199.9 4.3 %collective-permute-done.39 = bf16[256,896]{1,0:T(8,128)(2,1)S(1)} collective-permute-done((bf16[256,896]{1,0:T(8,128)(2,1)S(1)}, bf16[256,896]{1,0:T(8,128)(2,1)S(1)}, u32[]{:S(2)}, u32[]{:S(2)}) %collective-permute-start.39) | collective-permute-done | bytes 458784 | tf_op jit(solution)/shard_map/ppermute | solution.py:41
  205.7 6.7 %collective-permute-done.43 = bf16[256,896]{1,0:T(8,128)(2,1)S(1)} collective-permute-done((bf16[256,896]{1,0:T(8,128)(2,1)S(1)}, bf16[256,896]{1,0:T(8,128)(2,1)S(1)}, u32[]{:S(2)}, u32[]{:S(2)}) %collective-permute-start.43) | collective-permute-done | bytes 458784 | tf_op jit(solution)/shard_map/ppermute | solution.py:41
  214.9 4.3 %collective-permute-done.45 = bf16[256,896]{1,0:T(8,128)(2,1)S(1)} collective-permute-done((bf16[256,896]{1,0:T(8,128)(2,1)S(1)}, bf16[256,896]{1,0:T(8,128)(2,1)S(1)}, u32[]{:S(2)}, u32[]{:S(2)}) %collective-permute-start.45) | collective-permute-done | bytes 458784 | tf_op jit(solution)/shard_map/ppermute | solution.py:41
  221.0 4.9 %collective-permute-done.47 = bf16[256,896]{1,0:T(8,128)(2,1)S(1)} collective-permute-done((bf16[256,896]{1,0:T(8,128)(2,1)S(1)}, bf16[256,896]{1,0:T(8,128)(2,1)S(1)}, u32[]{:S(2)}, u32[]{:S(2)}) %collective-permute-start.47) | collective-permute-done | bytes 458784 | tf_op jit(solution)/shard_map/ppermute | solution.py:41
  225.9 7.3 %collective-permute-done.51 = bf16[256,896]{1,0:T(8,128)(2,1)S(1)} collective-permute-done((bf16[256,896]{1,0:T(8,128)(2,1)S(1)}, bf16[256,896]{1,0:T(8,128)(2,1)S(1)}, u32[]{:S(2)}, u32[]{:S(2)}) %collective-permute-start.51) | collective-permute-done | bytes 458784 | tf_op jit(solution)/shard_map/ppermute | solution.py:41
  235.7 5.5 %copy-done = bf16[2,8,2,256,896]{4,3,2,1,0:T(8,128)(2,1)} copy-done((bf16[2,8,2,256,896]{4,3,2,1,0:T(8,128)(2,1)}, bf16[2,8,2,256,896]{4,3,2,1,0:T(8,128)(2,1)S(1)}, u32[]{:S(2)}) %copy-start) | copy-done | bytes 14680088
  (149 shorter events, 56.3 us)
Async XLA Ops:
  11.4 13.7 %collective-permute-start.8 = (bf16[256,896]{1,0:T(8,128)(2,1)S(1)}, bf16[256,896]{1,0:T(8,128)(2,1)S(1)}, u32[]{:S(2)}, u32[]{:S(2)}) collective-permute-start(bf16[256,896]{1,0:T(8,128)(2,1)S(1)} %get-tuple-element.23), channel_id=1, source_target_pairs={{0,8},{2,10},{8,16},{10,18},{16,24},{18,26},{24,28},{26,30},{28,20... | collective-permute-start | bytes 1376264 | tf_op jit(solution)/shard_map/ppermute | solution.py:41
  14.4 19.8 %collective-permute-start.5 = (bf16[2,256,896]{2,1,0:T(8,128)(2,1)S(1)}, bf16[2,256,896]{2,1,0:T(8,128)(2,1)}, u32[]{:S(2)}, u32[]{:S(2)}) collective-permute-start(bf16[2,256,896]{2,1,0:T(8,128)(2,1)S(1)} %get-tuple-element.32), channel_id=1, source_target_pairs={{0,2},{2,0},{4,6},{6,4},{8,10},{10,8},{12,14},{14,12},{16,18},{18,... | collective-permute-start | bytes 2752520 | tf_op jit(solution)/shard_map/ppermute | solution.py:41
  14.4 37.7 %collective-permute-start.14 = (bf16[2,256,896]{2,1,0:T(8,128)(2,1)}, bf16[2,256,896]{2,1,0:T(8,128)(2,1)}, u32[]{:S(2)}, u32[]{:S(2)}) collective-permute-start(bf16[2,256,896]{2,1,0:T(8,128)(2,1)} %get-tuple-element.27), channel_id=1, source_target_pairs={{0,2},{2,0},{4,6},{6,4},{8,10},{10,8},{12,14},{14,12},{16,18},{18,... | collective-permute-start | bytes 2752520 | tf_op jit(solution)/shard_map/ppermute | solution.py:41
  14.9 38.8 %collective-permute-start.4 = (bf16[2,256,896]{2,1,0:T(8,128)(2,1)}, bf16[2,256,896]{2,1,0:T(8,128)(2,1)}, u32[]{:S(2)}, u32[]{:S(2)}) collective-permute-start(bf16[2,256,896]{2,1,0:T(8,128)(2,1)} %get-tuple-element.33), channel_id=1, source_target_pairs={{0,2},{2,0},{4,6},{6,4},{8,10},{10,8},{12,14},{14,12},{16,18},{18,... | collective-permute-start | bytes 2752520 | tf_op jit(solution)/shard_map/ppermute | solution.py:41
  28.7 20.1 %collective-permute-start.9 = (bf16[256,896]{1,0:T(8,128)(2,1)S(1)}, bf16[256,896]{1,0:T(8,128)(2,1)S(1)}, u32[]{:S(2)}, u32[]{:S(2)}) collective-permute-start(bf16[256,896]{1,0:T(8,128)(2,1)S(1)} %get-tuple-element.15), channel_id=1, source_target_pairs={{0,8},{2,10},{8,16},{10,18},{16,24},{18,26},{24,28},{26,30},{28,20... | collective-permute-start | bytes 1376264 | tf_op jit(solution)/shard_map/ppermute | solution.py:41
  34.2 85.7 %collective-permute-start = (bf16[384,4096]{1,0:T(8,128)(2,1)}, bf16[384,4096]{1,0:T(8,128)(2,1)S(1)}, u32[]{:S(2)}, u32[]{:S(2)}) collective-permute-start(bf16[384,4096]{1,0:T(8,128)(2,1)} %constant_dynamic-slice_fusion), channel_id=1, source_target_pairs={{0,1},{1,0},{2,3},{3,2},{4,5},{5,4},{6,7},{7,6},{8,9},{9,8},{10,11... | collective-permute-start | bytes 9437192 | tf_op jit(solution)/shard_map/ppermute | solution.py:115
  50.5 13.5 %collective-permute-start.10 = (bf16[256,896]{1,0:T(8,128)(2,1)S(1)}, bf16[256,896]{1,0:T(8,128)(2,1)S(1)}, u32[]{:S(2)}, u32[]{:S(2)}) collective-permute-start(bf16[256,896]{1,0:T(8,128)(2,1)S(1)} %get-tuple-element.13), channel_id=1, source_target_pairs={{0,8},{2,10},{8,16},{10,18},{16,24},{18,26},{24,28},{26,30},{28,20... | collective-permute-start | bytes 1376264 | tf_op jit(solution)/shard_map/ppermute | solution.py:41
  52.1 19.5 %collective-permute-start.20 = (bf16[256,896]{1,0:T(8,128)(2,1)S(1)}, bf16[256,896]{1,0:T(8,128)(2,1)S(1)}, u32[]{:S(2)}, u32[]{:S(2)}) collective-permute-start(bf16[256,896]{1,0:T(8,128)(2,1)S(1)} %get-tuple-element.12), channel_id=1, source_target_pairs={{0,8},{2,10},{8,16},{10,18},{16,24},{18,26},{24,28},{26,30},{28,20... | collective-permute-start | bytes 1376264 | tf_op jit(solution)/shard_map/ppermute | solution.py:41
  53.7 24.3 %collective-permute-start.13 = (bf16[2,256,896]{2,1,0:T(8,128)(2,1)}, bf16[2,256,896]{2,1,0:T(8,128)(2,1)}, u32[]{:S(2)}, u32[]{:S(2)}) collective-permute-start(bf16[2,256,896]{2,1,0:T(8,128)(2,1)} %get-tuple-element.28), channel_id=1, source_target_pairs={{0,2},{2,0},{4,6},{6,4},{8,10},{10,8},{12,14},{14,12},{16,18},{18,... | collective-permute-start | bytes 2752520 | tf_op jit(solution)/shard_map/ppermute | solution.py:41
  75.3 13.8 %collective-permute-start.15 = (bf16[256,896]{1,0:T(8,128)(2,1)}, bf16[256,896]{1,0:T(8,128)(2,1)}, u32[]{:S(2)}, u32[]{:S(2)}) collective-permute-start(bf16[256,896]{1,0:T(8,128)(2,1)} %get-tuple-element.24), channel_id=1, source_target_pairs={{8,0},{10,2},{16,8},{18,10},{24,16},{26,18},{28,24},{30,26},{20,28... | collective-permute-start | bytes 1376264 | tf_op jit(solution)/shard_map/ppermute | solution.py:41
  76.3 19.3 %collective-permute-start.23 = (bf16[256,896]{1,0:T(8,128)(2,1)}, bf16[256,896]{1,0:T(8,128)(2,1)}, u32[]{:S(2)}, u32[]{:S(2)}) collective-permute-start(bf16[256,896]{1,0:T(8,128)(2,1)} %get-tuple-element.25), channel_id=1, source_target_pairs={{8,0},{10,2},{16,8},{18,10},{24,16},{26,18},{28,24},{30,26},{20,28... | collective-permute-start | bytes 1376264 | tf_op jit(solution)/shard_map/ppermute | solution.py:41
  77.9 35.7 %collective-permute-start.12 = (bf16[2,256,896]{2,1,0:T(8,128)(2,1)}, bf16[2,256,896]{2,1,0:T(8,128)(2,1)}, u32[]{:S(2)}, u32[]{:S(2)}) collective-permute-start(bf16[2,256,896]{2,1,0:T(8,128)(2,1)} %get-tuple-element.29), channel_id=1, source_target_pairs={{0,2},{2,0},{4,6},{6,4},{8,10},{10,8},{12,14},{14,12},{16,18},{18,... | collective-permute-start | bytes 2752520 | tf_op jit(solution)/shard_map/ppermute | solution.py:41
  77.9 46.1 %collective-permute-start.3 = (bf16[2,256,896]{2,1,0:T(8,128)(2,1)}, bf16[2,256,896]{2,1,0:T(8,128)(2,1)}, u32[]{:S(2)}, u32[]{:S(2)}) collective-permute-start(bf16[2,256,896]{2,1,0:T(8,128)(2,1)} %get-tuple-element.26), channel_id=1, source_target_pairs={{0,2},{2,0},{4,6},{6,4},{8,10},{10,8},{12,14},{14,12},{16,18},{18,... | collective-permute-start | bytes 2752520 | tf_op jit(solution)/shard_map/ppermute | solution.py:41
  97.7 17.4 %collective-permute-start.16 = (bf16[256,896]{1,0:T(8,128)(2,1)S(1)}, bf16[256,896]{1,0:T(8,128)(2,1)S(1)}, u32[]{:S(2)}, u32[]{:S(2)}) collective-permute-start(bf16[256,896]{1,0:T(8,128)(2,1)S(1)} %get-tuple-element.19), channel_id=1, source_target_pairs={{8,0},{10,2},{16,8},{18,10},{24,16},{26,18},{28,24},{30,26},{20,28... | collective-permute-start | bytes 1376264 | tf_op jit(solution)/shard_map/ppermute | solution.py:41
  98.5 18.4 %collective-permute-start.24 = (bf16[256,896]{1,0:T(8,128)(2,1)S(1)}, bf16[256,896]{1,0:T(8,128)(2,1)S(1)}, u32[]{:S(2)}, u32[]{:S(2)}) collective-permute-start(bf16[256,896]{1,0:T(8,128)(2,1)S(1)} %get-tuple-element.18), channel_id=1, source_target_pairs={{8,0},{10,2},{16,8},{18,10},{24,16},{26,18},{28,24},{30,26},{20,28... | collective-permute-start | bytes 1376264 | tf_op jit(solution)/shard_map/ppermute | solution.py:41
  113.6 25.8 %collective-permute-start.2 = (bf16[384,512]{1,0:T(8,128)(2,1)}, bf16[384,512]{1,0:T(8,128)(2,1)}, u32[]{:S(2)}, u32[]{:S(2)}) collective-permute-start(bf16[384,512]{1,0:T(8,128)(2,1)} %param.8), channel_id=1, source_target_pairs={{0,1},{1,0},{2,3},{3,2},{4,5},{5,4},{6,7},{7,6},{8,9},{9,8},{10,11... | collective-permute-start | bytes 1179656 | tf_op jit(solution)/shard_map/ppermute | solution.py:115
  116.9 35.2 %collective-permute-start.21 = (bf16[256,896]{1,0:T(8,128)(2,1)}, bf16[256,896]{1,0:T(8,128)(2,1)}, u32[]{:S(2)}, u32[]{:S(2)}) collective-permute-start(bf16[256,896]{1,0:T(8,128)(2,1)} %get-tuple-element.10), channel_id=1, source_target_pairs={{0,8},{2,10},{8,16},{10,18},{16,24},{18,26},{24,28},{26,30},{28,20... | collective-permute-start | bytes 1376264 | tf_op jit(solution)/shard_map/ppermute | solution.py:41
  124.0 25.1 %collective-permute-start.1 = (bf16[384,512]{1,0:T(8,128)(2,1)}, bf16[384,512]{1,0:T(8,128)(2,1)S(1)}, u32[]{:S(2)}, u32[]{:S(2)}) collective-permute-start(bf16[384,512]{1,0:T(8,128)(2,1)} %fusion.8), channel_id=1, source_target_pairs={{0,1},{1,0},{2,3},{3,2},{4,5},{5,4},{6,7},{7,6},{8,9},{9,8},{10,11... | collective-permute-start | bytes 1179656 | tf_op jit(solution)/shard_map/ppermute | solution.py:115
  150.0 18.8 %collective-permute-start.27 = (bf16[256,896]{1,0:T(8,128)(2,1)S(1)}, bf16[256,896]{1,0:T(8,128)(2,1)S(1)}, u32[]{:S(2)}, u32[]{:S(2)}) collective-permute-start(bf16[256,896]{1,0:T(8,128)(2,1)S(1)} %get-tuple-element.7), channel_id=1, source_target_pairs={{0,8},{2,10},{8,16},{10,18},{16,24},{18,26},{24,28},{26,30},{28,20... | collective-permute-start | bytes 1376264 | tf_op jit(solution)/shard_map/ppermute | solution.py:41
  150.5 19.7 %collective-permute-start.33 = (bf16[256,896]{1,0:T(8,128)(2,1)S(1)}, bf16[256,896]{1,0:T(8,128)(2,1)S(1)}, u32[]{:S(2)}, u32[]{:S(2)}) collective-permute-start(bf16[256,896]{1,0:T(8,128)(2,1)S(1)} %get-tuple-element.7), channel_id=1, source_target_pairs={{8,0},{10,2},{16,8},{18,10},{24,16},{26,18},{28,24},{30,26},{20,28... | collective-permute-start | bytes 1376264 | tf_op jit(solution)/shard_map/ppermute | solution.py:41
  170.2 20.6 %collective-permute-start.35 = (bf16[256,896]{1,0:T(8,128)(2,1)S(1)}, bf16[256,896]{1,0:T(8,128)(2,1)S(1)}, u32[]{:S(2)}, u32[]{:S(2)}) collective-permute-start(bf16[256,896]{1,0:T(8,128)(2,1)S(1)} %collective-permute-done.27), channel_id=1, source_target_pairs={{0,8},{2,10},{8,16},{10,18},{16,24},{18,26},{24,28},{26,30},{28,20... | collective-permute-start | bytes 1376264 | tf_op jit(solution)/shard_map/ppermute | solution.py:41
  171.8 19.6 %collective-permute-start.34 = (bf16[256,896]{1,0:T(8,128)(2,1)S(1)}, bf16[256,896]{1,0:T(8,128)(2,1)S(1)}, u32[]{:S(2)}, u32[]{:S(2)}) collective-permute-start(bf16[256,896]{1,0:T(8,128)(2,1)S(1)} %collective-permute-done.33), channel_id=1, source_target_pairs={{0,2},{2,0},{4,6},{6,4},{8,10},{10,8},{12,14},{14,12},{16,18},{18,... | collective-permute-start | bytes 1376264 | tf_op jit(solution)/shard_map/ppermute | solution.py:41
  171.9 21.1 %collective-permute-start.41 = (bf16[256,896]{1,0:T(8,128)(2,1)S(1)}, bf16[256,896]{1,0:T(8,128)(2,1)S(1)}, u32[]{:S(2)}, u32[]{:S(2)}) collective-permute-start(bf16[256,896]{1,0:T(8,128)(2,1)S(1)} %collective-permute-done.33), channel_id=1, source_target_pairs={{8,0},{10,2},{16,8},{18,10},{24,16},{26,18},{28,24},{30,26},{20,28... | collective-permute-start | bytes 1376264 | tf_op jit(solution)/shard_map/ppermute | solution.py:41
  181.7 18.1 %collective-permute-start.37 = (bf16[256,896]{1,0:T(8,128)(2,1)S(1)}, bf16[256,896]{1,0:T(8,128)(2,1)S(1)}, u32[]{:S(2)}, u32[]{:S(2)}) collective-permute-start(bf16[256,896]{1,0:T(8,128)(2,1)S(1)} %collective-permute-done.29), channel_id=1, source_target_pairs={{8,0},{10,2},{16,8},{18,10},{24,16},{26,18},{28,24},{30,26},{20,28... | collective-permute-start | bytes 1376264 | tf_op jit(solution)/shard_map/ppermute | solution.py:41
  191.4 21.0 %collective-permute-start.43 = (bf16[256,896]{1,0:T(8,128)(2,1)S(1)}, bf16[256,896]{1,0:T(8,128)(2,1)S(1)}, u32[]{:S(2)}, u32[]{:S(2)}) collective-permute-start(bf16[256,896]{1,0:T(8,128)(2,1)S(1)} %collective-permute-done.35), channel_id=1, source_target_pairs={{0,8},{2,10},{8,16},{10,18},{16,24},{18,26},{24,28},{26,30},{28,20... | collective-permute-start | bytes 1376264 | tf_op jit(solution)/shard_map/ppermute | solution.py:41
  193.0 20.0 %collective-permute-start.42 = (bf16[256,896]{1,0:T(8,128)(2,1)S(1)}, bf16[256,896]{1,0:T(8,128)(2,1)S(1)}, u32[]{:S(2)}, u32[]{:S(2)}) collective-permute-start(bf16[256,896]{1,0:T(8,128)(2,1)S(1)} %collective-permute-done.41), channel_id=1, source_target_pairs={{0,2},{2,0},{4,6},{6,4},{8,10},{10,8},{12,14},{14,12},{16,18},{18,... | collective-permute-start | bytes 1376264 | tf_op jit(solution)/shard_map/ppermute | solution.py:41
  193.4 21.3 %collective-permute-start.49 = (bf16[256,896]{1,0:T(8,128)(2,1)S(1)}, bf16[256,896]{1,0:T(8,128)(2,1)S(1)}, u32[]{:S(2)}, u32[]{:S(2)}) collective-permute-start(bf16[256,896]{1,0:T(8,128)(2,1)S(1)} %collective-permute-done.41), channel_id=1, source_target_pairs={{8,0},{10,2},{16,8},{18,10},{24,16},{26,18},{28,24},{30,26},{20,28... | collective-permute-start | bytes 1376264 | tf_op jit(solution)/shard_map/ppermute | solution.py:41
  204.3 15.0 %collective-permute-start.45 = (bf16[256,896]{1,0:T(8,128)(2,1)S(1)}, bf16[256,896]{1,0:T(8,128)(2,1)S(1)}, u32[]{:S(2)}, u32[]{:S(2)}) collective-permute-start(bf16[256,896]{1,0:T(8,128)(2,1)S(1)} %collective-permute-done.37), channel_id=1, source_target_pairs={{8,0},{10,2},{16,8},{18,10},{24,16},{26,18},{28,24},{30,26},{20,28... | collective-permute-start | bytes 1376264 | tf_op jit(solution)/shard_map/ppermute | solution.py:41
  213.0 20.1 %collective-permute-start.51 = (bf16[256,896]{1,0:T(8,128)(2,1)S(1)}, bf16[256,896]{1,0:T(8,128)(2,1)S(1)}, u32[]{:S(2)}, u32[]{:S(2)}) collective-permute-start(bf16[256,896]{1,0:T(8,128)(2,1)S(1)} %collective-permute-done.43), channel_id=1, source_target_pairs={{0,8},{2,10},{8,16},{10,18},{16,24},{18,26},{24,28},{26,30},{28,20... | collective-permute-start | bytes 1376264 | tf_op jit(solution)/shard_map/ppermute | solution.py:41
  214.7 19.5 %collective-permute-start.50 = (bf16[256,896]{1,0:T(8,128)(2,1)S(1)}, bf16[256,896]{1,0:T(8,128)(2,1)S(1)}, u32[]{:S(2)}, u32[]{:S(2)}) collective-permute-start(bf16[256,896]{1,0:T(8,128)(2,1)S(1)} %collective-permute-done.49), channel_id=1, source_target_pairs={{0,2},{2,0},{4,6},{6,4},{8,10},{10,8},{12,14},{14,12},{16,18},{18,... | collective-permute-start | bytes 1376264 | tf_op jit(solution)/shard_map/ppermute | solution.py:41
  219.2 14.6 %collective-permute-start.46 = (bf16[256,896]{1,0:T(8,128)(2,1)S(1)}, bf16[256,896]{1,0:T(8,128)(2,1)S(1)}, u32[]{:S(2)}, u32[]{:S(2)}) collective-permute-start(bf16[256,896]{1,0:T(8,128)(2,1)S(1)} %collective-permute-done.45), channel_id=1, source_target_pairs={{0,2},{2,0},{4,6},{6,4},{8,10},{10,8},{12,14},{14,12},{16,18},{18,... | collective-permute-start | bytes 1376264 | tf_op jit(solution)/shard_map/ppermute | solution.py:41
  219.3 13.9 %collective-permute-start.53 = (bf16[256,896]{1,0:T(8,128)(2,1)S(1)}, bf16[256,896]{1,0:T(8,128)(2,1)S(1)}, u32[]{:S(2)}, u32[]{:S(2)}) collective-permute-start(bf16[256,896]{1,0:T(8,128)(2,1)S(1)} %collective-permute-done.45), channel_id=1, source_target_pairs={{8,0},{10,2},{16,8},{18,10},{24,16},{26,18},{28,24},{30,26},{20,28... | collective-permute-start | bytes 1376264 | tf_op jit(solution)/shard_map/ppermute | solution.py:41
  (34 other events, 381.7 us)

commit v2 on v0

v2 whole, which is shorter than its diff:
```python
import jax
import jax.numpy as jnp
from jax import lax
from jax.experimental import pallas as pl
from jax.experimental.pallas import tpu as pltpu
from jax.sharding import PartitionSpec as P

outer_rate = 0.7
momentum_decay = 0.9
f32 = jnp.float32
bf16 = jnp.bfloat16
after = lax.optimization_barrier


def ring_chip(pos, chips):
    return jnp.where(pos < chips // 2, 2 * pos, 2 * (chips - 1 - pos) + 1)


def ring_pos(chip, chips):
    return jnp.where(chip % 2 == 0, chip // 2, chips - 1 - chip // 2)


def ring_perms(n):
    chips = n // 2
    order = [2 * p if p < chips // 2 else 2 * (chips - 1 - p) + 1 for p in range(chips)]
    step = [(2 * order[p] + c, 2 * order[(p + 1 - 2 * c) % chips] + c) for p in range(chips) for c in range(2)]
    swap = [(r, r ^ 1) for r in range(n)]
    return step, swap


anywhere = pl.BlockSpec(memory_space=pltpu.HBM)
in_smem = pl.BlockSpec(memory_space=pltpu.SMEM)
in_vmem = pl.BlockSpec(memory_space=pltpu.VMEM)


class Chain:
    def __init__(self):
        self.token = None

    def call(self, kernel, name, out_shape, in_specs, out_specs, scratch, *operands, aliases={}, grant=8, gates=(),
             where=None, steps=1):
        single = not isinstance(out_shape, list)
        out_shape, out_specs = ([out_shape], [out_specs]) if single else (out_shape, out_specs)
        extra = list(gates) + ([] if self.token is None else [self.token])
        lead, inputs = int(where is not None), len(operands)

        def body(*refs):
            rest = refs[lead:]
            return kernel(*refs[:lead], *rest[:inputs], *rest[inputs + len(extra) + 1:])

        out_shape = [jax.ShapeDtypeStruct((8, 128), f32)] + out_shape
        in_specs = in_specs + [pl.BlockSpec(memory_space=pl.ANY)] * len(extra)
        out_specs = [pl.BlockSpec(memory_space=pl.ANY)] + out_specs
        params = dict(
            out_shape=out_shape,
            input_output_aliases={i + lead: o + 1 for i, o in aliases.items()},
            compiler_params=pltpu.CompilerParams(vmem_limit_bytes=grant * 2**20),
            cost_estimate=pl.CostEstimate(flops=0, bytes_accessed=0, transcendentals=0),
            name=name,
        )
        if where is None:
            params.update(in_specs=in_specs, out_specs=out_specs, scratch_shapes=scratch)
        else:
            params.update(grid_spec=pltpu.PrefetchScalarGridSpec(
                num_scalar_prefetch=1, grid=(steps,), in_specs=in_specs, out_specs=out_specs, scratch_shapes=scratch
            ))
        self.token, *outs = pl.pallas_call(body, **params)(*([] if where is None else [where]), *operands, *extra)
        return outs[0] if single else outs


def unit_type(rows, cols, kind=bf16):
    return jax.ShapeDtypeStruct((rows, cols), kind)


def run_copies(copies):
    for copy in copies:
        copy.start()
    return copies


def finish(copies):
    for copy in copies:
        copy.wait()


def fetch(chain, shards, places, apart=False):
    rows, cols = shards.shape[3:]
    count = len(places)

    def kernel(index_ref, shards_ref, *refs):
        outs, sems = refs[:-1], refs[-1]
        finish(run_copies([
            pltpu.make_async_copy(
                shards_ref.at[m, index_ref[2 * i], index_ref[2 * i + 1]], outs[m] if apart else outs[i].at[m], sems.at[i, m]
            )
            for i in range(count) for m in range(2)
        ]))

    shapes = [unit_type(rows, cols)] * 2 if apart else [jax.ShapeDtypeStruct((2, rows, cols), bf16)] * count
    return chain.call(
        kernel, "fetch", shapes, [in_smem, anywhere], [in_vmem] * len(shapes), [pltpu.SemaphoreType.DMA((count, 2))],
        jnp.stack([value for place in places for value in place]), shards, grant=44,
    )


def add(chain, own, other, came, m):
    rows, cols = own.shape[1:]

    def kernel(own_ref, other_ref, *refs):
        total = own_ref[m].astype(f32) + (other_ref[m] if len(other.shape) == 3 else other_ref[...]).astype(f32)
        for ref in refs[:-1]:
            total = total + ref[...].astype(f32)
        refs[-1][...] = total.astype(bf16)

    return chain.call(
        kernel, "add", unit_type(rows, cols), [in_vmem] * (2 + len(came)), in_vmem, [], own, other, *came
    )


def update(chain, own, other, came, anchor, momentum, m, workers, gates):
    rows, cols = own.shape[1:]

    def kernel(own_ref, other_ref, came_ref, anchor_ref, momentum_ref, out, new_ref):
        average = (own_ref[m].astype(f32) + other_ref[m].astype(f32) + came_ref[...].astype(f32)) / workers
        weights = anchor_ref[m, 0].astype(f32)
        pseudo_grad = weights - average
        momentum_new = momentum_decay * momentum_ref[m, 0] + pseudo_grad
        out[...] = (weights - outer_rate * (pseudo_grad + momentum_decay * momentum_new)).astype(bf16)
        new_ref[...] = momentum_new

    return chain.call(
        kernel, "update", [unit_type(rows, cols), unit_type(rows, cols, f32)], [in_vmem] * 5, [in_vmem] * 2, [],
        own, other, came, anchor, momentum, gates=gates,
    )


def store(chain, values, shape):
    def kernel(*refs):
        out, sems = refs[2:]
        finish(run_copies([pltpu.make_async_copy(refs[m], out.at[m, 0], sems.at[m]) for m in range(2)]))

    return chain.call(
        kernel, "store", jax.ShapeDtypeStruct(shape, f32), [in_vmem] * 2, anywhere, [pltpu.SemaphoreType.DMA((2,))], *values
    )


def place(chain, gathered, shape, index, entries):
    places = [entry for _, entry in entries]
    values = [value for value, _ in entries]
    aliased = gathered is not None

    def kernel(index_ref, *refs):
        out, sems = refs[len(places) + aliased], refs[-1]
        finish(run_copies([
            pltpu.make_async_copy(refs[i], out.at[m, index_ref[d]], sems.at[i]) for i, (m, d) in enumerate(places)
        ]))

    return chain.call(
        kernel, "place", jax.ShapeDtypeStruct(shape, bf16),
        [in_smem] + [in_vmem] * len(values) + [anywhere] * aliased, anywhere,
        [pltpu.SemaphoreType.DMA((len(places),))],
        index, *values, *([gathered] if aliased else []),
        aliases={len(values) + 1: 0} if aliased else {},
    )


def outer_step(chain, local_weights, anchor, momentum, inner):
    n = lax.axis_size("replica")
    chips = n // 2
    last = chips - 1
    rows, cols = anchor.shape[2], anchor.shape[3]
    perm, swap = ring_perms(n)
    me = lax.axis_index("replica")
    core = me % 2
    pos = ring_pos(me // 2, chips)
    ahead = [ring_chip((pos + d) % chips, chips) for d in range(chips)]
    behind = [ring_chip((pos - d + chips) % chips, chips) for d in range(chips)]
    mine = [jnp.where(core == 0, a, b) for a, b in zip(ahead, behind)]
    siblings = [jnp.where(core == 0, b, a) for a, b in zip(ahead, behind)]

    def send(x, perm):
        return lax.ppermute(x, "replica", perm)

    shards = local_weights[0].reshape(2, chips, 2, rows, cols)

    def mine_at(j):
        return mine[last - j], core

    def siblings_at(j):
        return siblings[last - j], 1 - core

    own, other = {}, {}

    def fetch_steps(*steps):
        values = fetch(chain, shards, [place(j) for place in (siblings_at, mine_at) for j in steps])
        for i, j in enumerate(steps):
            other[j] = [send(values[i], swap)] * 2
            own[j] = values[len(steps) + i]

    other[0] = [send(value, swap) for value in fetch(chain, shards, [siblings_at(0)], True)]
    own[0], own[1], own[2], *values = fetch(
        chain, shards, [mine_at(0), mine_at(1), mine_at(2), siblings_at(1), siblings_at(2)]
    )
    other[1], other[2] = ([send(value, swap)] * 2 for value in values)
    ahead_of = {0: [3, 4, 5]}
    ahead_of.update({j: [j + 4, j + 5] for j in range(2, chips, 2)})
    came = [[], []]
    for j in range(last):
        for m in range(2):
            came[m] = [send(add(chain, own[j], other[j][m], came[m], m), perm)]
        inner.early(j)
        steps = [i for i in ahead_of.get(j, []) if i <= last]
        if steps:
            fetch_steps(*steps)

    have = []
    momentum_new = []
    for m in range(2):
        gates = inner.first if m == 0 else []
        piece, momentum_m = update(chain, own[last], other[last][m], came[m][0], anchor, momentum, m, n, gates)
        have.append(piece)
        momentum_new.append(momentum_m)

    index = jnp.stack([2 * siblings[k] + core for k in range(chips)] + [2 * mine[k] + 1 - core for k in range(chips)])
    shape = (2, n, rows, cols)
    gathered = None
    entries = []
    for k in range(chips):
        held = []
        for m in range(2):
            value = have[m]
            if gathered is not None:
                value, gathered = after((value, gathered))
            if k < last:
                have[m] = send(value, perm)
            entries.append((value, (m, k)))
            held.append((send(value, swap), (m, chips + k)))
        gathered = place(chain, gathered, shape, index, entries)
        entries = held
        if k == 0:
            momentum_out = store(chain, momentum_new, momentum.shape)
        inner.late(k)
    gathered = place(chain, gathered, shape, index, entries)
    return gathered.reshape(2, n * rows, cols), momentum_out


def chosen(where_ref, a, b):
    return jnp.where(where_ref[1] == 0, a[...], b[...])


def own_keys_kernel(where_ref, tokens_ref, weight_ref, out, acc):
    step = pl.program_id(0)
    term = jnp.dot(tokens_ref[...], weight_ref[...], preferred_element_type=f32)

    @pl.when(step == 0)
    def _():
        acc[...] = term

    @pl.when(step > 0)
    def _():
        acc[...] += term

    @pl.when(step == pl.num_programs(0) - 1)
    def _():
        out[...] = acc[...]


def other_keys_kernel(where_ref, a_ref, b_ref, weight_ref, out, acc):
    step = pl.program_id(0)
    term = jnp.dot(chosen(where_ref, a_ref, b_ref), weight_ref[...], preferred_element_type=f32)

    @pl.when(step == 0)
    def _():
        acc[...] = term

    @pl.when(step > 0)
    def _():
        acc[...] += term

    @pl.when(step == pl.num_programs(0) - 1)
    def _():
        out[...] = acc[...].astype(bf16)


def product(a, b):
    return lax.dot_general(a, b, (((0,), (0,)), ((), ())), preferred_element_type=f32)


def own_term_kernel(where_ref, tokens_ref, cotangent_ref, *refs):
    refs[-1][...] = product(tokens_ref[...], cotangent_ref[...]).astype(bf16)


def grad_kernel(where_ref, term_ref, *refs):
    total = term_ref[...].astype(f32)
    for i in range(0, len(refs) // 4 * 4, 4):
        term = product(chosen(where_ref, *refs[i:i + 2]), chosen(where_ref, *refs[i + 2:i + 4]))
        total = total + term.astype(bf16).astype(f32)
    refs[-1][...] = total.astype(bf16)


class Inner:
    def __init__(self, chain, tokens, inner_weight, cotangent):
        self.chain = chain
        self.tokens, self.weight, self.cotangent = tokens, inner_weight[0], cotangent
        self.parts = lax.axis_size("fsdp")
        self.mine = lax.axis_index("fsdp")
        self.count = tokens.shape[0]
        self.depth, self.width = self.weight.shape
        self.tile = min(1024, self.depth // 2)
        self.steps = self.depth // self.tile
        core = lax.axis_index("replica") % 2
        self.where = jnp.stack([self.mine * self.steps, core])

    def shift(self, x, s, c):
        workers = lax.axis_size("replica")
        pairs = [
            (r * self.parts + k, r * self.parts + (k + s) % self.parts)
            for r in range(c, workers, 2) for k in range(self.parts)
        ]
        return lax.ppermute(x, ("replica", "fsdp"), pairs)

    def specs(self, first=0):
        block = (self.count, self.tile)
        own = pl.BlockSpec(block, lambda i, where: (0, where[0] + first + i))
        others = [pl.BlockSpec(block, lambda i, where, c=c: (0, jnp.where(where[1] == c, first + i, 0))) for c in range(2)]
        return own, others, pl.BlockSpec((self.tile, self.width), lambda i, where: (first + i, 0))

    def call(self, kernel, name, out_shape, in_specs, out_specs, scratch, steps, *operands, aliases={}):
        return self.chain.call(
            kernel, name, out_shape, in_specs, out_specs, scratch, *operands, aliases=aliases, grant=24,
            where=self.where, steps=steps,
        )

    def columns(self, owner):
        depth, width, count = self.depth, self.width, self.count

        def kernel(start_ref, tokens_ref, cotangent_ref, out, sems):
            start = pl.multiple_of(start_ref[0] * depth, depth)
            finish(run_copies([
                pltpu.make_async_copy(tokens_ref.at[:, pl.ds(start, depth)], out.at[:, pl.ds(0, depth)], sems.at[0]),
                pltpu.make_async_copy(cotangent_ref, out.at[:, pl.ds(depth, width)], sems.at[1]),
            ]))

        return self.chain.call(
            kernel, "columns", jax.ShapeDtypeStruct((count, depth + width), bf16), [in_smem, anywhere, anywhere], in_vmem,
            [pltpu.SemaphoreType.DMA((2,))], jnp.reshape(owner, (1,)), self.tokens, self.cotangent, grant=56,
        )

    def send_columns(self):
        values = [self.columns((self.mine + s) % self.parts) for s in range(1, self.parts)]
        self.first, self.second = ([self.shift(value, s, c) for s, value in enumerate(values, 1)] for c in range(2))

    def result(self, kind):
        return jax.ShapeDtypeStruct((self.count, self.width), kind)

    def multiply_own(self):
        own, _, weights = self.specs()
        self.keys = self.call(
            own_keys_kernel, "own_keys", self.result(f32), [own, weights],
            pl.BlockSpec((self.count, self.width), lambda i, where: (0, 0)),
            [pltpu.VMEM((self.count, self.width), f32)], self.steps, self.tokens, self.weight,
        )

    def multiply_others(self):
        _, others, weights = self.specs()
        out = [
            self.call(
                other_keys_kernel, "other_keys", self.result(bf16), [*others, weights],
                pl.BlockSpec((self.count, self.width), lambda i, where: (0, 0)),
                [pltpu.VMEM((self.count, self.width), f32)], self.steps, a, b, self.weight,
            )
            for a, b in zip(self.first, self.second)
        ]
        self.came = [self.shift(value, self.parts - s, c) for s, value in enumerate(out, 1) for c in range(2)]

    def halves(self, kernel, name, second, first_result, operands, in_specs):
        half = self.steps // 2
        return self.call(
            kernel, name, jax.ShapeDtypeStruct((self.depth, self.width), bf16), in_specs + [anywhere] * second,
            pl.BlockSpec((self.tile, self.width), lambda i, where: (half * second + i, 0)), [], half,
            *operands, *([first_result] if second else []), aliases={len(operands): 0} if second else {},
        )

    def own_term(self, second):
        own, _, _ = self.specs(self.steps // 2 * second)
        whole = pl.BlockSpec((self.count, self.width), lambda i, where: (0, 0))
        self.term = self.halves(
            own_term_kernel, "own_term", second, getattr(self, "term", None), [self.tokens, self.cotangent], [own, whole]
        )

    def other_terms(self, second):
        _, others, rows = self.specs(self.steps // 2 * second)
        last = self.depth // self.width
        cotangents = pl.BlockSpec((self.count, self.width), lambda i, where: (0, last))
        operands, in_specs = [self.term], [rows]
        for a, b in zip(self.first, self.second):
            operands += [a, b, a, b]
            in_specs += others + [cotangents] * 2
        self.grad = self.halves(
            grad_kernel, "grad", second, getattr(self, "grad", None), operands, in_specs
        )

    def finish_keys(self):
        keys = self.keys
        for value in self.came:
            keys = keys + value.astype(f32)
        self.keys = keys.astype(bf16)

    def early(self, j):
        if j == 0:
            self.send_columns()
        if j == 3:
            self.multiply_own()
        if j in (4, 5):
            self.own_term(j - 4)

    def late(self, k):
        if k == 3:
            self.multiply_others()
        if k in (4, 5):
            self.other_terms(k - 4)


def shards(tokens, inner_weight, cotangent, local_weights, anchor, momentum):
    chain = Chain()
    inner = Inner(chain, tokens, inner_weight, cotangent)
    new_weights, new_momentum = outer_step(chain, local_weights, anchor, momentum, inner)
    inner.finish_keys()
    return (inner.keys, inner.grad[None], new_weights, new_momentum)


def solution(mesh):
    return jax.shard_map(
        shards,
        mesh=mesh,
        in_specs=(
            P(("replica", "fsdp"), None),
            P("replica", "fsdp", None),
            P(("replica", "fsdp"), None),
            P("replica", None, "fsdp", None),
            P(None, "fsdp", "replica", None),
            P(None, "fsdp", "replica", None),
        ),
        out_specs=(
            P(("replica", "fsdp"), None),
            P("replica", "fsdp", None),
            P(None, "fsdp", None),
            P(None, "fsdp", "replica", None),
        ),
        check_vma=False,
    )
```

time: 543 us -> 188 us (0.35)
  waiting for transfers between devices: 474 us -> 35.9 us
  Pallas kernels: 0 us -> 82.7 us
  starting transfers between devices: 0.17 us -> 50.5 us
  matrix products: 19 us -> 0 us
  other arithmetic: 20 us -> 1.1 us
  between operations: 15.7 us -> 1.47 us
    reduce_scatter x2 -> x0, waiting for transfers between devices: 380 us -> none  [the longest x1 280 us: outer_step(): lax.psum_scatter(local_slab, 'replica', scatter_dimension=1, tiled=True)]
    all_gather x2 -> x0, waiting for transfers between devices: 93.5 us -> none  [the longest x1 93.5 us: outer_step(): gathered = lax.all_gather(new_piece, 'replica', axis=1, tiled=True)]
    pallas_call x0 -> x37, Pallas kernels: none -> 82.7 us  [call(): pl.pallas_call(body, **params)]
    ppermute x0 -> x57, starting transfers between devices: none -> 50.5 us  [the longest x53 40 us: send(): return lax.ppermute(x, 'replica', perm)]
    ppermute x0 -> x57, waiting for transfers between devices: none -> 35.9 us  [the longest x53 34.8 us: send(): return lax.ppermute(x, 'replica', perm)]
    dot_general x2 -> x0, matrix products: 19 us -> none  [the longest x1 9.62 us: inner_pass(): lax.dot_general(columns, cotangent, (((0,), (0,)), ((), ())), preferred_e...]
    convert_element_type x1, other arithmetic: 16.4 us -> 0.95 us  [finish_keys(): self.keys = keys.astype(bf16)]
    unnamed x9 -> x68, local copies, waits for them, and re-layouts: 13.2 us -> 15.3 us
  transfers between devices with their start and end apart: 4 -> 57, of which waited for: 3 -> 16; matrix products, arithmetic and copies ran while one was open for 4% -> 1% of each run, Pallas kernels for 0% -> 42%
where the time goes in v2:
time: 188 us; the launch traced here: 187 us
  Pallas kernels  82.7 us (44%)
  starting transfers between devices  50.5 us (27%)
  waiting for transfers between devices  35.9 us (19%)
  local copies, waits for them, and re-layouts  15.6 us (8%)
    pallas_call x37, Pallas kernels, call(): pl.pallas_call(body, **params)  82.7 us
    ppermute x53, starting transfers between devices, send(): return lax.ppermute(x, 'replica', perm)  40 us
    ppermute x53, waiting for transfers between devices, send(): return lax.ppermute(x, 'replica', perm)  34.8 us
    unnamed x68, local copies, waits for them, and re-layouts  15.3 us
    ppermute x4, starting transfers between devices, shift(): return lax.ppermute(x, ('replica', 'fsdp'), pairs)  10.4 us
  transfers between devices with their start and end apart: 57, of which 16 were waited for; matrix products, arithmetic and copies ran while one was open for 1% of the time, Pallas kernels for 42%

profile of v2, /device:TPU:0, one launch (start us, length us, event | category | flops | bytes accessed | tf_op | source)
XLA Modules:
  0.0 187.2 jit_solution(2939955628798599120)
XLA Ops:
  3.2 4.1 %fetch.5 = (f32[8,128]{1,0:T(8,128)S(1)}, bf16[2,256,896]{2,1,0:T(8,128)(2,1)S(1)}, bf16[2,256,896]{2,1,0:T(8,128)(2,1)S(1)}, bf16[2,256,896]{2,1,0:T(8,128)(2,1...) custom-call(s32[10]{0:T(128)S(1)} %stack.135.refs_0_, bf16[2,8,2,256,896]{4,3,2,1,0:T(8,128)(2,1)} %bitcast.37, ...), custom_call_target="tpu_custom_call" | custom-call | tf_op jit(solution)/shard_map/fetch/pallas_call | solution.py:67
  12.1 3.8 %columns.1 = (f32[8,128]{1,0:T(8,128)}, bf16[384,4608]{1,0:T(8,128)(2,1)}) custom-call(s32[1]{0:T(128)} %bitcast.10.refs_0_, bf16[384,8192]{1,0:T(8,128)(2,1)} %refs_1_.7, bf16[384,512]{1,0:T(8,128)(2,1)} %refs_2_.5, f32[8,128]{1,0:T(8,128)} %copy-done.31), custom_call_target="tpu_custom_call" | custom-call | tf_op jit(solution)/shard_map/columns/pallas_call | solution.py:67
  15.9 4.8 %collective-permute-start.11 = (bf16[384,4608]{1,0:T(8,128)(2,1)}, bf16[384,4608]{1,0:T(8,128)(2,1)S(1)}, u32[]{:S(2)}, u32[]{:S(2)}) collective-permute-start(bf16[384,4608]{1,0:T(8,128)(2,1)} %get-tuple-element.149), channel_id=1, source_target_pairs={{0,1},{1,0},{4,5},{5,4},{8,9},{9,8},{12,13},{13,12},{16,17},{17,16... | collective-permute-start | bytes 10616840 | tf_op jit(solution)/shard_map/ppermute | solution.py:320
  24.7 4.5 %fetch.6 = (f32[8,128]{1,0:T(8,128)S(1)}, bf16[2,256,896]{2,1,0:T(8,128)(2,1)S(1)}, bf16[2,256,896]{2,1,0:T(8,128)(2,1)}, bf16[2,256,896]{2,1,0:T(8,128)(2,1)}, ...) custom-call(s32[12]{0:T(128)S(1)} %stack.133.refs_0_, ...), custom_call_target="tpu_custom_call" | custom-call | tf_op jit(solution)/shard_map/fetch/pallas_call | solution.py:67
  38.3 3.8 %collective-permute-done.8.refs_2_ = bf16[256,896]{1,0:T(8,128)(2,1)S(1)} collective-permute-done((bf16[256,896]{1,0:T(8,128)(2,1)S(1)}, bf16[256,896]{1,0:T(8,128)(2,1)S(1)}, u32[]{:S(2)}, u32[]{:S(2)}) %collective-permute-start.8) | collective-permute-done | bytes 458784 | tf_op jit(solution)/shard_map/ppermute | solution.py:182
  42.1 2.2 %add.262 = (f32[8,128]{1,0:T(8,128)S(1)}, bf16[256,896]{1,0:T(8,128)(2,1)}) custom-call(bf16[2,256,896]{2,1,0:T(8,128)(2,1)S(1)} %copy-done.13, bf16[2,256,896]{2,1,0:T(8,128)(2,1)} %collective-permute-done.3.refs_1_, bf16[256,896]{1,0:T(8,128)(2,1)S(1)} %collective-permute-done.8.refs_2_, f32[8,128]{1,0:T(8,128)S(1)} %get-tuple-element.140.refs_3_), custom_call_target="tpu_custom_call" | custom-call | tf_op jit(solution)/shard_map/add/pallas_call | solution.py:67
  47.0 2.2 %add.263 = (f32[8,128]{1,0:T(8,128)S(1)}, bf16[256,896]{1,0:T(8,128)(2,1)}) custom-call(bf16[2,256,896]{2,1,0:T(8,128)(2,1)S(1)} %copy-done.13, bf16[2,256,896]{2,1,0:T(8,128)(2,1)} %collective-permute-done.3.refs_1_, bf16[256,896]{1,0:T(8,128)(2,1)S(1)} %collective-permute-done.7.refs_2_, f32[8,128]{1,0:T(8,128)S(1)} %get-tuple-element.141.refs_3_), custom_call_target="tpu_custom_call" | custom-call | tf_op jit(solution)/shard_map/add/pallas_call | solution.py:67
  51.8 3.6 %fetch.7 = (f32[8,128]{1,0:T(8,128)S(1)}, bf16[2,256,896]{2,1,0:T(8,128)(2,1)}, bf16[2,256,896]{2,1,0:T(8,128)(2,1)S(1)}, bf16[2,256,896]{2,1,0:T(8,128)(2,1)S(1)}, bf16[2,256,896]{2,1,0:T(8,128)(2,1)S(1)}) custom-call(s32[8]{0:T(128)S(1)} %stack.140.refs_0_, bf16[2,8,2,256,896]{4,3,2,1,0:T(8,128)(2,1)} %bitcast.39, f32[8,128]{1,0:T(8,128)S(1)} %get-tuple-element.144.refs_2_), custom_call_target="tpu_custom_call" | custom-call | tf_op jit(solution)/shard_map/fetch/pallas_call | solution.py:67
  55.5 2.4 %add.264 = (f32[8,128]{1,0:T(8,128)S(1)}, bf16[256,896]{1,0:T(8,128)(2,1)}) custom-call(bf16[2,256,896]{2,1,0:T(8,128)(2,1)S(1)} %copy-done.11, bf16[2,256,896]{2,1,0:T(8,128)(2,1)S(1)} %copy-done.15, bf16[256,896]{1,0:T(8,128)(2,1)} %collective-permute-done.10.refs_2_, f32[8,128]{1,0:T(8,128)S(1)} %get-tuple-element.145.refs_3_), custom_call_target="tpu_custom_call" | custom-call | tf_op jit(solution)/shard_map/add/pallas_call | solution.py:67
  59.3 2.0 %add.265 = (f32[8,128]{1,0:T(8,128)S(1)}, bf16[256,896]{1,0:T(8,128)(2,1)}) custom-call(bf16[2,256,896]{2,1,0:T(8,128)(2,1)S(1)} %copy-done.11, bf16[2,256,896]{2,1,0:T(8,128)(2,1)S(1)} %copy-done.15, bf16[256,896]{1,0:T(8,128)(2,1)} %collective-permute-done.9.refs_2_, f32[8,128]{1,0:T(8,128)S(1)} %get-tuple-element.146.refs_3_), custom_call_target="tpu_custom_call" | custom-call | tf_op jit(solution)/shard_map/add/pallas_call | solution.py:67
  61.9 2.8 %copy-done = bf16[384,8192]{1,0:T(8,128)(2,1)S(1)} copy-done((bf16[384,8192]{1,0:T(8,128)(2,1)S(1)}, bf16[384,8192]{1,0:T(8,128)(2,1)}, u32[]{:S(2)}) %copy-start) | copy-done | bytes 6291480
  64.7 2.2 %copy-done.3 = bf16[1,4096,512]{2,1,0:T(8,128)(2,1)S(1)} copy-done((bf16[1,4096,512]{2,1,0:T(8,128)(2,1)S(1)}, bf16[1,4096,512]{2,1,0:T(8,128)(2,1)}, u32[]{:S(2)}) %copy-start.3) | copy-done | bytes 4194328
  66.9 3.4 %own_keys.1 = (f32[8,128]{1,0:T(8,128)S(1)}, f32[384,512]{1,0:T(8,128)S(1)}) custom-call(s32[2]{0:T(128)S(1)} %pad_add_fusion.refs_0_, bf16[384,8192]{1,0:T(8,128)(2,1)S(1)} %copy-done, bf16[4096,512]{1,0:T(8,128)(2,1)S(1)} %bitcast.33, f32[8,128]{1,0:T(8,128)S(1)} %get-tuple-element.147.refs_3_), custom_call_target="tpu_custom_call" | custom-call | tf_op jit(solution)/shard_map/own_keys/pallas_call | solution.py:67
  75.8 2.5 %collective-permute-start.12 = (bf16[384,4608]{1,0:T(8,128)(2,1)}, bf16[384,4608]{1,0:T(8,128)(2,1)}, u32[]{:S(2)}, u32[]{:S(2)}) collective-permute-start(bf16[384,4608]{1,0:T(8,128)(2,1)} %get-tuple-element.149), channel_id=1, source_target_pairs={{2,3},{3,2},{6,7},{7,6},{10,11},{11,10},{14,15},{15,14},{18,19},{1... | collective-permute-start | bytes 10616840 | tf_op jit(solution)/shard_map/ppermute | solution.py:320
  78.3 2.2 %own_term.2 = (f32[8,128]{1,0:T(8,128)S(1)}, bf16[4096,512]{1,0:T(8,128)(2,1)S(1)}) custom-call(s32[2]{0:T(128)S(1)} %pad_add_fusion.refs_0_, bf16[384,8192]{1,0:T(8,128)(2,1)S(1)} %copy-done, bf16[384,512]{1,0:T(8,128)(2,1)S(1)} %copy-done.23, f32[8,128]{1,0:T(8,128)S(1)} %get-tuple-element.163.refs_3_), custom_call_target="tpu_custom_call" | custom-call | tf_op jit(solution)/shard_map/own_term/pallas_call | solution.py:67
  83.5 2.2 %collective-permute-done.21.refs_2_ = bf16[256,896]{1,0:T(8,128)(2,1)S(1)} collective-permute-done((bf16[256,896]{1,0:T(8,128)(2,1)S(1)}, bf16[256,896]{1,0:T(8,128)(2,1)S(1)}, u32[]{:S(2)}, u32[]{:S(2)}) %collective-permute-start.21) | collective-permute-done | bytes 458784 | tf_op jit(solution)/shard_map/ppermute | solution.py:182
  88.5 2.2 %own_term.3 = (f32[8,128]{1,0:T(8,128)S(1)}, bf16[4096,512]{1,0:T(8,128)(2,1)S(1)}) custom-call(s32[2]{0:T(128)S(1)} %pad_add_fusion.refs_0_, bf16[384,8192]{1,0:T(8,128)(2,1)S(1)} %copy-done, bf16[384,512]{1,0:T(8,128)(2,1)S(1)} %copy-done.23, bf16[4096,512]{1,0:T(8,128)(2,1)S(1)} %get-tuple-element.166.refs_3_, ...), custom_call_target="tpu_custom_call", output_to_operand_aliasing={{1}: (3, {})} | custom-call | tf_op jit(solution)/shard_map/own_term/pallas_call | solution.py:67
  90.7 2.1 %add.270 = (f32[8,128]{1,0:T(8,128)S(1)}, bf16[256,896]{1,0:T(8,128)(2,1)S(1)}) custom-call(bf16[2,256,896]{2,1,0:T(8,128)(2,1)S(1)} %copy-done.17, bf16[2,256,896]{2,1,0:T(8,128)(2,1)} %collective-permute-done.14.refs_1_, bf16[256,896]{1,0:T(8,128)(2,1)S(1)} %collective-permute-done.20.refs_2_, f32[8,128]{1,0:T(8,128)S(1)} %get-tuple-element.170.refs_3_), custom_call_target="tpu_custom_call" | custom-call | tf_op jit(solution)/shard_map/add/pallas_call | solution.py:67
  98.4 3.0 %collective-permute-done.22.refs_2_ = bf16[256,896]{1,0:T(8,128)(2,1)S(1)} collective-permute-done((bf16[256,896]{1,0:T(8,128)(2,1)S(1)}, bf16[256,896]{1,0:T(8,128)(2,1)S(1)}, u32[]{:S(2)}, u32[]{:S(2)}) %collective-permute-start.22) | collective-permute-done | bytes 458784 | tf_op jit(solution)/shard_map/ppermute | solution.py:182
  103.8 2.4 %collective-permute-done.25.refs_2_ = bf16[256,896]{1,0:T(8,128)(2,1)S(1)} collective-permute-done((bf16[256,896]{1,0:T(8,128)(2,1)S(1)}, bf16[256,896]{1,0:T(8,128)(2,1)S(1)}, u32[]{:S(2)}, u32[]{:S(2)}) %collective-permute-start.25) | collective-permute-done | bytes 458784 | tf_op jit(solution)/shard_map/ppermute | solution.py:182
  110.3 2.1 %place.9 = (f32[8,128]{1,0:T(8,128)S(1)}, bf16[2,16,256,896]{3,2,1,0:T(8,128)(2,1)}) custom-call(s32[16]{0:T(128)S(1)} %stack.157.refs_0_, bf16[256,896]{1,0:T(8,128)(2,1)} %get-tuple-element.175.refs_1_, bf16[256,896]{1,0:T(8,128)(2,1)} %get-tuple-element.178.refs_2_, f32[8,128]{1,0:T(8,128)S(1)} %get-tuple-element.179.refs_3_), custom_call_target="tpu_custom_call" | custom-call | tf_op jit(solution)/shard_map/place/pallas_call | solution.py:67
  113.5 3.7 %collective-permute-done.29.refs_4_ = bf16[256,896]{1,0:T(8,128)(2,1)} collective-permute-done((bf16[256,896]{1,0:T(8,128)(2,1)}, bf16[256,896]{1,0:T(8,128)(2,1)}, u32[]{:S(2)}, u32[]{:S(2)}) %collective-permute-start.29) | collective-permute-done | bytes 458784 | tf_op jit(solution)/shard_map/ppermute | solution.py:182
  122.6 2.4 %place.10 = (f32[8,128]{1,0:T(8,128)S(1)}, bf16[2,16,256,896]{3,2,1,0:T(8,128)(2,1)}) custom-call(s32[16]{0:T(128)S(1)} %stack.157.refs_0_, bf16[256,896]{1,0:T(8,128)(2,1)S(1)} %collective-permute-done.27.refs_1_, bf16[256,896]{1,0:T(8,128)(2,1)S(1)} %collective-permute-done.28.refs_2_, ...), custom_call_target="tpu_custom_call", output_to_operand_aliasing={{1}: (5, {})} | custom-call | tf_op jit(solution)/shard_map/place/pallas_call | solution.py:67
  130.5 3.1 %collective-permute-done.33.refs_3_ = bf16[256,896]{1,0:T(8,128)(2,1)S(1)} collective-permute-done((bf16[256,896]{1,0:T(8,128)(2,1)S(1)}, bf16[256,896]{1,0:T(8,128)(2,1)S(1)}, u32[]{:S(2)}, u32[]{:S(2)}) %collective-permute-start.33) | collective-permute-done | bytes 458784 | tf_op jit(solution)/shard_map/ppermute | solution.py:182
  134.6 3.9 %collective-permute-done.36.refs_4_ = bf16[256,896]{1,0:T(8,128)(2,1)S(1)} collective-permute-done((bf16[256,896]{1,0:T(8,128)(2,1)S(1)}, bf16[256,896]{1,0:T(8,128)(2,1)S(1)}, u32[]{:S(2)}, u32[]{:S(2)}) %collective-permute-start.36) | collective-permute-done | bytes 458784 | tf_op jit(solution)/shard_map/ppermute | solution.py:182
  144.4 3.9 %collective-permute-done.42.refs_4_ = bf16[256,896]{1,0:T(8,128)(2,1)S(1)} collective-permute-done((bf16[256,896]{1,0:T(8,128)(2,1)S(1)}, bf16[256,896]{1,0:T(8,128)(2,1)S(1)}, u32[]{:S(2)}, u32[]{:S(2)}) %collective-permute-start.42) | collective-permute-done | bytes 458784 | tf_op jit(solution)/shard_map/ppermute | solution.py:182
  149.3 4.7 %other_keys.1 = (f32[8,128]{1,0:T(8,128)S(1)}, bf16[384,512]{1,0:T(8,128)(2,1)S(1)}) custom-call(s32[2]{0:T(128)S(1)} %pad_add_fusion.refs_0_, bf16[384,4608]{1,0:T(8,128)(2,1)S(1)} %collective-permute-done.11.refs_5_.refs_1_.refs_2_.refs_4_, bf16[384,4608]{1,0:T(8,128)(2,1)} %collective-permute-done.12.refs_2_.refs_3_.refs_5_, ...), custom_call_target="tpu_custom_call" | custom-call | tf_op jit(solution)/shard_map/other_keys/pallas_call | solution.py:67
  159.2 4.5 %grad.2 = (f32[8,128]{1,0:T(8,128)S(1)}, bf16[4096,512]{1,0:T(8,128)(2,1)}) custom-call(s32[2]{0:T(128)S(1)} %pad_add_fusion.refs_0_, bf16[4096,512]{1,0:T(8,128)(2,1)S(1)} %copy-done.2, bf16[384,4608]{1,0:T(8,128)(2,1)S(1)} %collective-permute-done.11.refs_5_.refs_1_.refs_2_.refs_4_, bf16[384,4608]{1,0:T(8,128)(2,1)} %collective-permute-done.12.refs_2_.refs_3_.refs_5_, ...), custom_call_target="tpu_custom_call" | custom-call | tf_op jit(solution)/shard_map/grad/pallas_call | solution.py:67
  167.2 2.7 %collective-permute-done.51.refs_4_ = bf16[256,896]{1,0:T(8,128)(2,1)S(1)} collective-permute-done((bf16[256,896]{1,0:T(8,128)(2,1)S(1)}, bf16[256,896]{1,0:T(8,128)(2,1)S(1)}, u32[]{:S(2)}, u32[]{:S(2)}) %collective-permute-start.51) | collective-permute-done | bytes 458784 | tf_op jit(solution)/shard_map/ppermute | solution.py:182
  171.8 2.5 %collective-permute-start.37 = (bf16[384,512]{1,0:T(8,128)(2,1)S(1)}, bf16[384,512]{1,0:T(8,128)(2,1)S(1)}, u32[]{:S(2)}, u32[]{:S(2)}) collective-permute-start(bf16[384,512]{1,0:T(8,128)(2,1)S(1)} %get-tuple-element.202), channel_id=1, source_target_pairs={{0,1},{1,0},{4,5},{5,4},{8,9},{9,8},{12,13},{13,12},{16,17},{17,16... | collective-permute-start | bytes 1179656 | tf_op jit(solution)/shard_map/ppermute | solution.py:320
  174.2 4.5 %grad.3 = (f32[8,128]{1,0:T(8,128)S(1)}, bf16[4096,512]{1,0:T(8,128)(2,1)}) custom-call(s32[2]{0:T(128)S(1)} %pad_add_fusion.refs_0_, bf16[4096,512]{1,0:T(8,128)(2,1)S(1)} %copy-done.2, bf16[384,4608]{1,0:T(8,128)(2,1)S(1)} %collective-permute-done.11.refs_5_.refs_1_.refs_2_.refs_4_, ...), custom_call_target="tpu_custom_call", output_to_operand_aliasing={{1}: (6, {})} | custom-call | tf_op jit(solution)/shard_map/grad/pallas_call | solution.py:67
  178.8 1.8 place.15
  (194 shorter events, 87.7 us)
Async XLA Ops:
  9.2 22.9 %collective-permute-start.4 = (bf16[2,256,896]{2,1,0:T(8,128)(2,1)}, bf16[2,256,896]{2,1,0:T(8,128)(2,1)}, u32[]{:S(2)}, u32[]{:S(2)}) collective-permute-start(bf16[2,256,896]{2,1,0:T(8,128)(2,1)} %get-tuple-element.133), channel_id=1, source_target_pairs={{0,2},{2,0},{4,6},{6,4},{8,10},{10,8},{12,14},{14,12},{16,18},{18,... | collective-permute-start | bytes 2752520 | tf_op jit(solution)/shard_map/ppermute | solution.py:182
  9.6 28.6 %collective-permute-start.3 = (bf16[2,256,896]{2,1,0:T(8,128)(2,1)}, bf16[2,256,896]{2,1,0:T(8,128)(2,1)}, u32[]{:S(2)}, u32[]{:S(2)}) collective-permute-start(bf16[2,256,896]{2,1,0:T(8,128)(2,1)} %get-tuple-element.131), channel_id=1, source_target_pairs={{0,2},{2,0},{4,6},{6,4},{8,10},{10,8},{12,14},{14,12},{16,18},{18,... | collective-permute-start | bytes 2752520 | tf_op jit(solution)/shard_map/ppermute | solution.py:182
  15.9 85.4 %collective-permute-start.11 = (bf16[384,4608]{1,0:T(8,128)(2,1)}, bf16[384,4608]{1,0:T(8,128)(2,1)S(1)}, u32[]{:S(2)}, u32[]{:S(2)}) collective-permute-start(bf16[384,4608]{1,0:T(8,128)(2,1)} %get-tuple-element.149), channel_id=1, source_target_pairs={{0,1},{1,0},{4,5},{5,4},{8,9},{9,8},{12,13},{13,12},{16,17},{17,16... | collective-permute-start | bytes 10616840 | tf_op jit(solution)/shard_map/ppermute | solution.py:320
  20.7 11.4 %collective-permute-start.6 = (bf16[256,896]{1,0:T(8,128)(2,1)}, bf16[256,896]{1,0:T(8,128)(2,1)}, u32[]{:S(2)}, u32[]{:S(2)}) collective-permute-start(bf16[256,896]{1,0:T(8,128)(2,1)} %get-tuple-element.135), channel_id=1, source_target_pairs={{0,8},{2,6},{8,16},{10,2},{16,24},{18,10},{24,28},{26,18},{28,20},... | collective-permute-start | bytes 1376264 | tf_op jit(solution)/shard_map/ppermute | solution.py:182
  22.4 12.9 %collective-permute-start.5 = (bf16[256,896]{1,0:T(8,128)(2,1)}, bf16[256,896]{1,0:T(8,128)(2,1)}, u32[]{:S(2)}, u32[]{:S(2)}) collective-permute-start(bf16[256,896]{1,0:T(8,128)(2,1)} %get-tuple-element.134), channel_id=1, source_target_pairs={{0,8},{2,6},{8,16},{10,2},{16,24},{18,10},{24,28},{26,18},{28,20},... | collective-permute-start | bytes 1376264 | tf_op jit(solution)/shard_map/ppermute | solution.py:182
  32.1 18.7 %collective-permute-start.2 = (bf16[2,256,896]{2,1,0:T(8,128)(2,1)S(1)}, bf16[2,256,896]{2,1,0:T(8,128)(2,1)S(1)}, u32[]{:S(2)}, u32[]{:S(2)}) collective-permute-start(bf16[2,256,896]{2,1,0:T(8,128)(2,1)S(1)} %get-tuple-element.129), channel_id=1, source_target_pairs={{0,2},{2,0},{4,6},{6,4},{8,10},{10,8},{12,14},{14,12},{16,18},{18,... | collective-permute-start | bytes 2752520 | tf_op jit(solution)/shard_map/ppermute | solution.py:182
  36.7 10.3 %collective-permute-start.7 = (bf16[256,896]{1,0:T(8,128)(2,1)S(1)}, bf16[256,896]{1,0:T(8,128)(2,1)S(1)}, u32[]{:S(2)}, u32[]{:S(2)}) collective-permute-start(bf16[256,896]{1,0:T(8,128)(2,1)S(1)} %get-tuple-element.138), channel_id=1, source_target_pairs={{0,8},{2,6},{8,16},{10,2},{16,24},{18,10},{24,28},{26,18},{28,20},... | collective-permute-start | bytes 1376264 | tf_op jit(solution)/shard_map/ppermute | solution.py:182
  38.3 23.6 %collective-permute-start.16 = (bf16[2,256,896]{2,1,0:T(8,128)(2,1)}, bf16[2,256,896]{2,1,0:T(8,128)(2,1)}, u32[]{:S(2)}, u32[]{:S(2)}) collective-permute-start(bf16[2,256,896]{2,1,0:T(8,128)(2,1)} %get-tuple-element.157), channel_id=1, source_target_pairs={{0,2},{2,0},{4,6},{6,4},{8,10},{10,8},{12,14},{14,12},{16,18},{18,... | collective-permute-start | bytes 2752520 | tf_op jit(solution)/shard_map/ppermute | solution.py:182
  44.3 11.2 %collective-permute-start.10 = (bf16[256,896]{1,0:T(8,128)(2,1)}, bf16[256,896]{1,0:T(8,128)(2,1)}, u32[]{:S(2)}, u32[]{:S(2)}) collective-permute-start(bf16[256,896]{1,0:T(8,128)(2,1)} %get-tuple-element.143), channel_id=1, source_target_pairs={{0,8},{2,6},{8,16},{10,2},{16,24},{18,10},{24,28},{26,18},{28,20},... | collective-permute-start | bytes 1376264 | tf_op jit(solution)/shard_map/ppermute | solution.py:182
  51.7 24.1 %collective-permute-start.15 = (bf16[2,256,896]{2,1,0:T(8,128)(2,1)}, bf16[2,256,896]{2,1,0:T(8,128)(2,1)}, u32[]{:S(2)}, u32[]{:S(2)}) collective-permute-start(bf16[2,256,896]{2,1,0:T(8,128)(2,1)} %get-tuple-element.155), channel_id=1, source_target_pairs={{0,2},{2,0},{4,6},{6,4},{8,10},{10,8},{12,14},{14,12},{16,18},{18,... | collective-permute-start | bytes 2752520 | tf_op jit(solution)/shard_map/ppermute | solution.py:182
  57.8 12.6 %collective-permute-start.17 = (bf16[256,896]{1,0:T(8,128)(2,1)}, bf16[256,896]{1,0:T(8,128)(2,1)}, u32[]{:S(2)}, u32[]{:S(2)}) collective-permute-start(bf16[256,896]{1,0:T(8,128)(2,1)} %get-tuple-element.158), channel_id=1, source_target_pairs={{0,8},{2,6},{8,16},{10,2},{16,24},{18,10},{24,28},{26,18},{28,20},... | collective-permute-start | bytes 1376264 | tf_op jit(solution)/shard_map/ppermute | solution.py:182
  61.4 12.2 %collective-permute-start.19 = (bf16[256,896]{1,0:T(8,128)(2,1)}, bf16[256,896]{1,0:T(8,128)(2,1)}, u32[]{:S(2)}, u32[]{:S(2)}) collective-permute-start(bf16[256,896]{1,0:T(8,128)(2,1)} %get-tuple-element.161), channel_id=1, source_target_pairs={{0,8},{2,6},{8,16},{10,2},{16,24},{18,10},{24,28},{26,18},{28,20},... | collective-permute-start | bytes 1376264 | tf_op jit(solution)/shard_map/ppermute | solution.py:182
  61.8 25.3 %collective-permute-start.14 = (bf16[2,256,896]{2,1,0:T(8,128)(2,1)}, bf16[2,256,896]{2,1,0:T(8,128)(2,1)}, u32[]{:S(2)}, u32[]{:S(2)}) collective-permute-start(bf16[2,256,896]{2,1,0:T(8,128)(2,1)} %get-tuple-element.153), channel_id=1, source_target_pairs={{0,2},{2,0},{4,6},{6,4},{8,10},{10,8},{12,14},{14,12},{16,18},{18,... | collective-permute-start | bytes 2752520 | tf_op jit(solution)/shard_map/ppermute | solution.py:182
  75.1 10.6 %collective-permute-start.21 = (bf16[256,896]{1,0:T(8,128)(2,1)S(1)}, bf16[256,896]{1,0:T(8,128)(2,1)S(1)}, u32[]{:S(2)}, u32[]{:S(2)}) collective-permute-start(bf16[256,896]{1,0:T(8,128)(2,1)S(1)} %get-tuple-element.167), channel_id=1, source_target_pairs={{0,8},{2,6},{8,16},{10,2},{16,24},{18,10},{24,28},{26,18},{28,20},... | collective-permute-start | bytes 1376264 | tf_op jit(solution)/shard_map/ppermute | solution.py:182
  75.8 73.5 %collective-permute-start.12 = (bf16[384,4608]{1,0:T(8,128)(2,1)}, bf16[384,4608]{1,0:T(8,128)(2,1)}, u32[]{:S(2)}, u32[]{:S(2)}) collective-permute-start(bf16[384,4608]{1,0:T(8,128)(2,1)} %get-tuple-element.149), channel_id=1, source_target_pairs={{2,3},{3,2},{6,7},{7,6},{10,11},{11,10},{14,15},{15,14},{18,19},{1... | collective-permute-start | bytes 10616840 | tf_op jit(solution)/shard_map/ppermute | solution.py:320
  85.7 12.7 %collective-permute-start.13 = (bf16[2,256,896]{2,1,0:T(8,128)(2,1)S(1)}, bf16[2,256,896]{2,1,0:T(8,128)(2,1)S(1)}, u32[]{:S(2)}, u32[]{:S(2)}) collective-permute-start(bf16[2,256,896]{2,1,0:T(8,128)(2,1)S(1)} %copy-done.33), channel_id=1, source_target_pairs={{0,2},{2,0},{4,6},{6,4},{8,10},{10,8},{12,14},{14,12},{16,18},{18,... | collective-permute-start | bytes 2752520 | tf_op jit(solution)/shard_map/ppermute | solution.py:182
  109.7 12.3 %collective-permute-start.27 = (bf16[256,896]{1,0:T(8,128)(2,1)}, bf16[256,896]{1,0:T(8,128)(2,1)S(1)}, u32[]{:S(2)}, u32[]{:S(2)}) collective-permute-start(bf16[256,896]{1,0:T(8,128)(2,1)} %get-tuple-element.175.refs_1_), channel_id=1, source_target_pairs={{0,2},{2,0},{4,6},{6,4},{8,10},{10,8},{12,14},{14,12},{16,18},{18,... | collective-permute-start | bytes 1376264 | tf_op jit(solution)/shard_map/ppermute | solution.py:182
  109.8 12.3 %collective-permute-start.28 = (bf16[256,896]{1,0:T(8,128)(2,1)}, bf16[256,896]{1,0:T(8,128)(2,1)S(1)}, u32[]{:S(2)}, u32[]{:S(2)}) collective-permute-start(bf16[256,896]{1,0:T(8,128)(2,1)} %get-tuple-element.178.refs_2_), channel_id=1, source_target_pairs={{0,2},{2,0},{4,6},{6,4},{8,10},{10,8},{12,14},{14,12},{16,18},{18,... | collective-permute-start | bytes 1376264 | tf_op jit(solution)/shard_map/ppermute | solution.py:182
  112.4 12.6 %collective-permute-start.26 = (bf16[256,896]{1,0:T(8,128)(2,1)}, bf16[256,896]{1,0:T(8,128)(2,1)S(1)}, u32[]{:S(2)}, u32[]{:S(2)}) collective-permute-start(bf16[256,896]{1,0:T(8,128)(2,1)} %collective-permute-done.24.refs_3_), channel_id=1, source_target_pairs={{0,8},{2,6},{8,16},{10,2},{16,24},{18,10},{24,28},{26,18},{28,20},... | collective-permute-start | bytes 1376264 | tf_op jit(solution)/shard_map/ppermute | solution.py:182
  126.9 11.6 %collective-permute-start.36 = (bf16[256,896]{1,0:T(8,128)(2,1)S(1)}, bf16[256,896]{1,0:T(8,128)(2,1)S(1)}, u32[]{:S(2)}, u32[]{:S(2)}) collective-permute-start(bf16[256,896]{1,0:T(8,128)(2,1)S(1)} %collective-permute-done.31.refs_4_), channel_id=1, source_target_pairs={{0,8},{2,6},{8,16},{10,2},{16,24},{18,10},{24,28},{26,18},{28,20},... | collective-permute-start | bytes 1376264 | tf_op jit(solution)/shard_map/ppermute | solution.py:182
  128.2 11.3 %collective-permute-start.30 = (bf16[256,896]{1,0:T(8,128)(2,1)S(1)}, bf16[256,896]{1,0:T(8,128)(2,1)S(1)}, u32[]{:S(2)}, u32[]{:S(2)}) collective-permute-start(bf16[256,896]{1,0:T(8,128)(2,1)S(1)} %collective-permute-done.26.refs_3_), channel_id=1, source_target_pairs={{0,2},{2,0},{4,6},{6,4},{8,10},{10,8},{12,14},{14,12},{16,18},{18,... | collective-permute-start | bytes 1376264 | tf_op jit(solution)/shard_map/ppermute | solution.py:182
  128.2 11.3 %collective-permute-start.32 = (bf16[256,896]{1,0:T(8,128)(2,1)S(1)}, bf16[256,896]{1,0:T(8,128)(2,1)S(1)}, u32[]{:S(2)}, u32[]{:S(2)}) collective-permute-start(bf16[256,896]{1,0:T(8,128)(2,1)S(1)} %collective-permute-done.31.refs_4_), channel_id=1, source_target_pairs={{0,2},{2,0},{4,6},{6,4},{8,10},{10,8},{12,14},{14,12},{16,18},{18,... | collective-permute-start | bytes 1376264 | tf_op jit(solution)/shard_map/ppermute | solution.py:182
  139.5 14.6 %collective-permute-start.39 = (bf16[256,896]{1,0:T(8,128)(2,1)S(1)}, bf16[256,896]{1,0:T(8,128)(2,1)S(1)}, u32[]{:S(2)}, u32[]{:S(2)}) collective-permute-start(bf16[256,896]{1,0:T(8,128)(2,1)S(1)} %collective-permute-done.33.refs_3_), channel_id=1, source_target_pairs={{0,2},{2,0},{4,6},{6,4},{8,10},{10,8},{12,14},{14,12},{16,18},{18,... | collective-permute-start | bytes 1376264 | tf_op jit(solution)/shard_map/ppermute | solution.py:182
  139.5 15.1 %collective-permute-start.40 = (bf16[256,896]{1,0:T(8,128)(2,1)S(1)}, bf16[256,896]{1,0:T(8,128)(2,1)S(1)}, u32[]{:S(2)}, u32[]{:S(2)}) collective-permute-start(bf16[256,896]{1,0:T(8,128)(2,1)S(1)} %collective-permute-done.36.refs_4_), channel_id=1, source_target_pairs={{0,2},{2,0},{4,6},{6,4},{8,10},{10,8},{12,14},{14,12},{16,18},{18,... | collective-permute-start | bytes 1376264 | tf_op jit(solution)/shard_map/ppermute | solution.py:182
  143.4 13.0 %collective-permute-start.45 = (bf16[256,896]{1,0:T(8,128)(2,1)S(1)}, bf16[256,896]{1,0:T(8,128)(2,1)S(1)}, u32[]{:S(2)}, u32[]{:S(2)}) collective-permute-start(bf16[256,896]{1,0:T(8,128)(2,1)S(1)} %collective-permute-done.41.refs_3_), channel_id=1, source_target_pairs={{0,8},{2,6},{8,16},{10,2},{16,24},{18,10},{24,28},{26,18},{28,20},... | collective-permute-start | bytes 1376264 | tf_op jit(solution)/shard_map/ppermute | solution.py:182
  158.2 11.7 %collective-permute-start.51 = (bf16[256,896]{1,0:T(8,128)(2,1)S(1)}, bf16[256,896]{1,0:T(8,128)(2,1)S(1)}, u32[]{:S(2)}, u32[]{:S(2)}) collective-permute-start(bf16[256,896]{1,0:T(8,128)(2,1)S(1)} %collective-permute-done.46.refs_4_), channel_id=1, source_target_pairs={{0,8},{2,6},{8,16},{10,2},{16,24},{18,10},{24,28},{26,18},{28,20},... | collective-permute-start | bytes 1376264 | tf_op jit(solution)/shard_map/ppermute | solution.py:182
  159.2 12.6 %collective-permute-start.49 = (bf16[256,896]{1,0:T(8,128)(2,1)S(1)}, bf16[256,896]{1,0:T(8,128)(2,1)S(1)}, u32[]{:S(2)}, u32[]{:S(2)}) collective-permute-start(bf16[256,896]{1,0:T(8,128)(2,1)S(1)} %collective-permute-done.45.refs_3_), channel_id=1, source_target_pairs={{0,2},{2,0},{4,6},{6,4},{8,10},{10,8},{12,14},{14,12},{16,18},{18,... | collective-permute-start | bytes 1376264 | tf_op jit(solution)/shard_map/ppermute | solution.py:182
  163.7 15.1 %collective-permute-start.50 = (bf16[256,896]{1,0:T(8,128)(2,1)S(1)}, bf16[256,896]{1,0:T(8,128)(2,1)S(1)}, u32[]{:S(2)}, u32[]{:S(2)}) collective-permute-start(bf16[256,896]{1,0:T(8,128)(2,1)S(1)} %collective-permute-done.46.refs_4_), channel_id=1, source_target_pairs={{0,2},{2,0},{4,6},{6,4},{8,10},{10,8},{12,14},{14,12},{16,18},{18,... | collective-permute-start | bytes 1376264 | tf_op jit(solution)/shard_map/ppermute | solution.py:182
  166.0 14.6 %collective-permute-start.48 = (bf16[256,896]{1,0:T(8,128)(2,1)S(1)}, bf16[256,896]{1,0:T(8,128)(2,1)S(1)}, u32[]{:S(2)}, u32[]{:S(2)}) collective-permute-start(bf16[256,896]{1,0:T(8,128)(2,1)S(1)} %collective-permute-done.47.refs_3_), channel_id=1, source_target_pairs={{0,8},{2,6},{8,16},{10,2},{16,24},{18,10},{24,28},{26,18},{28,20},... | collective-permute-start | bytes 1376264 | tf_op jit(solution)/shard_map/ppermute | solution.py:182
  169.9 11.2 %collective-permute-start.53 = (bf16[256,896]{1,0:T(8,128)(2,1)S(1)}, bf16[256,896]{1,0:T(8,128)(2,1)S(1)}, u32[]{:S(2)}, u32[]{:S(2)}) collective-permute-start(bf16[256,896]{1,0:T(8,128)(2,1)S(1)} %collective-permute-done.51.refs_4_), channel_id=1, source_target_pairs={{0,8},{2,6},{8,16},{10,2},{16,24},{18,10},{24,28},{26,18},{28,20},... | collective-permute-start | bytes 1376264 | tf_op jit(solution)/shard_map/ppermute | solution.py:182
  171.1 10.1 %collective-permute-start.38 = (bf16[384,512]{1,0:T(8,128)(2,1)S(1)}, bf16[384,512]{1,0:T(8,128)(2,1)S(1)}, u32[]{:S(2)}, u32[]{:S(2)}) collective-permute-start(bf16[384,512]{1,0:T(8,128)(2,1)S(1)} %get-tuple-element.202), channel_id=1, source_target_pairs={{2,3},{3,2},{6,7},{7,6},{10,11},{11,10},{14,15},{15,14},{18,19},{1... | collective-permute-start | bytes 1179656 | tf_op jit(solution)/shard_map/ppermute | solution.py:320
  171.8 11.0 %collective-permute-start.37 = (bf16[384,512]{1,0:T(8,128)(2,1)S(1)}, bf16[384,512]{1,0:T(8,128)(2,1)S(1)}, u32[]{:S(2)}, u32[]{:S(2)}) collective-permute-start(bf16[384,512]{1,0:T(8,128)(2,1)S(1)} %get-tuple-element.202), channel_id=1, source_target_pairs={{0,1},{1,0},{4,5},{5,4},{8,9},{9,8},{12,13},{13,12},{16,17},{17,16... | collective-permute-start | bytes 1179656 | tf_op jit(solution)/shard_map/ppermute | solution.py:320
  (59 other events, 393.9 us)

commit v3 on v2

v3 whole, which is shorter than its diff:
```python
import jax
import jax.numpy as jnp
from jax import lax
from jax.experimental import pallas as pl
from jax.experimental.pallas import tpu as pltpu
from jax.sharding import PartitionSpec as P

outer_rate = 0.7
momentum_decay = 0.9
f32 = jnp.float32
bf16 = jnp.bfloat16
after = lax.optimization_barrier


def ring_chip(pos, chips):
    return jnp.where(pos < chips // 2, 2 * pos, 2 * (chips - 1 - pos) + 1)


def ring_pos(chip, chips):
    return jnp.where(chip % 2 == 0, chip // 2, chips - 1 - chip // 2)


def ring_perms(n):
    chips = n // 2
    order = [2 * p if p < chips // 2 else 2 * (chips - 1 - p) + 1 for p in range(chips)]
    step = [(2 * order[p] + c, 2 * order[(p + 1 - 2 * c) % chips] + c) for p in range(chips) for c in range(2)]
    swap = [(r, r ^ 1) for r in range(n)]
    return step, swap


in_hbm = pl.BlockSpec(memory_space=pltpu.HBM)
in_smem = pl.BlockSpec(memory_space=pltpu.SMEM)
in_vmem = pl.BlockSpec(memory_space=pltpu.VMEM)


def in_place(value):
    return pltpu.with_memory_space_constraint(value, pltpu.HBM)


class Chain:
    def __init__(self):
        self.token = None
        self.gates = []

    def call(self, kernel, name, out_shape, in_specs, out_specs, scratch, *operands, aliases={}, grant=8, where=None,
             steps=1):
        single = not isinstance(out_shape, list)
        out_shape, out_specs = ([out_shape], [out_specs]) if single else (out_shape, out_specs)
        extra = self.gates + ([] if self.token is None else [self.token])
        self.gates = []
        lead, inputs = int(where is not None), len(operands)

        def body(*refs):
            rest = refs[lead:]
            return kernel(*refs[:lead], *rest[:inputs], *rest[inputs + len(extra) + 1:])

        out_shape = [jax.ShapeDtypeStruct((8, 128), f32)] + out_shape
        in_specs = in_specs + [pl.BlockSpec(memory_space=pl.ANY)] * len(extra)
        out_specs = [pl.BlockSpec(memory_space=pl.ANY)] + out_specs
        params = dict(
            out_shape=out_shape,
            input_output_aliases={i + lead: o + 1 for i, o in aliases.items()},
            compiler_params=pltpu.CompilerParams(vmem_limit_bytes=grant * 2**20),
            cost_estimate=pl.CostEstimate(flops=0, bytes_accessed=0, transcendentals=0),
            name=name,
        )
        if where is None:
            params.update(in_specs=in_specs, out_specs=out_specs, scratch_shapes=scratch)
        else:
            params.update(grid_spec=pltpu.PrefetchScalarGridSpec(
                num_scalar_prefetch=1, grid=(steps,), in_specs=in_specs, out_specs=out_specs, scratch_shapes=scratch
            ))
        self.token, *outs = pl.pallas_call(body, **params)(*([] if where is None else [where]), *operands, *extra)
        return outs[0] if single else outs


def unit_type(rows, cols, kind=bf16):
    return jax.ShapeDtypeStruct((rows, cols), kind)


def run_copies(copies):
    for copy in copies:
        copy.start()
    return copies


def finish(copies):
    for copy in copies:
        copy.wait()


def follow(chain, value, gate):
    chain.gates = [gate]
    return chain.call(
        lambda *refs: None, "follow", jax.ShapeDtypeStruct(value.shape, value.dtype), [in_hbm], in_hbm, [], value,
        aliases={0: 0},
    )


def place(chain, gathered, shape, index, entries):
    places = [entry for _, entry in entries]
    values = [value for value, _ in entries]
    aliased = gathered is not None

    def kernel(index_ref, *refs):
        out, sems = refs[len(places) + aliased], refs[-1]
        finish(run_copies([
            pltpu.make_async_copy(refs[i], out.at[m, index_ref[d]], sems.at[i]) for i, (m, d) in enumerate(places)
        ]))

    return chain.call(
        kernel, "place", jax.ShapeDtypeStruct(shape, bf16),
        [in_smem] + [in_vmem] * len(values) + [in_hbm] * aliased, in_hbm,
        [pltpu.SemaphoreType.DMA((len(places),))],
        index, *values, *([gathered] if aliased else []),
        aliases={len(values) + 1: 0} if aliased else {},
    )


def outer_step(chain, local_weights, anchor, momentum, inner):
    n = lax.axis_size("replica")
    chips = n // 2
    last = chips - 1
    rows, cols = anchor.shape[2], anchor.shape[3]
    perm, swap = ring_perms(n)
    me = lax.axis_index("replica")
    core = me % 2
    pos = ring_pos(me // 2, chips)
    ahead = [ring_chip((pos + d) % chips, chips) for d in range(chips)]
    behind = [ring_chip((pos - d + chips) % chips, chips) for d in range(chips)]
    mine = [jnp.where(core == 0, a, b) for a, b in zip(ahead, behind)]
    siblings = [jnp.where(core == 0, b, a) for a, b in zip(ahead, behind)]

    def send(x, perm):
        return lax.ppermute(x, "replica", perm)

    shards = local_weights[0].reshape(2, chips, 2, rows, cols)

    def mine_at(j):
        return mine[last - j], core

    def siblings_at(j):
        return siblings[last - j], 1 - core

    def rows_at(array, m, chip, c):
        return lax.dynamic_slice(array, (m, chip, c, 0, 0), (1, 1, 1, rows, cols)).reshape(rows, cols)

    units = {(j, m): rows_at(shards, m, *siblings_at(j)) for j in range(2) for m in range(2)}
    inner.send_columns(units[1, 1])
    early = {key: send(value, swap) for key, value in units.items()}
    rest, *first = after((shards, *early.values()))
    early = dict(zip(early, first))
    whole = send(rest, swap)

    def pair(whole, j, m):
        theirs = early[j, m] if (j, m) in early else rows_at(whole, m, *mine_at(j))
        return rows_at(shards, m, *mine_at(j)).astype(f32) + theirs.astype(f32)

    came = [None, None]
    for j in range(last):
        if j == last - 1:
            came[0] = inner.wait_first(came[0])
        for m in range(2):
            total = pair(whole, j, m)
            if j:
                total = total + came[m].astype(f32)
            out = total.astype(bf16)
            if (j, m) < (1, 1):
                following = (j, 1) if m == 0 else (j + 1, 0)
                early[following], out = after((early[following], out))
            elif (j, m) == (1, 1):
                whole = follow(chain, whole, out)
            else:
                whole, out = after((whole, out))
            if m == 1 and j in (2, 3, 4):
                whole = inner.early(j, out, whole)
            came[m] = send(out, perm)

    have = []
    momentum_out = []
    for m in range(2):
        average = (pair(whole, last, m) + came[m].astype(f32)) / n
        weights = anchor[m, 0].astype(f32)
        pseudo_grad = weights - average
        momentum_new = momentum_decay * momentum[m, 0] + pseudo_grad
        piece = (weights - outer_rate * (pseudo_grad + momentum_decay * momentum_new)).astype(bf16)
        whole, piece, momentum_new = after((whole, piece, momentum_new))
        have.append(piece)
        momentum_out.append(momentum_new)

    index = jnp.stack([2 * siblings[k] + core for k in range(chips)] + [2 * mine[k] + 1 - core for k in range(chips)])
    shape = (2, n, rows, cols)
    gathered = None
    entries = []
    for k in range(chips):
        held = []
        for m in range(2):
            value = have[m]
            if gathered is not None:
                value, gathered = after((value, gathered))
            if k < last:
                have[m] = send(value, perm)
            entries.append((value, (m, k)))
            held.append((send(value, swap), (m, chips + k)))
        gathered = place(chain, gathered, shape, index, entries)
        entries = held
        if k == 1:
            gathered, momentum_out = after((gathered, jnp.stack(momentum_out)[:, None]))
        inner.late(k)
        if k == last - 1:
            have[0], inner.keys = after((have[0], inner.keys))
    gathered = place(chain, gathered, shape, index, entries)
    return gathered.reshape(2, n * rows, cols), momentum_out


def chosen(where_ref, a, b):
    return jnp.where(where_ref[1] == 0, a[...], b[...])


def product(a, b):
    return lax.dot_general(a, b, (((0,), (0,)), ((), ())), preferred_element_type=f32)


def keys_kernel(where_ref, *refs):
    *values, weight_ref, out, acc = refs
    step = pl.program_id(0)
    value = values[0][...] if len(values) == 1 else chosen(where_ref, *values)
    term = jnp.dot(value, weight_ref[...], preferred_element_type=f32)

    @pl.when(step == 0)
    def _():
        acc[...] = term

    @pl.when(step > 0)
    def _():
        acc[...] += term

    @pl.when(step == pl.num_programs(0) - 1)
    def _():
        out[...] = acc[...].astype(out.dtype)


def own_term_kernel(where_ref, tokens_ref, cotangent_ref, *refs):
    refs[-1][...] = product(tokens_ref[...], cotangent_ref[...]).astype(bf16)


def grad_kernel(where_ref, term_ref, *refs):
    total = term_ref[...].astype(f32)
    for i in range(0, len(refs) // 4 * 4, 4):
        term = product(chosen(where_ref, *refs[i:i + 2]), chosen(where_ref, *refs[i + 2:i + 4]))
        total = total + term.astype(bf16).astype(f32)
    refs[-1][...] = total.astype(bf16)


class Inner:
    def __init__(self, chain, tokens, inner_weight, cotangent):
        self.chain = chain
        self.terms = []
        self.tokens, self.weight, self.cotangent = tokens, inner_weight[0], cotangent
        self.parts = lax.axis_size("fsdp")
        self.mine = lax.axis_index("fsdp")
        self.count = tokens.shape[0]
        self.depth, self.width = self.weight.shape
        self.tile = min(1024, self.depth // 2)
        self.steps = self.depth // self.tile
        core = lax.axis_index("replica") % 2
        self.where = jnp.stack([self.mine * self.steps, core])

    def shift(self, x, s, c=None):
        if c is None:
            return lax.ppermute(x, "fsdp", [(k, (k + s) % self.parts) for k in range(self.parts)])
        workers = lax.axis_size("replica")
        pairs = [
            (r * self.parts + k, r * self.parts + (k + s) % self.parts)
            for r in range(c, workers, 2) for k in range(self.parts)
        ]
        return lax.ppermute(x, ("replica", "fsdp"), pairs)

    def specs(self, first=0):
        block = (self.count, self.tile)
        ahead = dict(pipeline_mode=pl.Buffered(2))
        own = pl.BlockSpec(block, lambda i, where: (0, where[0] + first + i), **ahead)
        others = [
            pl.BlockSpec(block, lambda i, where, c=c: (0, jnp.where(where[1] == c, first + i, 0)), **ahead) for c in range(2)
        ]
        return own, others, pl.BlockSpec((self.tile, self.width), lambda i, where: (first + i, 0), **ahead)

    def call(self, kernel, name, out_shape, in_specs, out_specs, scratch, steps, *operands, aliases={}):
        return self.chain.call(
            kernel, name, out_shape, in_specs, out_specs, scratch, *operands, aliases=aliases, grant=20,
            where=self.where, steps=steps,
        )

    def columns(self, owner):
        depth, width, count = self.depth, self.width, self.count

        def kernel(start_ref, tokens_ref, cotangent_ref, out, sems):
            start = pl.multiple_of(start_ref[0] * depth, depth)
            finish(run_copies([
                pltpu.make_async_copy(tokens_ref.at[:, pl.ds(start, depth)], out.at[:, pl.ds(0, depth)], sems.at[0]),
                pltpu.make_async_copy(cotangent_ref, out.at[:, pl.ds(depth, width)], sems.at[1]),
            ]))

        return self.chain.call(
            kernel, "columns", jax.ShapeDtypeStruct((count, depth + width), bf16), [in_smem, in_hbm, in_hbm], in_vmem,
            [pltpu.SemaphoreType.DMA((2,))], jnp.reshape(owner, (1,)), in_place(self.tokens), in_place(self.cotangent),
        )

    def send_columns(self, gate):
        self.chain.gates = [gate]
        values = [self.columns((self.mine + s) % self.parts) for s in range(1, self.parts)]
        self.first, self.second = ([self.shift(value, s, c) for s, value in enumerate(values, 1)] for c in range(2))

    def result(self, kind):
        return jax.ShapeDtypeStruct((self.count, self.width), kind)

    def multiply_keys(self, values, kind):
        own, others, weights = self.specs()
        return self.call(
            keys_kernel, "keys", self.result(kind), ([own] if len(values) == 1 else others) + [weights],
            pl.BlockSpec((self.count, self.width), lambda i, where: (0, 0)),
            [pltpu.VMEM((self.count, self.width), f32)], self.steps, *values, in_place(self.weight),
        )

    def own_term(self, second):
        half = self.steps // 2
        own, _, _ = self.specs(half * second)
        return self.call(
            own_term_kernel, "own_term", jax.ShapeDtypeStruct((self.depth // 2, self.width), bf16),
            [own, pl.BlockSpec((self.count, self.width), lambda i, where: (0, 0))],
            pl.BlockSpec((self.tile, self.width), lambda i, where: (i, 0)), [], half, in_place(self.tokens), self.cotangent,
        )

    def add_terms(self, second):
        half = self.steps // 2
        _, others, _ = self.specs(half * second)
        last = self.depth // self.width
        cotangents = pl.BlockSpec((self.count, self.width), lambda i, where: (0, last))
        operands, in_specs = [self.terms[second]], [pl.BlockSpec((self.tile, self.width), lambda i, where: (i, 0))]
        for a, b in zip(self.first, self.second):
            operands += [a, b, a, b]
            in_specs += others + [cotangents] * 2
        self.grad = self.call(
            grad_kernel, "grad", jax.ShapeDtypeStruct((self.depth, self.width), bf16), in_specs + [in_hbm] * second,
            pl.BlockSpec((self.tile, self.width), lambda i, where: (half * second + i, 0)), [], half,
            *operands, *([self.grad] if second else []), aliases={len(operands): 0} if second else {},
        )

    def wait_first(self, gate):
        gate, *self.first = after((gate, *self.first))
        return gate

    def early(self, j, gate, whole):
        self.chain.gates = [gate]
        if j == 2:
            self.keys = self.multiply_keys([in_place(self.tokens)], f32)
            whole, self.keys = after((whole, self.keys))
        else:
            term = self.own_term(j - 2 - 1)
            whole, term = after((whole, term))
            self.terms.append(term)
        return whole

    def finish_keys(self):
        def kernel(where_ref, keys_ref, *refs):
            total = keys_ref[...]
            for ref in refs[:-1]:
                total = total + ref[...].astype(f32)
            refs[-1][...] = total.astype(bf16)

        rows = pl.BlockSpec((self.count // 2, self.width), lambda i, where: (i, 0))
        self.keys = self.call(
            kernel, "finish_keys", self.result(bf16), [rows] * (1 + len(self.came)), rows, [], 2, self.keys, *self.came
        )

    def late(self, k):
        if k == 2:
            others = [self.multiply_keys(pair, bf16) for pair in zip(self.first, self.second)]
            self.came = [self.shift(value, self.parts - s) for s, value in enumerate(others, 1)]
        if k in (3, 4):
            self.add_terms(k - 3)
        if k == 6:
            self.finish_keys()


def shards(tokens, inner_weight, cotangent, local_weights, anchor, momentum):
    chain = Chain()
    inner = Inner(chain, tokens, inner_weight, cotangent)
    new_weights, new_momentum = outer_step(chain, local_weights, anchor, momentum, inner)
    return (inner.keys, inner.grad[None], new_weights, new_momentum)


def solution(mesh):
    return jax.shard_map(
        shards,
        mesh=mesh,
        in_specs=(
            P(("replica", "fsdp"), None),
            P("replica", "fsdp", None),
            P(("replica", "fsdp"), None),
            P("replica", None, "fsdp", None),
            P(None, "fsdp", "replica", None),
            P(None, "fsdp", "replica", None),
        ),
        out_specs=(
            P(("replica", "fsdp"), None),
            P("replica", "fsdp", None),
            P(None, "fsdp", None),
            P(None, "fsdp", "replica", None),
        ),
        check_vma=False,
    )
```

time: 188 us -> 179 us (0.952)
  other arithmetic: 1.1 us -> 37.5 us
  Pallas kernels: 82.7 us -> 48.6 us
  waiting for transfers between devices: 35.9 us -> 49.5 us
  starting transfers between devices: 50.5 us -> 37.2 us
  local copies, waits for them, and re-layouts: 15.6 us -> 3.67 us
    pallas_call x37 -> x18, Pallas kernels: 82.7 us -> 48.6 us  [call(): pl.pallas_call(body, **params)]
    convert_element_type x1 -> x16, other arithmetic: 0.95 us -> 34.6 us  [the longest x14 28 us: outer_step(): out = total.astype(bf16)]
    unnamed x68 -> x18, local copies, waits for them, and re-layouts: 15.3 us -> 1.98 us
    ppermute x53 -> x49, starting transfers between devices: 40 us -> 30.9 us  [send(): return lax.ppermute(x, 'replica', perm)]
    ppermute x0 -> x1, waiting for transfers between devices: none -> 8.24 us  [shift(): lax.ppermute(x, 'fsdp', [(k, (k + s) % self.parts) for k in range(self.pa...]
    ppermute x53 -> x49, waiting for transfers between devices: 34.8 us -> 41.2 us  [send(): return lax.ppermute(x, 'replica', perm)]
    ppermute x4 -> x2, starting transfers between devices: 10.4 us -> 5.84 us  [shift(): return lax.ppermute(x, ('replica', 'fsdp'), pairs)]
    broadcast_in_dim x0 -> x1, other arithmetic: none -> 2.8 us  [outer_step(): gathered, momentum_out = after((gathered, jnp.stack(momentum_out)[:, None]))]
  transfers between devices with their start and end apart: 57 -> 52, of which waited for: 16 -> 22; matrix products, arithmetic and copies ran while one was open for 1% -> 21% of each run, Pallas kernels for 42% -> 27%
where the time goes in v3:
time: 179 us; the launch traced here: 178 us
  waiting for transfers between devices  49.5 us (28%)
  Pallas kernels  48.6 us (27%)
  other arithmetic  37.5 us (21%)
  starting transfers between devices  37.2 us (21%)
  local copies, waits for them, and re-layouts  3.67 us (2%)
    pallas_call x18, Pallas kernels, call(): pl.pallas_call(body, **params)  48.6 us
    ppermute x49, waiting for transfers between devices, send(): return lax.ppermute(x, 'replica', perm)  41.2 us
    ppermute x49, starting transfers between devices, send(): return lax.ppermute(x, 'replica', perm)  30.9 us
    convert_element_type x14, other arithmetic, outer_step(): out = total.astype(bf16)  28 us
    ppermute x1, waiting for transfers between devices, shift(): lax.ppermute(x, 'fsdp', [(k, (k + s) % self.parts) for k in range(self.pa...  8.24 us
    convert_element_type x2, other arithmetic, outer_step(): (weights - outer_rate * (pseudo_grad + momentum_decay * momentum_new)).as...  6.59 us
    ppermute x2, starting transfers between devices, shift(): return lax.ppermute(x, ('replica', 'fsdp'), pairs)  5.84 us
  transfers between devices with their start and end apart: 52, of which 22 were waited for; matrix products, arithmetic and copies ran while one was open for 21% of the time, Pallas kernels for 27%

profile of v3, /device:TPU:0, one launch (start us, length us, event | category | flops | bytes accessed | tf_op | source)
XLA Modules:
  0.0 177.6 jit_solution(13786526521737424004)
XLA Ops:
  8.6 2.7 %collective-permute-start.5 = (bf16[256,896]{1,0:T(8,128)(2,1)}, bf16[256,896]{1,0:T(8,128)(2,1)}, u32[]{:S(2)}, u32[]{:S(2)}) collective-permute-start(bf16[256,896]{1,0:T(8,128)(2,1)} %fusion.2), channel_id=1, source_target_pairs={{0,8},{2,6},{8,16},{10,2},{16,24},{18,10},{24,28},{26,18},{28,20},... | collective-permute-start | bytes 1376264 | tf_op jit(solution)/shard_map/ppermute | solution.py:135
  14.8 3.8 %columns.1 = (f32[8,128]{1,0:T(8,128)S(1)}, bf16[384,4608]{1,0:T(8,128)(2,1)}) custom-call(s32[1]{0:T(128)} %bitcast.9.refs_0_, bf16[384,8192]{1,0:T(8,128)(2,1)} %refs_1_.7, bf16[384,512]{1,0:T(8,128)(2,1)} %refs_2_.5, bf16[256,896]{1,0:T(8,128)(2,1)S(1)} %get-tuple-element.234.refs_3_), custom_call_target="tpu_custom_call" | custom-call | tf_op jit(solution)/shard_map/columns/pallas_call | solution.py:73
  18.6 3.4 %collective-permute-start.16 = (bf16[384,4608]{1,0:T(8,128)(2,1)}, bf16[384,4608]{1,0:T(8,128)(2,1)S(1)}, u32[]{:S(2)}, u32[]{:S(2)}) collective-permute-start(bf16[384,4608]{1,0:T(8,128)(2,1)} %get-tuple-element.152), channel_id=1, source_target_pairs={{0,1},{1,0},{4,5},{5,4},{8,9},{9,8},{12,13},{13,12},{16,17},{17,16... | collective-permute-start | bytes 10616840 | tf_op jit(solution)/shard_map/ppermute | solution.py:277
  22.0 2.2 %fusion.5 = bf16[256,896]{1,0:T(8,128)(2,1)} fusion(bf16[256,896]{1,0:T(8,128)(2,1)} %collective-permute-done.5, bf16[256,896]{1,0:T(8,128)(2,1)} %copy-done.8, bf16[2,8,2,256,896]{4,3,2,1,0:T(8,128)(2,1)} %bitcast.133, s32[]{:T(128)S(6)} %select_n.247, s32[]{:T(128)S(6)} %select_n.248), kind=kLoop, calls=%fused_computation.13 | loop fusion | flops 1376256 | bytes 1835016 | tf_op jit(solution)/shard_map/convert_element_type | solution.py:167
  25.8 2.2 %fusion.7.refs_1_ = bf16[256,896]{1,0:T(8,128)(2,1)} fusion(bf16[256,896]{1,0:T(8,128)(2,1)} %collective-permute-done.6, bf16[256,896]{1,0:T(8,128)(2,1)} %copy-done.7, bf16[2,8,2,256,896]{4,3,2,1,0:T(8,128)(2,1)} %bitcast.134, s32[]{:T(128)S(6)} %select_n.247, s32[]{:T(128)S(6)} %select_n.248), kind=kLoop, calls=%fused_computation.16 | loop fusion | flops 1376256 | bytes 1835016 | tf_op jit(solution)/shard_map/convert_element_type | solution.py:167
  29.6 3.5 %collective-permute-done.7 = bf16[256,896]{1,0:T(8,128)(2,1)} collective-permute-done((bf16[256,896]{1,0:T(8,128)(2,1)}, bf16[256,896]{1,0:T(8,128)(2,1)}, u32[]{:S(2)}, u32[]{:S(2)}) %collective-permute-start.7) | collective-permute-done | bytes 458784 | tf_op jit(solution)/shard_map/ppermute | solution.py:135
  33.0 2.3 %fusion.19 = bf16[256,896]{1,0:T(8,128)(2,1)} fusion(bf16[256,896]{1,0:T(8,128)(2,1)} %collective-permute-done.7, bf16[2,8,2,256,896]{4,3,2,1,0:T(8,128)(2,1)} %get-tuple-element.159, s32[]{:T(128)S(6)} %select_n.257, s32[]{:T(128)S(6)} %select_n.248, bf16[2,8,2,256,896]{4,3,2,1,0:T(8,128)(2,1)} %bitcast.135), kind=kLoop, calls=%fused_computation.42 | loop fusion | flops 1376256 | bytes 1835016 | tf_op jit(solution)/shard_map/convert_element_type | solution.py:167
  38.0 2.2 %fusion.18.refs_3_ = bf16[256,896]{1,0:T(8,128)(2,1)} fusion(bf16[256,896]{1,0:T(8,128)(2,1)} %collective-permute-done.8, bf16[2,8,2,256,896]{4,3,2,1,0:T(8,128)(2,1)} %get-tuple-element.159, s32[]{:T(128)S(6)} %select_n.257, s32[]{:T(128)S(6)} %select_n.248, bf16[2,8,2,256,896]{4,3,2,1,0:T(8,128)(2,1)} %bitcast.136), kind=kLoop, calls=%fused_computation.40 | loop fusion | flops 1376256 | bytes 1835016 | tf_op jit(solution)/shard_map/convert_element_type | solution.py:167
  41.8 5.6 %keys.2 = (f32[8,128]{1,0:T(8,128)S(1)}, f32[384,512]{1,0:T(8,128)S(1)}) custom-call(s32[2]{0:T(128)S(1)} %pad_add_fusion.refs_0_, bf16[384,8192]{1,0:T(8,128)(2,1)} %refs_1_.7, bf16[4096,512]{1,0:T(8,128)(2,1)} %bitcast.127, bf16[256,896]{1,0:T(8,128)(2,1)} %fusion.18.refs_3_, f32[8,128]{1,0:T(8,128)S(1)} %get-tuple-element.131.refs_4_), custom_call_target="tpu_custom_call" | custom-call | tf_op jit(solution)/shard_map/keys/pallas_call | solution.py:73
  48.4 2.2 %fusion.17 = bf16[256,896]{1,0:T(8,128)(2,1)} fusion(bf16[256,896]{1,0:T(8,128)(2,1)} %collective-permute-done.9, bf16[2,8,2,256,896]{4,3,2,1,0:T(8,128)(2,1)} %get-tuple-element.159, s32[]{:T(128)S(6)} %select_n.260, s32[]{:T(128)S(6)} %select_n.248, bf16[2,8,2,256,896]{4,3,2,1,0:T(8,128)(2,1)} %bitcast.137), kind=kLoop, calls=%fused_computation.38 | loop fusion | flops 1376256 | bytes 1835016 | tf_op jit(solution)/shard_map/convert_element_type | solution.py:167
  52.2 2.2 %fusion.16.refs_3_ = bf16[256,896]{1,0:T(8,128)(2,1)} fusion(bf16[256,896]{1,0:T(8,128)(2,1)} %collective-permute-done.10, bf16[2,8,2,256,896]{4,3,2,1,0:T(8,128)(2,1)} %get-tuple-element.159, s32[]{:T(128)S(6)} %select_n.260, s32[]{:T(128)S(6)} %select_n.248, bf16[2,8,2,256,896]{4,3,2,1,0:T(8,128)(2,1)} %bitcast.138), kind=kLoop, calls=%fused_computation.36 | loop fusion | flops 1376256 | bytes 1835016 | tf_op jit(solution)/shard_map/convert_element_type | solution.py:167
  55.9 3.2 %own_term.2 = (f32[8,128]{1,0:T(8,128)S(1)}, bf16[2048,512]{1,0:T(8,128)(2,1)S(1)}) custom-call(s32[2]{0:T(128)S(1)} %pad_add_fusion.refs_0_, bf16[384,8192]{1,0:T(8,128)(2,1)} %refs_1_.7, bf16[384,512]{1,0:T(8,128)(2,1)S(1)} %copy-done, bf16[256,896]{1,0:T(8,128)(2,1)} %fusion.16.refs_3_, f32[8,128]{1,0:T(8,128)S(1)} %get-tuple-element.138.refs_4_), custom_call_target="tpu_custom_call" | custom-call | tf_op jit(solution)/shard_map/own_term/pallas_call | solution.py:73
  67.4 3.2 %own_term.3 = (f32[8,128]{1,0:T(8,128)S(1)}, bf16[2048,512]{1,0:T(8,128)(2,1)S(1)}) custom-call(s32[2]{0:T(128)S(1)} %pad_add_fusion.refs_0_, bf16[384,8192]{1,0:T(8,128)(2,1)} %refs_1_.7, bf16[384,512]{1,0:T(8,128)(2,1)S(1)} %copy-done, bf16[256,896]{1,0:T(8,128)(2,1)S(1)} %fusion.14.refs_3_, f32[8,128]{1,0:T(8,128)S(1)} %get-tuple-element.145.refs_4_), custom_call_target="tpu_custom_call" | custom-call | tf_op jit(solution)/shard_map/own_term/pallas_call | solution.py:73
  73.2 2.4 %collective-permute-start.33 = (bf16[384,4608]{1,0:T(8,128)(2,1)}, bf16[384,4608]{1,0:T(8,128)(2,1)}, u32[]{:S(2)}, u32[]{:S(2)}) collective-permute-start(bf16[384,4608]{1,0:T(8,128)(2,1)} %get-tuple-element.152), channel_id=1, source_target_pairs={{2,3},{3,2},{6,7},{7,6},{10,11},{11,10},{14,15},{15,14},{18,19},{1... | collective-permute-start | bytes 10616840 | tf_op jit(solution)/shard_map/ppermute | solution.py:277
  77.5 3.8 %collective-permute-done.15 = bf16[256,896]{1,0:T(8,128)(2,1)S(1)} collective-permute-done((bf16[256,896]{1,0:T(8,128)(2,1)S(1)}, bf16[256,896]{1,0:T(8,128)(2,1)S(1)}, u32[]{:S(2)}, u32[]{:S(2)}) %collective-permute-start.15) | collective-permute-done | bytes 458784 | tf_op jit(solution)/shard_map/ppermute | solution.py:135
  81.2 2.1 %fusion.11 = bf16[256,896]{1,0:T(8,128)(2,1)} fusion(bf16[256,896]{1,0:T(8,128)(2,1)S(1)} %collective-permute-done.15, bf16[2,8,2,256,896]{4,3,2,1,0:T(8,128)(2,1)} %get-tuple-element.159, s32[]{:T(128)S(6)} %select_n.238, s32[]{:T(128)S(6)} %select_n.248, bf16[2,8,2,256,896]{4,3,2,1,0:T(8,128)(2,1)} %bitcast.143), kind=kLoop, calls=%fused_computation.26 | loop fusion | flops 1376256 | bytes 1835016 | tf_op jit(solution)/shard_map/convert_element_type | solution.py:167
  83.8 2.4 %collective-permute-done.17 = bf16[256,896]{1,0:T(8,128)(2,1)S(1)} collective-permute-done((bf16[256,896]{1,0:T(8,128)(2,1)S(1)}, bf16[256,896]{1,0:T(8,128)(2,1)S(1)}, u32[]{:S(2)}, u32[]{:S(2)}) %collective-permute-start.17) | collective-permute-done | bytes 458784 | tf_op jit(solution)/shard_map/ppermute | solution.py:135
  88.7 3.4 %collective-permute-done.18 = bf16[256,896]{1,0:T(8,128)(2,1)} collective-permute-done((bf16[256,896]{1,0:T(8,128)(2,1)}, bf16[256,896]{1,0:T(8,128)(2,1)}, u32[]{:S(2)}, u32[]{:S(2)}) %collective-permute-start.18) | collective-permute-done | bytes 458784 | tf_op jit(solution)/shard_map/ppermute | solution.py:135
  92.1 3.3 %fusion = (bf16[256,896]{1,0:T(8,128)(2,1)}, f32[256,896]{1,0:T(8,128)}) fusion(bf16[256,896]{1,0:T(8,128)(2,1)} %collective-permute-done.18, bf16[2,1,256,896]{3,2,1,0:T(8,128)(2,1)} %param.10, bf16[2,8,2,256,896]{4,3,2,1,0:T(8,128)(2,1)} %get-tuple-element.159, s32[]{:T(128)S(6)} %select_n.268, s32[]{:T(128)S(6)} %select_n.248, ...), kind=kLoop, calls=%fused_computation.5 | loop fusion | flops 3440640 | bytes 4128776 | tf_op jit(solution)/shard_map/convert_element_type | solution.py:186
  97.0 3.3 %fusion.1 = (bf16[256,896]{1,0:T(8,128)(2,1)}, f32[256,896]{1,0:T(8,128)}) fusion(bf16[256,896]{1,0:T(8,128)(2,1)} %collective-permute-done.20, bf16[2,1,256,896]{3,2,1,0:T(8,128)(2,1)} %param.10, bf16[2,8,2,256,896]{4,3,2,1,0:T(8,128)(2,1)} %get-tuple-element.159, s32[]{:T(128)S(6)} %select_n.268, s32[]{:T(128)S(6)} %select_n.248, ...), kind=kLoop, calls=%fused_computation.6 | loop fusion | flops 3440640 | bytes 4128776 | tf_op jit(solution)/shard_map/convert_element_type | solution.py:186
  101.5 2.1 %place.9 = (f32[8,128]{1,0:T(8,128)S(1)}, bf16[2,16,256,896]{3,2,1,0:T(8,128)(2,1)}) custom-call(s32[16]{0:T(128)S(1)} %stack.88.refs_0_, bf16[256,896]{1,0:T(8,128)(2,1)} %get-tuple-element.158.refs_1_, bf16[256,896]{1,0:T(8,128)(2,1)} %get-tuple-element.161.refs_2_, f32[8,128]{1,0:T(8,128)S(1)} %get-tuple-element.162.refs_3_), custom_call_target="tpu_custom_call" | custom-call | tf_op jit(solution)/shard_map/place/pallas_call | solution.py:73
  104.6 4.5 %collective-permute-done.24.refs_4_ = bf16[256,896]{1,0:T(8,128)(2,1)} collective-permute-done((bf16[256,896]{1,0:T(8,128)(2,1)}, bf16[256,896]{1,0:T(8,128)(2,1)}, u32[]{:S(2)}, u32[]{:S(2)}) %collective-permute-start.24) | collective-permute-done | bytes 458784 | tf_op jit(solution)/shard_map/ppermute | solution.py:135
  109.6 2.8 %maximum_bitcast_fusion = f32[2,1,256,896]{3,2,0,1:T(8,128)} fusion(f32[1,256,896]{2,1,0:T(8,128)} %bitcast.149, f32[1,256,896]{2,1,0:T(8,128)} %bitcast.148), kind=kLoop, calls=%fused_computation | loop fusion | flops 458752 | bytes 3670016 | tf_op jit(solution)/shard_map/broadcast_in_dim | solution.py:208
  112.9 2.6 %place.10 = (f32[8,128]{1,0:T(8,128)S(1)}, bf16[2,16,256,896]{3,2,1,0:T(8,128)(2,1)}) custom-call(s32[16]{0:T(128)S(1)} %stack.88.refs_0_, bf16[256,896]{1,0:T(8,128)(2,1)S(1)} %collective-permute-done.22.refs_1_, bf16[256,896]{1,0:T(8,128)(2,1)} %collective-permute-done.23.refs_2_, ...), custom_call_target="tpu_custom_call", output_to_operand_aliasing={{1}: (5, {})} | custom-call | tf_op jit(solution)/shard_map/place/pallas_call | solution.py:73
  116.0 2.9 %collective-permute-done.28.refs_4_ = bf16[256,896]{1,0:T(8,128)(2,1)S(1)} collective-permute-done((bf16[256,896]{1,0:T(8,128)(2,1)}, bf16[256,896]{1,0:T(8,128)(2,1)S(1)}, u32[]{:S(2)}, u32[]{:S(2)}) %collective-permute-start.28) | collective-permute-done | bytes 458784 | tf_op jit(solution)/shard_map/ppermute | solution.py:135
  121.7 2.4 %collective-permute-done.25.refs_3_ = bf16[256,896]{1,0:T(8,128)(2,1)S(1)} collective-permute-done((bf16[256,896]{1,0:T(8,128)(2,1)S(1)}, bf16[256,896]{1,0:T(8,128)(2,1)S(1)}, u32[]{:S(2)}, u32[]{:S(2)}) %collective-permute-start.25) | collective-permute-done | bytes 458784 | tf_op jit(solution)/shard_map/ppermute | solution.py:135
  124.5 4.5 %collective-permute-done.32.refs_4_ = bf16[256,896]{1,0:T(8,128)(2,1)S(1)} collective-permute-done((bf16[256,896]{1,0:T(8,128)(2,1)S(1)}, bf16[256,896]{1,0:T(8,128)(2,1)S(1)}, u32[]{:S(2)}, u32[]{:S(2)}) %collective-permute-start.32) | collective-permute-done | bytes 458784 | tf_op jit(solution)/shard_map/ppermute | solution.py:135
  129.4 5.6 %keys.3 = (f32[8,128]{1,0:T(8,128)S(1)}, bf16[384,512]{1,0:T(8,128)(2,1)S(1)}) custom-call(s32[2]{0:T(128)S(1)} %pad_add_fusion.refs_0_, bf16[384,4608]{1,0:T(8,128)(2,1)S(1)} %collective-permute-done.16.refs_1_.refs_2_.refs_4_, bf16[384,4608]{1,0:T(8,128)(2,1)} %collective-permute-done.33.refs_2_.refs_3_.refs_5_, bf16[4096,512]{1,0:T(8,128)(2,1)} %bitcast.128, ...), custom_call_target="tpu_custom_call" | custom-call | tf_op jit(solution)/shard_map/keys/pallas_call | solution.py:73
  139.2 4.5 %grad.2 = (f32[8,128]{1,0:T(8,128)S(1)}, bf16[4096,512]{1,0:T(8,128)(2,1)}) custom-call(s32[2]{0:T(128)S(1)} %pad_add_fusion.refs_0_, bf16[2048,512]{1,0:T(8,128)(2,1)S(1)} %copy-done.4, bf16[384,4608]{1,0:T(8,128)(2,1)S(1)} %collective-permute-done.16.refs_1_.refs_2_.refs_4_, bf16[384,4608]{1,0:T(8,128)(2,1)} %collective-permute-done.33.refs_2_.refs_3_.refs_5_, ...), custom_call_target="tpu_custom_call" | custom-call | tf_op jit(solution)/shard_map/grad/pallas_call | solution.py:73
  147.4 3.5 %collective-permute-done.41.refs_4_ = bf16[256,896]{1,0:T(8,128)(2,1)S(1)} collective-permute-done((bf16[256,896]{1,0:T(8,128)(2,1)S(1)}, bf16[256,896]{1,0:T(8,128)(2,1)S(1)}, u32[]{:S(2)}, u32[]{:S(2)}) %collective-permute-start.41) | collective-permute-done | bytes 458784 | tf_op jit(solution)/shard_map/ppermute | solution.py:135
  151.3 4.5 %grad.3 = (f32[8,128]{1,0:T(8,128)S(1)}, bf16[4096,512]{1,0:T(8,128)(2,1)}) custom-call(s32[2]{0:T(128)S(1)} %pad_add_fusion.refs_0_, bf16[2048,512]{1,0:T(8,128)(2,1)S(1)} %copy-done.2, bf16[384,4608]{1,0:T(8,128)(2,1)S(1)} %collective-permute-done.16.refs_1_.refs_2_.refs_4_, ...), custom_call_target="tpu_custom_call", output_to_operand_aliasing={{1}: (6, {})} | custom-call | tf_op jit(solution)/shard_map/grad/pallas_call | solution.py:73
  164.0 8.2 %collective-permute-done.43.refs_2_ = bf16[384,512]{1,0:T(8,128)(2,1)S(1)} collective-permute-done((bf16[384,512]{1,0:T(8,128)(2,1)S(1)}, bf16[384,512]{1,0:T(8,128)(2,1)S(1)}, u32[]{:S(2)}, u32[]{:S(2)}) %collective-permute-start.43) | collective-permute-done | bytes 393248 | tf_op jit(solution)/shard_map/ppermute | solution.py:271
  (128 shorter events, 69.0 us)
Async XLA Ops:
  6.3 23.3 %collective-permute-start.4 = (bf16[2,8,2,256,896]{4,3,2,1,0:T(8,128)(2,1)}, bf16[2,8,2,256,896]{4,3,2,1,0:T(8,128)(2,1)}, u32[]{:S(2)}, u32[]{:S(2)}) collective-permute-start(bf16[2,8,2,256,896]{4,3,2,1,0:T(8,128)(2,1)} %bitcast.130), channel_id=1, source_target_pairs={{0,2},{2,0},{4,6},{6,4},{8,10},{10,8},{12,14},{14,12},{16,18},{18,... | collective-permute-start | bytes 44040200 | tf_op jit(solution)/shard_map/ppermute | solution.py:135
  8.6 13.4 %collective-permute-start.5 = (bf16[256,896]{1,0:T(8,128)(2,1)}, bf16[256,896]{1,0:T(8,128)(2,1)}, u32[]{:S(2)}, u32[]{:S(2)}) collective-permute-start(bf16[256,896]{1,0:T(8,128)(2,1)} %fusion.2), channel_id=1, source_target_pairs={{0,8},{2,6},{8,16},{10,2},{16,24},{18,10},{24,28},{26,18},{28,20},... | collective-permute-start | bytes 1376264 | tf_op jit(solution)/shard_map/ppermute | solution.py:135
  13.2 12.6 %collective-permute-start.6 = (bf16[256,896]{1,0:T(8,128)(2,1)}, bf16[256,896]{1,0:T(8,128)(2,1)}, u32[]{:S(2)}, u32[]{:S(2)}) collective-permute-start(bf16[256,896]{1,0:T(8,128)(2,1)} %fusion.3), channel_id=1, source_target_pairs={{0,8},{2,6},{8,16},{10,2},{16,24},{18,10},{24,28},{26,18},{28,20},... | collective-permute-start | bytes 1376264 | tf_op jit(solution)/shard_map/ppermute | solution.py:135
  18.6 58.9 %collective-permute-start.16 = (bf16[384,4608]{1,0:T(8,128)(2,1)}, bf16[384,4608]{1,0:T(8,128)(2,1)S(1)}, u32[]{:S(2)}, u32[]{:S(2)}) collective-permute-start(bf16[384,4608]{1,0:T(8,128)(2,1)} %get-tuple-element.152), channel_id=1, source_target_pairs={{0,1},{1,0},{4,5},{5,4},{8,9},{9,8},{12,13},{13,12},{16,17},{17,16... | collective-permute-start | bytes 10616840 | tf_op jit(solution)/shard_map/ppermute | solution.py:277
  28.1 9.9 %collective-permute-start.8 = (bf16[256,896]{1,0:T(8,128)(2,1)}, bf16[256,896]{1,0:T(8,128)(2,1)}, u32[]{:S(2)}, u32[]{:S(2)}) collective-permute-start(bf16[256,896]{1,0:T(8,128)(2,1)} %fusion.7.refs_1_), channel_id=1, source_target_pairs={{0,8},{2,6},{8,16},{10,2},{16,24},{18,10},{24,28},{26,18},{28,20},... | collective-permute-start | bytes 1376264 | tf_op jit(solution)/shard_map/ppermute | solution.py:135
  35.3 13.1 %collective-permute-start.9 = (bf16[256,896]{1,0:T(8,128)(2,1)}, bf16[256,896]{1,0:T(8,128)(2,1)}, u32[]{:S(2)}, u32[]{:S(2)}) collective-permute-start(bf16[256,896]{1,0:T(8,128)(2,1)} %fusion.19), channel_id=1, source_target_pairs={{0,8},{2,6},{8,16},{10,2},{16,24},{18,10},{24,28},{26,18},{28,20},... | collective-permute-start | bytes 1376264 | tf_op jit(solution)/shard_map/ppermute | solution.py:135
  40.2 12.0 %collective-permute-start.10 = (bf16[256,896]{1,0:T(8,128)(2,1)}, bf16[256,896]{1,0:T(8,128)(2,1)}, u32[]{:S(2)}, u32[]{:S(2)}) collective-permute-start(bf16[256,896]{1,0:T(8,128)(2,1)} %fusion.18.refs_3_), channel_id=1, source_target_pairs={{0,8},{2,6},{8,16},{10,2},{16,24},{18,10},{24,28},{26,18},{28,20},... | collective-permute-start | bytes 1376264 | tf_op jit(solution)/shard_map/ppermute | solution.py:135
  54.4 10.0 %collective-permute-start.12 = (bf16[256,896]{1,0:T(8,128)(2,1)}, bf16[256,896]{1,0:T(8,128)(2,1)}, u32[]{:S(2)}, u32[]{:S(2)}) collective-permute-start(bf16[256,896]{1,0:T(8,128)(2,1)} %fusion.16.refs_3_), channel_id=1, source_target_pairs={{0,8},{2,6},{8,16},{10,2},{16,24},{18,10},{24,28},{26,18},{28,20},... | collective-permute-start | bytes 1376264 | tf_op jit(solution)/shard_map/ppermute | solution.py:135
  61.3 9.4 %collective-permute-start.13 = (bf16[256,896]{1,0:T(8,128)(2,1)S(1)}, bf16[256,896]{1,0:T(8,128)(2,1)S(1)}, u32[]{:S(2)}, u32[]{:S(2)}) collective-permute-start(bf16[256,896]{1,0:T(8,128)(2,1)S(1)} %fusion.15), channel_id=1, source_target_pairs={{0,8},{2,6},{8,16},{10,2},{16,24},{18,10},{24,28},{26,18},{28,20},... | collective-permute-start | bytes 1376264 | tf_op jit(solution)/shard_map/ppermute | solution.py:135
  65.9 9.8 %collective-permute-start.14 = (bf16[256,896]{1,0:T(8,128)(2,1)S(1)}, bf16[256,896]{1,0:T(8,128)(2,1)S(1)}, u32[]{:S(2)}, u32[]{:S(2)}) collective-permute-start(bf16[256,896]{1,0:T(8,128)(2,1)S(1)} %fusion.14.refs_3_), channel_id=1, source_target_pairs={{0,8},{2,6},{8,16},{10,2},{16,24},{18,10},{24,28},{26,18},{28,20},... | collective-permute-start | bytes 1376264 | tf_op jit(solution)/shard_map/ppermute | solution.py:135
  73.2 56.2 %collective-permute-start.33 = (bf16[384,4608]{1,0:T(8,128)(2,1)}, bf16[384,4608]{1,0:T(8,128)(2,1)}, u32[]{:S(2)}, u32[]{:S(2)}) collective-permute-start(bf16[384,4608]{1,0:T(8,128)(2,1)} %get-tuple-element.152), channel_id=1, source_target_pairs={{2,3},{3,2},{6,7},{7,6},{10,11},{11,10},{14,15},{15,14},{18,19},{1... | collective-permute-start | bytes 10616840 | tf_op jit(solution)/shard_map/ppermute | solution.py:277
  100.8 11.6 %collective-permute-start.23 = (bf16[256,896]{1,0:T(8,128)(2,1)}, bf16[256,896]{1,0:T(8,128)(2,1)}, u32[]{:S(2)}, u32[]{:S(2)}) collective-permute-start(bf16[256,896]{1,0:T(8,128)(2,1)} %get-tuple-element.161.refs_2_), channel_id=1, source_target_pairs={{0,2},{2,0},{4,6},{6,4},{8,10},{10,8},{12,14},{14,12},{16,18},{18,... | collective-permute-start | bytes 1376264 | tf_op jit(solution)/shard_map/ppermute | solution.py:135
  100.9 11.5 %collective-permute-start.22 = (bf16[256,896]{1,0:T(8,128)(2,1)}, bf16[256,896]{1,0:T(8,128)(2,1)S(1)}, u32[]{:S(2)}, u32[]{:S(2)}) collective-permute-start(bf16[256,896]{1,0:T(8,128)(2,1)} %get-tuple-element.158.refs_1_), channel_id=1, source_target_pairs={{0,2},{2,0},{4,6},{6,4},{8,10},{10,8},{12,14},{14,12},{16,18},{18,... | collective-permute-start | bytes 1376264 | tf_op jit(solution)/shard_map/ppermute | solution.py:135
  104.2 11.3 %collective-permute-start.21 = (bf16[256,896]{1,0:T(8,128)(2,1)}, bf16[256,896]{1,0:T(8,128)(2,1)S(1)}, u32[]{:S(2)}, u32[]{:S(2)}) collective-permute-start(bf16[256,896]{1,0:T(8,128)(2,1)} %collective-permute-done.19.refs_3_), channel_id=1, source_target_pairs={{0,8},{2,6},{8,16},{10,2},{16,24},{18,10},{24,28},{26,18},{28,20},... | collective-permute-start | bytes 1376264 | tf_op jit(solution)/shard_map/ppermute | solution.py:135
  109.1 9.7 %collective-permute-start.28 = (bf16[256,896]{1,0:T(8,128)(2,1)}, bf16[256,896]{1,0:T(8,128)(2,1)S(1)}, u32[]{:S(2)}, u32[]{:S(2)}) collective-permute-start(bf16[256,896]{1,0:T(8,128)(2,1)} %collective-permute-done.24.refs_4_), channel_id=1, source_target_pairs={{0,8},{2,6},{8,16},{10,2},{16,24},{18,10},{24,28},{26,18},{28,20},... | collective-permute-start | bytes 1376264 | tf_op jit(solution)/shard_map/ppermute | solution.py:135
  118.9 10.1 %collective-permute-start.32 = (bf16[256,896]{1,0:T(8,128)(2,1)S(1)}, bf16[256,896]{1,0:T(8,128)(2,1)S(1)}, u32[]{:S(2)}, u32[]{:S(2)}) collective-permute-start(bf16[256,896]{1,0:T(8,128)(2,1)S(1)} %collective-permute-done.28.refs_4_), channel_id=1, source_target_pairs={{0,8},{2,6},{8,16},{10,2},{16,24},{18,10},{24,28},{26,18},{28,20},... | collective-permute-start | bytes 1376264 | tf_op jit(solution)/shard_map/ppermute | solution.py:135
  119.3 16.0 %collective-permute-start.31 = (bf16[256,896]{1,0:T(8,128)(2,1)S(1)}, bf16[256,896]{1,0:T(8,128)(2,1)S(1)}, u32[]{:S(2)}, u32[]{:S(2)}) collective-permute-start(bf16[256,896]{1,0:T(8,128)(2,1)S(1)} %collective-permute-done.28.refs_4_), channel_id=1, source_target_pairs={{0,2},{2,0},{4,6},{6,4},{8,10},{10,8},{12,14},{14,12},{16,18},{18,... | collective-permute-start | bytes 1376264 | tf_op jit(solution)/shard_map/ppermute | solution.py:135
  119.3 16.3 %collective-permute-start.30 = (bf16[256,896]{1,0:T(8,128)(2,1)S(1)}, bf16[256,896]{1,0:T(8,128)(2,1)S(1)}, u32[]{:S(2)}, u32[]{:S(2)}) collective-permute-start(bf16[256,896]{1,0:T(8,128)(2,1)S(1)} %collective-permute-done.21.refs_3_), channel_id=1, source_target_pairs={{0,2},{2,0},{4,6},{6,4},{8,10},{10,8},{12,14},{14,12},{16,18},{18,... | collective-permute-start | bytes 1376264 | tf_op jit(solution)/shard_map/ppermute | solution.py:135
  124.0 13.4 %collective-permute-start.29 = (bf16[256,896]{1,0:T(8,128)(2,1)S(1)}, bf16[256,896]{1,0:T(8,128)(2,1)S(1)}, u32[]{:S(2)}, u32[]{:S(2)}) collective-permute-start(bf16[256,896]{1,0:T(8,128)(2,1)S(1)} %collective-permute-done.25.refs_3_), channel_id=1, source_target_pairs={{0,8},{2,6},{8,16},{10,2},{16,24},{18,10},{24,28},{26,18},{28,20},... | collective-permute-start | bytes 1376264 | tf_op jit(solution)/shard_map/ppermute | solution.py:135
  128.9 9.8 %collective-permute-start.37 = (bf16[256,896]{1,0:T(8,128)(2,1)S(1)}, bf16[256,896]{1,0:T(8,128)(2,1)S(1)}, u32[]{:S(2)}, u32[]{:S(2)}) collective-permute-start(bf16[256,896]{1,0:T(8,128)(2,1)S(1)} %collective-permute-done.32.refs_4_), channel_id=1, source_target_pairs={{0,8},{2,6},{8,16},{10,2},{16,24},{18,10},{24,28},{26,18},{28,20},... | collective-permute-start | bytes 1376264 | tf_op jit(solution)/shard_map/ppermute | solution.py:135
  135.1 9.6 %collective-permute-start.36 = (bf16[256,896]{1,0:T(8,128)(2,1)S(1)}, bf16[256,896]{1,0:T(8,128)(2,1)S(1)}, u32[]{:S(2)}, u32[]{:S(2)}) collective-permute-start(bf16[256,896]{1,0:T(8,128)(2,1)S(1)} %collective-permute-done.32.refs_4_), channel_id=1, source_target_pairs={{0,2},{2,0},{4,6},{6,4},{8,10},{10,8},{12,14},{14,12},{16,18},{18,... | collective-permute-start | bytes 1376264 | tf_op jit(solution)/shard_map/ppermute | solution.py:135
  135.3 9.4 %collective-permute-start.35 = (bf16[256,896]{1,0:T(8,128)(2,1)S(1)}, bf16[256,896]{1,0:T(8,128)(2,1)S(1)}, u32[]{:S(2)}, u32[]{:S(2)}) collective-permute-start(bf16[256,896]{1,0:T(8,128)(2,1)S(1)} %collective-permute-done.25.refs_3_), channel_id=1, source_target_pairs={{0,2},{2,0},{4,6},{6,4},{8,10},{10,8},{12,14},{14,12},{16,18},{18,... | collective-permute-start | bytes 1376264 | tf_op jit(solution)/shard_map/ppermute | solution.py:135
  138.8 12.1 %collective-permute-start.41 = (bf16[256,896]{1,0:T(8,128)(2,1)S(1)}, bf16[256,896]{1,0:T(8,128)(2,1)S(1)}, u32[]{:S(2)}, u32[]{:S(2)}) collective-permute-start(bf16[256,896]{1,0:T(8,128)(2,1)S(1)} %collective-permute-done.37.refs_4_), channel_id=1, source_target_pairs={{0,8},{2,6},{8,16},{10,2},{16,24},{18,10},{24,28},{26,18},{28,20},... | collective-permute-start | bytes 1376264 | tf_op jit(solution)/shard_map/ppermute | solution.py:135
  143.7 12.2 %collective-permute-start.40 = (bf16[256,896]{1,0:T(8,128)(2,1)S(1)}, bf16[256,896]{1,0:T(8,128)(2,1)S(1)}, u32[]{:S(2)}, u32[]{:S(2)}) collective-permute-start(bf16[256,896]{1,0:T(8,128)(2,1)S(1)} %collective-permute-done.37.refs_4_), channel_id=1, source_target_pairs={{0,2},{2,0},{4,6},{6,4},{8,10},{10,8},{12,14},{14,12},{16,18},{18,... | collective-permute-start | bytes 1376264 | tf_op jit(solution)/shard_map/ppermute | solution.py:135
  144.7 11.7 %collective-permute-start.39 = (bf16[256,896]{1,0:T(8,128)(2,1)S(1)}, bf16[256,896]{1,0:T(8,128)(2,1)S(1)}, u32[]{:S(2)}, u32[]{:S(2)}) collective-permute-start(bf16[256,896]{1,0:T(8,128)(2,1)S(1)} %collective-permute-done.29.refs_3_), channel_id=1, source_target_pairs={{0,2},{2,0},{4,6},{6,4},{8,10},{10,8},{12,14},{14,12},{16,18},{18,... | collective-permute-start | bytes 1376264 | tf_op jit(solution)/shard_map/ppermute | solution.py:135
  146.6 11.6 %collective-permute-start.38 = (bf16[256,896]{1,0:T(8,128)(2,1)S(1)}, bf16[256,896]{1,0:T(8,128)(2,1)S(1)}, u32[]{:S(2)}, u32[]{:S(2)}) collective-permute-start(bf16[256,896]{1,0:T(8,128)(2,1)S(1)} %collective-permute-done.34.refs_3_), channel_id=1, source_target_pairs={{0,8},{2,6},{8,16},{10,2},{16,24},{18,10},{24,28},{26,18},{28,20},... | collective-permute-start | bytes 1376264 | tf_op jit(solution)/shard_map/ppermute | solution.py:135
  150.9 9.8 %collective-permute-start.46 = (bf16[256,896]{1,0:T(8,128)(2,1)S(1)}, bf16[256,896]{1,0:T(8,128)(2,1)S(1)}, u32[]{:S(2)}, u32[]{:S(2)}) collective-permute-start(bf16[256,896]{1,0:T(8,128)(2,1)S(1)} %collective-permute-done.41.refs_4_), channel_id=1, source_target_pairs={{0,8},{2,6},{8,16},{10,2},{16,24},{18,10},{24,28},{26,18},{28,20},... | collective-permute-start | bytes 1376264 | tf_op jit(solution)/shard_map/ppermute | solution.py:135
  158.2 15.5 %collective-permute-start.42 = (bf16[256,896]{1,0:T(8,128)(2,1)S(1)}, bf16[256,896]{1,0:T(8,128)(2,1)S(1)}, u32[]{:S(2)}, u32[]{:S(2)}) collective-permute-start(bf16[256,896]{1,0:T(8,128)(2,1)S(1)} %collective-permute-done.38.refs_3_), channel_id=1, source_target_pairs={{0,8},{2,6},{8,16},{10,2},{16,24},{18,10},{24,28},{26,18},{28,20},... | collective-permute-start | bytes 1376264 | tf_op jit(solution)/shard_map/ppermute | solution.py:135
  160.7 12.9 %collective-permute-start.48 = (bf16[256,896]{1,0:T(8,128)(2,1)S(1)}, bf16[256,896]{1,0:T(8,128)(2,1)S(1)}, u32[]{:S(2)}, u32[]{:S(2)}) collective-permute-start(bf16[256,896]{1,0:T(8,128)(2,1)S(1)} %collective-permute-done.46.refs_4_), channel_id=1, source_target_pairs={{0,8},{2,6},{8,16},{10,2},{16,24},{18,10},{24,28},{26,18},{28,20},... | collective-permute-start | bytes 1376264 | tf_op jit(solution)/shard_map/ppermute | solution.py:135
  161.2 11.1 %collective-permute-start.43 = (bf16[384,512]{1,0:T(8,128)(2,1)S(1)}, bf16[384,512]{1,0:T(8,128)(2,1)S(1)}, u32[]{:S(2)}, u32[]{:S(2)}) collective-permute-start(bf16[384,512]{1,0:T(8,128)(2,1)S(1)} %get-tuple-element.206), channel_id=1, source_target_pairs={{0,1},{1,0},{2,3},{3,2},{4,5},{5,4},{6,7},{7,6},{8,9},{9,8},{10,11... | collective-permute-start | bytes 1179656 | tf_op jit(solution)/shard_map/ppermute | solution.py:271
  161.7 12.5 %collective-permute-start.51 = (bf16[256,896]{1,0:T(8,128)(2,1)S(1)}, bf16[256,896]{1,0:T(8,128)(2,1)S(1)}, u32[]{:S(2)}, u32[]{:S(2)}) collective-permute-start(bf16[256,896]{1,0:T(8,128)(2,1)S(1)} %collective-permute-done.46.refs_4_), channel_id=1, source_target_pairs={{0,2},{2,0},{4,6},{6,4},{8,10},{10,8},{12,14},{14,12},{16,18},{18,... | collective-permute-start | bytes 1376264 | tf_op jit(solution)/shard_map/ppermute | solution.py:135
  161.7 12.4 %collective-permute-start.50 = (bf16[256,896]{1,0:T(8,128)(2,1)S(1)}, bf16[256,896]{1,0:T(8,128)(2,1)S(1)}, u32[]{:S(2)}, u32[]{:S(2)}) collective-permute-start(bf16[256,896]{1,0:T(8,128)(2,1)S(1)} %collective-permute-done.38.refs_3_), channel_id=1, source_target_pairs={{0,2},{2,0},{4,6},{6,4},{8,10},{10,8},{12,14},{14,12},{16,18},{18,... | collective-permute-start | bytes 1376264 | tf_op jit(solution)/shard_map/ppermute | solution.py:135
  (29 other events, 212.3 us)

commit v4 on v3

--- a/solution.py
+++ b/solution.py
@@ -145,12 +145,8 @@
     def rows_at(array, m, chip, c):
         return lax.dynamic_slice(array, (m, chip, c, 0, 0), (1, 1, 1, rows, cols)).reshape(rows, cols)
 
-    units = {(j, m): rows_at(shards, m, *siblings_at(j)) for j in range(2) for m in range(2)}
-    inner.send_columns(units[1, 1])
-    early = {key: send(value, swap) for key, value in units.items()}
-    rest, *first = after((shards, *early.values()))
-    early = dict(zip(early, first))
-    whole = send(rest, swap)
+    early = {(j, m): send(rows_at(shards, m, *siblings_at(j)), swap) for j in range(2) for m in range(2)}
+    whole = None
 
     def pair(whole, j, m):
         theirs = early[j, m] if (j, m) in early else rows_at(whole, m, *mine_at(j))
@@ -165,6 +161,12 @@
             if j:
                 total = total + came[m].astype(f32)
             out = total.astype(bf16)
+            if (j, m) == (0, 0):
+                rest, out = after((shards, out))
+                keys = [key for key in early if key != (0, 0)]
+                rest, *values = after((rest, *(early[key] for key in keys)))
+                early.update(zip(keys, values))
+                whole = send(rest, swap)
             if (j, m) < (1, 1):
                 following = (j, 1) if m == 0 else (j + 1, 0)
                 early[following], out = after((early[following], out))
@@ -172,7 +174,9 @@
                 whole = follow(chain, whole, out)
             else:
                 whole, out = after((whole, out))
-            if m == 1 and j in (2, 3, 4):
+            if (j, m) == (0, 1):
+                inner.send_columns(out)
+            if m == 1 and j in (2, 5):
                 whole = inner.early(j, out, whole)
             came[m] = send(out, perm)
 
@@ -204,7 +208,7 @@
             held.append((send(value, swap), (m, chips + k)))
         gathered = place(chain, gathered, shape, index, entries)
         entries = held
-        if k == 1:
+        if k == 6:
             gathered, momentum_out = after((gathered, jnp.stack(momentum_out)[:, None]))
         inner.late(k)
         if k == last - 1:
@@ -326,9 +330,9 @@
         half = self.steps // 2
         own, _, _ = self.specs(half * second)
         return self.call(
-            own_term_kernel, "own_term", jax.ShapeDtypeStruct((self.depth // 2, self.width), bf16),
+            own_term_kernel, "own_term", pltpu.HBM((self.depth // 2, self.width), bf16),
             [own, pl.BlockSpec((self.count, self.width), lambda i, where: (0, 0))],
-            pl.BlockSpec((self.tile, self.width), lambda i, where: (i, 0)), [], half, in_place(self.tokens), self.cotangent,
+            pl.BlockSpec((self.tile, self.width), lambda i, where: (i, 0)), [], half, in_place(self.tokens), in_place(self.cotangent),
         )
 
     def add_terms(self, second):
@@ -338,7 +342,7 @@
         cotangents = pl.BlockSpec((self.count, self.width), lambda i, where: (0, last))
         operands, in_specs = [self.terms[second]], [pl.BlockSpec((self.tile, self.width), lambda i, where: (i, 0))]
         for a, b in zip(self.first, self.second):
-            operands += [a, b, a, b]
+            operands += [in_place(value) for value in (a, b, a, b)]
             in_specs += others + [cotangents] * 2
         self.grad = self.call(
             grad_kernel, "grad", jax.ShapeDtypeStruct((self.depth, self.width), bf16), in_specs + [in_hbm] * second,
@@ -352,13 +356,9 @@
 
     def early(self, j, gate, whole):
         self.chain.gates = [gate]
-        if j == 2:
-            self.keys = self.multiply_keys([in_place(self.tokens)], f32)
-            whole, self.keys = after((whole, self.keys))
-        else:
-            term = self.own_term(j - 2 - 1)
-            whole, term = after((whole, term))
-            self.terms.append(term)
+        term = self.own_term(len(self.terms))
+        whole, term = after((whole, term))
+        self.terms.append(term)
         return whole
 
     def finish_keys(self):
@@ -374,11 +374,15 @@
         )
 
     def late(self, k):
+        if k == 1:
+            self.keys = self.multiply_keys([in_place(self.tokens)], f32)
         if k == 2:
-            others = [self.multiply_keys(pair, bf16) for pair in zip(self.first, self.second)]
+            others = [
+                self.multiply_keys([in_place(value) for value in pair], bf16) for pair in zip(self.first, self.second)
+            ]
             self.came = [self.shift(value, self.parts - s) for s, value in enumerate(others, 1)]
-        if k in (3, 4):
-            self.add_terms(k - 3)
+        if k in (4, 5):
+            self.add_terms(k - 4)
         if k == 6:
             self.finish_keys()
 

time: 179 us -> 171 us (0.955)
  starting transfers between devices: 37.2 us -> 51.9 us
  other arithmetic: 37.5 us -> 25.2 us
  waiting for transfers between devices: 49.5 us -> 38.5 us
  Pallas kernels: 48.6 us -> 50.5 us
    ppermute x49, starting transfers between devices: 30.9 us -> 44.5 us  [send(): return lax.ppermute(x, 'replica', perm)]
    convert_element_type x14, other arithmetic: 28 us -> 18.8 us  [outer_step(): out = total.astype(bf16)]
    ppermute x1, waiting for transfers between devices: 8.24 us -> 0.38 us  [shift(): lax.ppermute(x, 'fsdp', [(k, (k + s) % self.parts) for k in range(self.pa...]
    ppermute x49, waiting for transfers between devices: 41.2 us -> 38.2 us  [send(): return lax.ppermute(x, 'replica', perm)]
    unnamed x18 -> x8, local copies, waits for them, and re-layouts: 1.98 us -> 0.02 us
    pallas_call x18, Pallas kernels: 48.6 us -> 50.5 us  [call(): pl.pallas_call(body, **params)]
  transfers between devices with their start and end apart: 52 -> 52, of which waited for: 22 -> 22; matrix products, arithmetic and copies ran while one was open for 21% -> 15% of each run, Pallas kernels for 27% -> 29%
where the time goes in v4:
time: 171 us; the launch traced here: 170 us
  starting transfers between devices  51.9 us (30%)
  Pallas kernels  50.5 us (30%)
  waiting for transfers between devices  38.5 us (23%)
  other arithmetic  25.2 us (15%)
  local copies, waits for them, and re-layouts  2.46 us (1%)
    pallas_call x18, Pallas kernels, call(): pl.pallas_call(body, **params)  50.5 us
    ppermute x49, starting transfers between devices, send(): return lax.ppermute(x, 'replica', perm)  44.5 us
    ppermute x49, waiting for transfers between devices, send(): return lax.ppermute(x, 'replica', perm)  38.2 us
    convert_element_type x14, other arithmetic, outer_step(): out = total.astype(bf16)  18.8 us
    ppermute x2, starting transfers between devices, shift(): return lax.ppermute(x, ('replica', 'fsdp'), pairs)  5.89 us
    convert_element_type x2, other arithmetic, outer_step(): (weights - outer_rate * (pseudo_grad + momentum_decay * momentum_new)).as...  4.88 us
  transfers between devices with their start and end apart: 52, of which 22 were waited for; matrix products, arithmetic and copies ran while one was open for 15% of the time, Pallas kernels for 29%

profile of v4, /device:TPU:0, one launch (start us, length us, event | category | flops | bytes accessed | tf_op | source)
XLA Modules:
  0.0 169.7 jit_solution(6749538279814065627)
XLA Ops:
  0.8 2.4 %dynamic-slice_bitcast_fusion = (bf16[256,896]{1,0:T(8,128)(2,1)S(1)}, bf16[256,896]{1,0:T(8,128)(2,1)S(1)}, bf16[256,896]{1,0:T(8,128)(2,1)}, bf16[256,896]{1,0:T(8,128)(2,1)S(1)}) fusion(bf16[2,8,2,256,896]{4,3,2,1,0:T(8,128)(2,1)} %bitcast.129, s32[]{:T(128)S(6)} %select_n.248, s32[]{:T(128)S(6)} %select_n.242, s32[]{:T(128)S(6)} %select_n.241), kind=kLoop, calls=%fused_computation.43 | loop fusion | bytes 3670028 | tf_op jit(solution)/shard_map/reshape | solution.py:146
  7.4 2.7 %collective-permute-start.5 = (bf16[256,896]{1,0:T(8,128)(2,1)S(1)}, bf16[256,896]{1,0:T(8,128)(2,1)S(1)}, u32[]{:S(2)}, u32[]{:S(2)}) collective-permute-start(bf16[256,896]{1,0:T(8,128)(2,1)S(1)} %fusion.7), channel_id=1, source_target_pairs={{0,8},{2,6},{8,16},{10,2},{16,24},{18,10},{24,28},{26,18},{28,20},... | collective-permute-start | bytes 1376264 | tf_op jit(solution)/shard_map/ppermute | solution.py:135
  12.9 3.8 %columns.1 = (f32[8,128]{1,0:T(8,128)S(1)}, bf16[384,4608]{1,0:T(8,128)(2,1)}) custom-call(s32[1]{0:T(128)} %bitcast.9.refs_0_, bf16[384,8192]{1,0:T(8,128)(2,1)} %refs_1_.7, bf16[384,512]{1,0:T(8,128)(2,1)} %refs_2_.5, bf16[256,896]{1,0:T(8,128)(2,1)S(1)} %fusion.2.refs_3_), custom_call_target="tpu_custom_call" | custom-call | tf_op jit(solution)/shard_map/columns/pallas_call | solution.py:73
  16.6 3.4 %collective-permute-start.16 = (bf16[384,4608]{1,0:T(8,128)(2,1)}, bf16[384,4608]{1,0:T(8,128)(2,1)}, u32[]{:S(2)}, u32[]{:S(2)}) collective-permute-start(bf16[384,4608]{1,0:T(8,128)(2,1)} %get-tuple-element.150), channel_id=1, source_target_pairs={{0,1},{1,0},{4,5},{5,4},{8,9},{9,8},{12,13},{13,12},{16,17},{17,16... | collective-permute-start | bytes 10616840 | tf_op jit(solution)/shard_map/ppermute | solution.py:281
  25.6 3.9 %collective-permute-done.4.refs_0_ = bf16[2,8,2,256,896]{4,3,2,1,0:T(8,128)(2,1)} collective-permute-done((bf16[2,8,2,256,896]{4,3,2,1,0:T(8,128)(2,1)}, bf16[2,8,2,256,896]{4,3,2,1,0:T(8,128)(2,1)}, u32[]{:S(2)}, u32[]{:S(2)}) %collective-permute-start.4) | collective-permute-done | bytes 14680096 | tf_op jit(solution)/shard_map/ppermute | solution.py:135
  31.1 2.7 %collective-permute-start.9 = (bf16[256,896]{1,0:T(8,128)(2,1)S(1)}, bf16[256,896]{1,0:T(8,128)(2,1)S(1)}, u32[]{:S(2)}, u32[]{:S(2)}) collective-permute-start(bf16[256,896]{1,0:T(8,128)(2,1)S(1)} %fusion.19), channel_id=1, source_target_pairs={{0,8},{2,6},{8,16},{10,2},{16,24},{18,10},{24,28},{26,18},{28,20},... | collective-permute-start | bytes 1376264 | tf_op jit(solution)/shard_map/ppermute | solution.py:135
  37.7 4.3 %own_term.2 = (f32[8,128]{1,0:T(8,128)S(1)}, bf16[2048,512]{1,0:T(8,128)(2,1)}) custom-call(s32[2]{0:T(128)S(1)} %pad_add_fusion.refs_0_, bf16[384,8192]{1,0:T(8,128)(2,1)} %refs_1_.7, bf16[384,512]{1,0:T(8,128)(2,1)} %refs_2_.5, bf16[256,896]{1,0:T(8,128)(2,1)S(1)} %fusion.18.refs_3_, f32[8,128]{1,0:T(8,128)S(1)} %get-tuple-element.131.refs_4_), custom_call_target="tpu_custom_call" | custom-call | tf_op jit(solution)/shard_map/own_term/pallas_call | solution.py:73
  46.7 2.1 %collective-permute-start.12 = (bf16[256,896]{1,0:T(8,128)(2,1)S(1)}, bf16[256,896]{1,0:T(8,128)(2,1)S(1)}, u32[]{:S(2)}, u32[]{:S(2)}) collective-permute-start(bf16[256,896]{1,0:T(8,128)(2,1)S(1)} %fusion.16), channel_id=1, source_target_pairs={{0,8},{2,6},{8,16},{10,2},{16,24},{18,10},{24,28},{26,18},{28,20},... | collective-permute-start | bytes 1376264 | tf_op jit(solution)/shard_map/ppermute | solution.py:135
  48.9 3.0 %collective-permute-done.11 = bf16[256,896]{1,0:T(8,128)(2,1)S(1)} collective-permute-done((bf16[256,896]{1,0:T(8,128)(2,1)S(1)}, bf16[256,896]{1,0:T(8,128)(2,1)S(1)}, u32[]{:S(2)}, u32[]{:S(2)}) %collective-permute-start.11) | collective-permute-done | bytes 458784 | tf_op jit(solution)/shard_map/ppermute | solution.py:135
  54.8 2.0 %collective-permute-done.12 = bf16[256,896]{1,0:T(8,128)(2,1)S(1)} collective-permute-done((bf16[256,896]{1,0:T(8,128)(2,1)S(1)}, bf16[256,896]{1,0:T(8,128)(2,1)S(1)}, u32[]{:S(2)}, u32[]{:S(2)}) %collective-permute-start.12) | collective-permute-done | bytes 458784 | tf_op jit(solution)/shard_map/ppermute | solution.py:135
  59.7 2.0 %collective-permute-done.13 = bf16[256,896]{1,0:T(8,128)(2,1)S(1)} collective-permute-done((bf16[256,896]{1,0:T(8,128)(2,1)S(1)}, bf16[256,896]{1,0:T(8,128)(2,1)S(1)}, u32[]{:S(2)}, u32[]{:S(2)}) %collective-permute-start.13) | collective-permute-done | bytes 458784 | tf_op jit(solution)/shard_map/ppermute | solution.py:135
  64.6 2.5 %collective-permute-start.33 = (bf16[384,4608]{1,0:T(8,128)(2,1)}, bf16[384,4608]{1,0:T(8,128)(2,1)}, u32[]{:S(2)}, u32[]{:S(2)}) collective-permute-start(bf16[384,4608]{1,0:T(8,128)(2,1)} %get-tuple-element.150), channel_id=1, source_target_pairs={{2,3},{3,2},{6,7},{7,6},{10,11},{11,10},{14,15},{15,14},{18,19},{1... | collective-permute-start | bytes 10616840 | tf_op jit(solution)/shard_map/ppermute | solution.py:281
  69.6 4.3 %own_term.3 = (f32[8,128]{1,0:T(8,128)S(1)}, bf16[2048,512]{1,0:T(8,128)(2,1)}) custom-call(s32[2]{0:T(128)S(1)} %pad_add_fusion.refs_0_, bf16[384,8192]{1,0:T(8,128)(2,1)} %refs_1_.7, bf16[384,512]{1,0:T(8,128)(2,1)} %refs_2_.5, bf16[256,896]{1,0:T(8,128)(2,1)S(1)} %fusion.12.refs_3_, f32[8,128]{1,0:T(8,128)S(1)} %get-tuple-element.146.refs_4_), custom_call_target="tpu_custom_call" | custom-call | tf_op jit(solution)/shard_map/own_term/pallas_call | solution.py:73
  77.0 2.1 %fusion.10 = bf16[256,896]{1,0:T(8,128)(2,1)} fusion(bf16[256,896]{1,0:T(8,128)(2,1)S(1)} %collective-permute-done.17, bf16[2,8,2,256,896]{4,3,2,1,0:T(8,128)(2,1)} %get-tuple-element.156, s32[]{:T(128)S(6)} %select_n.241, s32[]{:T(128)S(6)} %select_n.239, bf16[2,8,2,256,896]{4,3,2,1,0:T(8,128)(2,1)} %bitcast.144), kind=kLoop, calls=%fused_computation.24 | loop fusion | flops 1376256 | bytes 1835016 | tf_op jit(solution)/shard_map/convert_element_type | solution.py:163
  80.1 3.6 %collective-permute-done.18 = bf16[256,896]{1,0:T(8,128)(2,1)S(1)} collective-permute-done((bf16[256,896]{1,0:T(8,128)(2,1)S(1)}, bf16[256,896]{1,0:T(8,128)(2,1)S(1)}, u32[]{:S(2)}, u32[]{:S(2)}) %collective-permute-start.18) | collective-permute-done | bytes 458784 | tf_op jit(solution)/shard_map/ppermute | solution.py:135
  83.7 1.9 %fusion = (bf16[256,896]{1,0:T(8,128)(2,1)S(1)}, f32[256,896]{1,0:T(8,128)S(1)}) fusion(bf16[256,896]{1,0:T(8,128)(2,1)S(1)} %collective-permute-done.18, bf16[2,1,256,896]{3,2,1,0:T(8,128)(2,1)S(1)} %copy-done.3, bf16[2,8,2,256,896]{4,3,2,1,0:T(8,128)(2,1)} %get-tuple-element.156, s32[]{:T(128)S(6)} %select_n.268, s32[]{:T(128)S(6)} %select_n.239, ...), kind=kLoop, calls=%fused_computation.5 | loop fusion | flops 3440640 | bytes 4128776 | tf_op jit(solution)/shard_map/convert_element_type | solution.py:190
  86.8 1.8 %collective-permute-done.20 = bf16[256,896]{1,0:T(8,128)(2,1)S(1)} collective-permute-done((bf16[256,896]{1,0:T(8,128)(2,1)}, bf16[256,896]{1,0:T(8,128)(2,1)S(1)}, u32[]{:S(2)}, u32[]{:S(2)}) %collective-permute-start.20) | collective-permute-done | bytes 458784 | tf_op jit(solution)/shard_map/ppermute | solution.py:135
  88.6 3.0 %fusion.1 = (bf16[256,896]{1,0:T(8,128)(2,1)S(1)}, f32[256,896]{1,0:T(8,128)}) fusion(bf16[256,896]{1,0:T(8,128)(2,1)S(1)} %collective-permute-done.20, bf16[2,1,256,896]{3,2,1,0:T(8,128)(2,1)} %param.10, bf16[2,8,2,256,896]{4,3,2,1,0:T(8,128)(2,1)} %get-tuple-element.156, s32[]{:T(128)S(6)} %select_n.268, s32[]{:T(128)S(6)} %select_n.239, ...), kind=kLoop, calls=%fused_computation.6 | loop fusion | flops 3440640 | bytes 4128776 | tf_op jit(solution)/shard_map/convert_element_type | solution.py:190
  96.4 3.6 %collective-permute-done.24.refs_4_ = bf16[256,896]{1,0:T(8,128)(2,1)S(1)} collective-permute-done((bf16[256,896]{1,0:T(8,128)(2,1)S(1)}, bf16[256,896]{1,0:T(8,128)(2,1)S(1)}, u32[]{:S(2)}, u32[]{:S(2)}) %collective-permute-start.24) | collective-permute-done | bytes 458784 | tf_op jit(solution)/shard_map/ppermute | solution.py:135
  101.7 1.8 %place.10 = (f32[8,128]{1,0:T(8,128)S(1)}, bf16[2,16,256,896]{3,2,1,0:T(8,128)(2,1)}) custom-call(s32[16]{0:T(128)S(1)} %stack.88.refs_0_, bf16[256,896]{1,0:T(8,128)(2,1)S(1)} %collective-permute-done.22.refs_1_, bf16[256,896]{1,0:T(8,128)(2,1)S(1)} %collective-permute-done.23.refs_2_, ...), custom_call_target="tpu_custom_call", output_to_operand_aliasing={{1}: (5, {})} | custom-call | tf_op jit(solution)/shard_map/place/pallas_call | solution.py:73
  106.1 3.8 %collective-permute-done.28.refs_4_ = bf16[256,896]{1,0:T(8,128)(2,1)S(1)} collective-permute-done((bf16[256,896]{1,0:T(8,128)(2,1)S(1)}, bf16[256,896]{1,0:T(8,128)(2,1)S(1)}, u32[]{:S(2)}, u32[]{:S(2)}) %collective-permute-start.28) | collective-permute-done | bytes 458784 | tf_op jit(solution)/shard_map/ppermute | solution.py:135
  111.0 5.6 %keys.2 = (f32[8,128]{1,0:T(8,128)S(1)}, f32[384,512]{1,0:T(8,128)S(1)}) custom-call(s32[2]{0:T(128)S(1)} %pad_add_fusion.refs_0_, bf16[384,8192]{1,0:T(8,128)(2,1)} %refs_1_.7, bf16[4096,512]{1,0:T(8,128)(2,1)} %bitcast.127, f32[8,128]{1,0:T(8,128)S(1)} %get-tuple-element.171.refs_3_), custom_call_target="tpu_custom_call" | custom-call | tf_op jit(solution)/shard_map/keys/pallas_call | solution.py:73
  117.2 1.8 %place.11 = (f32[8,128]{1,0:T(8,128)S(1)}, bf16[2,16,256,896]{3,2,1,0:T(8,128)(2,1)}) custom-call(s32[16]{0:T(128)S(1)} %stack.88.refs_0_, bf16[256,896]{1,0:T(8,128)(2,1)S(1)} %collective-permute-done.26.refs_1_, bf16[256,896]{1,0:T(8,128)(2,1)S(1)} %collective-permute-done.27.refs_2_, ...), custom_call_target="tpu_custom_call", output_to_operand_aliasing={{1}: (5, {})} | custom-call | tf_op jit(solution)/shard_map/place/pallas_call | solution.py:73
  121.7 5.9 %keys.3 = (f32[8,128]{1,0:T(8,128)S(1)}, bf16[384,512]{1,0:T(8,128)(2,1)S(1)}) custom-call(s32[2]{0:T(128)S(1)} %pad_add_fusion.refs_0_, bf16[384,4608]{1,0:T(8,128)(2,1)} %collective-permute-done.16.refs_1_.refs_2_.refs_4_, bf16[384,4608]{1,0:T(8,128)(2,1)} %collective-permute-done.33.refs_2_.refs_3_.refs_5_, bf16[4096,512]{1,0:T(8,128)(2,1)} %bitcast.128, ...), custom_call_target="tpu_custom_call" | custom-call | tf_op jit(solution)/shard_map/keys/pallas_call | solution.py:73
  128.2 1.8 %place.12 = (f32[8,128]{1,0:T(8,128)S(1)}, bf16[2,16,256,896]{3,2,1,0:T(8,128)(2,1)}) custom-call(s32[16]{0:T(128)S(1)} %stack.88.refs_0_, bf16[256,896]{1,0:T(8,128)(2,1)S(1)} %collective-permute-done.30.refs_1_, bf16[256,896]{1,0:T(8,128)(2,1)S(1)} %collective-permute-done.31.refs_2_, ...), custom_call_target="tpu_custom_call", output_to_operand_aliasing={{1}: (5, {})} | custom-call | tf_op jit(solution)/shard_map/place/pallas_call | solution.py:73
  134.5 1.8 %place.13 = (f32[8,128]{1,0:T(8,128)S(1)}, bf16[2,16,256,896]{3,2,1,0:T(8,128)(2,1)}) custom-call(s32[16]{0:T(128)S(1)} %stack.88.refs_0_, bf16[256,896]{1,0:T(8,128)(2,1)S(1)} %collective-permute-done.35.refs_1_, bf16[256,896]{1,0:T(8,128)(2,1)S(1)} %collective-permute-done.36.refs_2_, ...), custom_call_target="tpu_custom_call", output_to_operand_aliasing={{1}: (5, {})} | custom-call | tf_op jit(solution)/shard_map/place/pallas_call | solution.py:73
  136.3 2.2 %collective-permute-done.34.refs_3_ = bf16[256,896]{1,0:T(8,128)(2,1)S(1)} collective-permute-done((bf16[256,896]{1,0:T(8,128)(2,1)S(1)}, bf16[256,896]{1,0:T(8,128)(2,1)S(1)}, u32[]{:S(2)}, u32[]{:S(2)}) %collective-permute-start.34) | collective-permute-done | bytes 458784 | tf_op jit(solution)/shard_map/ppermute | solution.py:135
  139.2 4.3 %collective-permute-done.41.refs_4_ = bf16[256,896]{1,0:T(8,128)(2,1)S(1)} collective-permute-done((bf16[256,896]{1,0:T(8,128)(2,1)S(1)}, bf16[256,896]{1,0:T(8,128)(2,1)S(1)}, u32[]{:S(2)}, u32[]{:S(2)}) %collective-permute-start.41) | collective-permute-done | bytes 458784 | tf_op jit(solution)/shard_map/ppermute | solution.py:135
  144.7 5.0 %grad.2 = (f32[8,128]{1,0:T(8,128)S(1)}, bf16[4096,512]{1,0:T(8,128)(2,1)}) custom-call(s32[2]{0:T(128)S(1)} %pad_add_fusion.refs_0_, bf16[2048,512]{1,0:T(8,128)(2,1)S(1)} %copy-done.1, bf16[384,4608]{1,0:T(8,128)(2,1)} %collective-permute-done.16.refs_1_.refs_2_.refs_4_, bf16[384,4608]{1,0:T(8,128)(2,1)} %collective-permute-done.33.refs_2_.refs_3_.refs_5_, ...), custom_call_target="tpu_custom_call" | custom-call | tf_op jit(solution)/shard_map/grad/pallas_call | solution.py:73
  149.7 1.8 %place.14 = (f32[8,128]{1,0:T(8,128)S(1)}, bf16[2,16,256,896]{3,2,1,0:T(8,128)(2,1)}) custom-call(s32[16]{0:T(128)S(1)} %stack.88.refs_0_, bf16[256,896]{1,0:T(8,128)(2,1)S(1)} %collective-permute-done.39.refs_1_, bf16[256,896]{1,0:T(8,128)(2,1)S(1)} %collective-permute-done.40.refs_2_, ...), custom_call_target="tpu_custom_call", output_to_operand_aliasing={{1}: (5, {})} | custom-call | tf_op jit(solution)/shard_map/place/pallas_call | solution.py:73
  156.9 4.7 %grad.3 = (f32[8,128]{1,0:T(8,128)S(1)}, bf16[4096,512]{1,0:T(8,128)(2,1)}) custom-call(s32[2]{0:T(128)S(1)} %pad_add_fusion.refs_0_, bf16[2048,512]{1,0:T(8,128)(2,1)S(1)} %copy-done, bf16[384,4608]{1,0:T(8,128)(2,1)} %collective-permute-done.16.refs_1_.refs_2_.refs_4_, ...), custom_call_target="tpu_custom_call", output_to_operand_aliasing={{1}: (6, {})} | custom-call | tf_op jit(solution)/shard_map/grad/pallas_call | solution.py:73
  166.3 1.8 %place.16 = (f32[8,128]{1,0:T(8,128)S(1)}, bf16[2,16,256,896]{3,2,1,0:T(8,128)(2,1)}) custom-call(s32[16]{0:T(128)S(1)} %stack.88.refs_0_, bf16[256,896]{1,0:T(8,128)(2,1)S(1)} %collective-permute-done.50.refs_1_, bf16[256,896]{1,0:T(8,128)(2,1)S(1)} %collective-permute-done.51.refs_2_, ...), custom_call_target="tpu_custom_call", output_to_operand_aliasing={{1}: (5, {})} | custom-call | tf_op jit(solution)/shard_map/place/pallas_call | solution.py:73
  (118 shorter events, 71.1 us)
Async XLA Ops:
  7.0 22.5 %collective-permute-start.4 = (bf16[2,8,2,256,896]{4,3,2,1,0:T(8,128)(2,1)}, bf16[2,8,2,256,896]{4,3,2,1,0:T(8,128)(2,1)}, u32[]{:S(2)}, u32[]{:S(2)}) collective-permute-start(bf16[2,8,2,256,896]{4,3,2,1,0:T(8,128)(2,1)} %bitcast.131), channel_id=1, source_target_pairs={{0,2},{2,0},{4,6},{6,4},{8,10},{10,8},{12,14},{14,12},{16,18},{18,... | collective-permute-start | bytes 44040200 | tf_op jit(solution)/shard_map/ppermute | solution.py:135
  7.4 12.6 %collective-permute-start.5 = (bf16[256,896]{1,0:T(8,128)(2,1)S(1)}, bf16[256,896]{1,0:T(8,128)(2,1)S(1)}, u32[]{:S(2)}, u32[]{:S(2)}) collective-permute-start(bf16[256,896]{1,0:T(8,128)(2,1)S(1)} %fusion.7), channel_id=1, source_target_pairs={{0,8},{2,6},{8,16},{10,2},{16,24},{18,10},{24,28},{26,18},{28,20},... | collective-permute-start | bytes 1376264 | tf_op jit(solution)/shard_map/ppermute | solution.py:135
  11.2 11.6 %collective-permute-start.6 = (bf16[256,896]{1,0:T(8,128)(2,1)S(1)}, bf16[256,896]{1,0:T(8,128)(2,1)S(1)}, u32[]{:S(2)}, u32[]{:S(2)}) collective-permute-start(bf16[256,896]{1,0:T(8,128)(2,1)S(1)} %fusion.2.refs_3_), channel_id=1, source_target_pairs={{0,8},{2,6},{8,16},{10,2},{16,24},{18,10},{24,28},{26,18},{28,20},... | collective-permute-start | bytes 1376264 | tf_op jit(solution)/shard_map/ppermute | solution.py:135
  16.6 57.2 %collective-permute-start.16 = (bf16[384,4608]{1,0:T(8,128)(2,1)}, bf16[384,4608]{1,0:T(8,128)(2,1)}, u32[]{:S(2)}, u32[]{:S(2)}) collective-permute-start(bf16[384,4608]{1,0:T(8,128)(2,1)} %get-tuple-element.150), channel_id=1, source_target_pairs={{0,1},{1,0},{4,5},{5,4},{8,9},{9,8},{12,13},{13,12},{16,17},{17,16... | collective-permute-start | bytes 10616840 | tf_op jit(solution)/shard_map/ppermute | solution.py:281
  24.1 10.6 %collective-permute-start.8 = (bf16[256,896]{1,0:T(8,128)(2,1)S(1)}, bf16[256,896]{1,0:T(8,128)(2,1)S(1)}, u32[]{:S(2)}, u32[]{:S(2)}) collective-permute-start(bf16[256,896]{1,0:T(8,128)(2,1)S(1)} %fusion.6.refs_1_), channel_id=1, source_target_pairs={{0,8},{2,6},{8,16},{10,2},{16,24},{18,10},{24,28},{26,18},{28,20},... | collective-permute-start | bytes 1376264 | tf_op jit(solution)/shard_map/ppermute | solution.py:135
  31.1 10.9 %collective-permute-start.9 = (bf16[256,896]{1,0:T(8,128)(2,1)S(1)}, bf16[256,896]{1,0:T(8,128)(2,1)S(1)}, u32[]{:S(2)}, u32[]{:S(2)}) collective-permute-start(bf16[256,896]{1,0:T(8,128)(2,1)S(1)} %fusion.19), channel_id=1, source_target_pairs={{0,8},{2,6},{8,16},{10,2},{16,24},{18,10},{24,28},{26,18},{28,20},... | collective-permute-start | bytes 1376264 | tf_op jit(solution)/shard_map/ppermute | solution.py:135
  36.0 9.2 %collective-permute-start.10 = (bf16[256,896]{1,0:T(8,128)(2,1)S(1)}, bf16[256,896]{1,0:T(8,128)(2,1)}, u32[]{:S(2)}, u32[]{:S(2)}) collective-permute-start(bf16[256,896]{1,0:T(8,128)(2,1)S(1)} %fusion.18.refs_3_), channel_id=1, source_target_pairs={{0,8},{2,6},{8,16},{10,2},{16,24},{18,10},{24,28},{26,18},{28,20},... | collective-permute-start | bytes 1376264 | tf_op jit(solution)/shard_map/ppermute | solution.py:135
  46.7 10.1 %collective-permute-start.12 = (bf16[256,896]{1,0:T(8,128)(2,1)S(1)}, bf16[256,896]{1,0:T(8,128)(2,1)S(1)}, u32[]{:S(2)}, u32[]{:S(2)}) collective-permute-start(bf16[256,896]{1,0:T(8,128)(2,1)S(1)} %fusion.16), channel_id=1, source_target_pairs={{0,8},{2,6},{8,16},{10,2},{16,24},{18,10},{24,28},{26,18},{28,20},... | collective-permute-start | bytes 1376264 | tf_op jit(solution)/shard_map/ppermute | solution.py:135
  63.1 10.8 %collective-permute-start.15 = (bf16[256,896]{1,0:T(8,128)(2,1)S(1)}, bf16[256,896]{1,0:T(8,128)(2,1)S(1)}, u32[]{:S(2)}, u32[]{:S(2)}) collective-permute-start(bf16[256,896]{1,0:T(8,128)(2,1)S(1)} %fusion.13), channel_id=1, source_target_pairs={{0,8},{2,6},{8,16},{10,2},{16,24},{18,10},{24,28},{26,18},{28,20},... | collective-permute-start | bytes 1376264 | tf_op jit(solution)/shard_map/ppermute | solution.py:135
  64.6 57.0 %collective-permute-start.33 = (bf16[384,4608]{1,0:T(8,128)(2,1)}, bf16[384,4608]{1,0:T(8,128)(2,1)}, u32[]{:S(2)}, u32[]{:S(2)}) collective-permute-start(bf16[384,4608]{1,0:T(8,128)(2,1)} %get-tuple-element.150), channel_id=1, source_target_pairs={{2,3},{3,2},{6,7},{7,6},{10,11},{11,10},{14,15},{15,14},{18,19},{1... | collective-permute-start | bytes 10616840 | tf_op jit(solution)/shard_map/ppermute | solution.py:281
  79.1 9.5 %collective-permute-start.20 = (bf16[256,896]{1,0:T(8,128)(2,1)}, bf16[256,896]{1,0:T(8,128)(2,1)S(1)}, u32[]{:S(2)}, u32[]{:S(2)}) collective-permute-start(bf16[256,896]{1,0:T(8,128)(2,1)} %fusion.10), channel_id=1, source_target_pairs={{0,8},{2,6},{8,16},{10,2},{16,24},{18,10},{24,28},{26,18},{28,20},... | collective-permute-start | bytes 1376264 | tf_op jit(solution)/shard_map/ppermute | solution.py:135
  85.6 9.2 %collective-permute-start.19 = (bf16[256,896]{1,0:T(8,128)(2,1)S(1)}, bf16[256,896]{1,0:T(8,128)(2,1)S(1)}, u32[]{:S(2)}, u32[]{:S(2)}) collective-permute-start(bf16[256,896]{1,0:T(8,128)(2,1)S(1)} %get-tuple-element.155.refs_1_), channel_id=1, source_target_pairs={{0,8},{2,6},{8,16},{10,2},{16,24},{18,10},{24,28},{26,18},{28,20},... | collective-permute-start | bytes 1376264 | tf_op jit(solution)/shard_map/ppermute | solution.py:135
  94.9 10.1 %collective-permute-start.21 = (bf16[256,896]{1,0:T(8,128)(2,1)S(1)}, bf16[256,896]{1,0:T(8,128)(2,1)S(1)}, u32[]{:S(2)}, u32[]{:S(2)}) collective-permute-start(bf16[256,896]{1,0:T(8,128)(2,1)S(1)} %collective-permute-done.19.refs_3_), channel_id=1, source_target_pairs={{0,8},{2,6},{8,16},{10,2},{16,24},{18,10},{24,28},{26,18},{28,20},... | collective-permute-start | bytes 1376264 | tf_op jit(solution)/shard_map/ppermute | solution.py:135
  100.1 9.8 %collective-permute-start.28 = (bf16[256,896]{1,0:T(8,128)(2,1)S(1)}, bf16[256,896]{1,0:T(8,128)(2,1)S(1)}, u32[]{:S(2)}, u32[]{:S(2)}) collective-permute-start(bf16[256,896]{1,0:T(8,128)(2,1)S(1)} %collective-permute-done.24.refs_4_), channel_id=1, source_target_pairs={{0,8},{2,6},{8,16},{10,2},{16,24},{18,10},{24,28},{26,18},{28,20},... | collective-permute-start | bytes 1376264 | tf_op jit(solution)/shard_map/ppermute | solution.py:135
  101.2 15.5 %collective-permute-start.27 = (bf16[256,896]{1,0:T(8,128)(2,1)S(1)}, bf16[256,896]{1,0:T(8,128)(2,1)S(1)}, u32[]{:S(2)}, u32[]{:S(2)}) collective-permute-start(bf16[256,896]{1,0:T(8,128)(2,1)S(1)} %collective-permute-done.24.refs_4_), channel_id=1, source_target_pairs={{0,2},{2,0},{4,6},{6,4},{8,10},{10,8},{12,14},{14,12},{16,18},{18,... | collective-permute-start | bytes 1376264 | tf_op jit(solution)/shard_map/ppermute | solution.py:135
  101.2 15.5 %collective-permute-start.26 = (bf16[256,896]{1,0:T(8,128)(2,1)S(1)}, bf16[256,896]{1,0:T(8,128)(2,1)S(1)}, u32[]{:S(2)}, u32[]{:S(2)}) collective-permute-start(bf16[256,896]{1,0:T(8,128)(2,1)S(1)} %collective-permute-done.19.refs_3_), channel_id=1, source_target_pairs={{0,2},{2,0},{4,6},{6,4},{8,10},{10,8},{12,14},{14,12},{16,18},{18,... | collective-permute-start | bytes 1376264 | tf_op jit(solution)/shard_map/ppermute | solution.py:135
  105.0 14.1 %collective-permute-start.25 = (bf16[256,896]{1,0:T(8,128)(2,1)S(1)}, bf16[256,896]{1,0:T(8,128)(2,1)S(1)}, u32[]{:S(2)}, u32[]{:S(2)}) collective-permute-start(bf16[256,896]{1,0:T(8,128)(2,1)S(1)} %collective-permute-done.21.refs_3_), channel_id=1, source_target_pairs={{0,8},{2,6},{8,16},{10,2},{16,24},{18,10},{24,28},{26,18},{28,20},... | collective-permute-start | bytes 1376264 | tf_op jit(solution)/shard_map/ppermute | solution.py:135
  109.9 10.7 %collective-permute-start.32 = (bf16[256,896]{1,0:T(8,128)(2,1)S(1)}, bf16[256,896]{1,0:T(8,128)(2,1)S(1)}, u32[]{:S(2)}, u32[]{:S(2)}) collective-permute-start(bf16[256,896]{1,0:T(8,128)(2,1)S(1)} %collective-permute-done.28.refs_4_), channel_id=1, source_target_pairs={{0,8},{2,6},{8,16},{10,2},{16,24},{18,10},{24,28},{26,18},{28,20},... | collective-permute-start | bytes 1376264 | tf_op jit(solution)/shard_map/ppermute | solution.py:135
  116.6 11.1 %collective-permute-start.31 = (bf16[256,896]{1,0:T(8,128)(2,1)S(1)}, bf16[256,896]{1,0:T(8,128)(2,1)S(1)}, u32[]{:S(2)}, u32[]{:S(2)}) collective-permute-start(bf16[256,896]{1,0:T(8,128)(2,1)S(1)} %collective-permute-done.28.refs_4_), channel_id=1, source_target_pairs={{0,2},{2,0},{4,6},{6,4},{8,10},{10,8},{12,14},{14,12},{16,18},{18,... | collective-permute-start | bytes 1376264 | tf_op jit(solution)/shard_map/ppermute | solution.py:135
  116.7 11.5 %collective-permute-start.30 = (bf16[256,896]{1,0:T(8,128)(2,1)S(1)}, bf16[256,896]{1,0:T(8,128)(2,1)S(1)}, u32[]{:S(2)}, u32[]{:S(2)}) collective-permute-start(bf16[256,896]{1,0:T(8,128)(2,1)S(1)} %collective-permute-done.21.refs_3_), channel_id=1, source_target_pairs={{0,2},{2,0},{4,6},{6,4},{8,10},{10,8},{12,14},{14,12},{16,18},{18,... | collective-permute-start | bytes 1376264 | tf_op jit(solution)/shard_map/ppermute | solution.py:135
  119.0 11.0 %collective-permute-start.29 = (bf16[256,896]{1,0:T(8,128)(2,1)S(1)}, bf16[256,896]{1,0:T(8,128)(2,1)S(1)}, u32[]{:S(2)}, u32[]{:S(2)}) collective-permute-start(bf16[256,896]{1,0:T(8,128)(2,1)S(1)} %collective-permute-done.25.refs_3_), channel_id=1, source_target_pairs={{0,8},{2,6},{8,16},{10,2},{16,24},{18,10},{24,28},{26,18},{28,20},... | collective-permute-start | bytes 1376264 | tf_op jit(solution)/shard_map/ppermute | solution.py:135
  120.6 11.9 %collective-permute-start.37 = (bf16[256,896]{1,0:T(8,128)(2,1)S(1)}, bf16[256,896]{1,0:T(8,128)(2,1)S(1)}, u32[]{:S(2)}, u32[]{:S(2)}) collective-permute-start(bf16[256,896]{1,0:T(8,128)(2,1)S(1)} %collective-permute-done.32.refs_4_), channel_id=1, source_target_pairs={{0,8},{2,6},{8,16},{10,2},{16,24},{18,10},{24,28},{26,18},{28,20},... | collective-permute-start | bytes 1376264 | tf_op jit(solution)/shard_map/ppermute | solution.py:135
  132.5 11.0 %collective-permute-start.41 = (bf16[256,896]{1,0:T(8,128)(2,1)S(1)}, bf16[256,896]{1,0:T(8,128)(2,1)S(1)}, u32[]{:S(2)}, u32[]{:S(2)}) collective-permute-start(bf16[256,896]{1,0:T(8,128)(2,1)S(1)} %collective-permute-done.37.refs_4_), channel_id=1, source_target_pairs={{0,8},{2,6},{8,16},{10,2},{16,24},{18,10},{24,28},{26,18},{28,20},... | collective-permute-start | bytes 1376264 | tf_op jit(solution)/shard_map/ppermute | solution.py:135
  134.0 10.2 %collective-permute-start.40 = (bf16[256,896]{1,0:T(8,128)(2,1)S(1)}, bf16[256,896]{1,0:T(8,128)(2,1)S(1)}, u32[]{:S(2)}, u32[]{:S(2)}) collective-permute-start(bf16[256,896]{1,0:T(8,128)(2,1)S(1)} %collective-permute-done.37.refs_4_), channel_id=1, source_target_pairs={{0,2},{2,0},{4,6},{6,4},{8,10},{10,8},{12,14},{14,12},{16,18},{18,... | collective-permute-start | bytes 1376264 | tf_op jit(solution)/shard_map/ppermute | solution.py:135
  134.0 15.7 %collective-permute-start.39 = (bf16[256,896]{1,0:T(8,128)(2,1)S(1)}, bf16[256,896]{1,0:T(8,128)(2,1)S(1)}, u32[]{:S(2)}, u32[]{:S(2)}) collective-permute-start(bf16[256,896]{1,0:T(8,128)(2,1)S(1)} %collective-permute-done.29.refs_3_), channel_id=1, source_target_pairs={{0,2},{2,0},{4,6},{6,4},{8,10},{10,8},{12,14},{14,12},{16,18},{18,... | collective-permute-start | bytes 1376264 | tf_op jit(solution)/shard_map/ppermute | solution.py:135
  138.6 12.9 %collective-permute-start.38 = (bf16[256,896]{1,0:T(8,128)(2,1)S(1)}, bf16[256,896]{1,0:T(8,128)(2,1)S(1)}, u32[]{:S(2)}, u32[]{:S(2)}) collective-permute-start(bf16[256,896]{1,0:T(8,128)(2,1)S(1)} %collective-permute-done.34.refs_3_), channel_id=1, source_target_pairs={{0,8},{2,6},{8,16},{10,2},{16,24},{18,10},{24,28},{26,18},{28,20},... | collective-permute-start | bytes 1376264 | tf_op jit(solution)/shard_map/ppermute | solution.py:135
  143.5 9.8 %collective-permute-start.46 = (bf16[256,896]{1,0:T(8,128)(2,1)S(1)}, bf16[256,896]{1,0:T(8,128)(2,1)S(1)}, u32[]{:S(2)}, u32[]{:S(2)}) collective-permute-start(bf16[256,896]{1,0:T(8,128)(2,1)S(1)} %collective-permute-done.41.refs_4_), channel_id=1, source_target_pairs={{0,8},{2,6},{8,16},{10,2},{16,24},{18,10},{24,28},{26,18},{28,20},... | collective-permute-start | bytes 1376264 | tf_op jit(solution)/shard_map/ppermute | solution.py:135
  144.2 17.5 %collective-permute-start.45 = (bf16[256,896]{1,0:T(8,128)(2,1)S(1)}, bf16[256,896]{1,0:T(8,128)(2,1)S(1)}, u32[]{:S(2)}, u32[]{:S(2)}) collective-permute-start(bf16[256,896]{1,0:T(8,128)(2,1)S(1)} %collective-permute-done.41.refs_4_), channel_id=1, source_target_pairs={{0,2},{2,0},{4,6},{6,4},{8,10},{10,8},{12,14},{14,12},{16,18},{18,... | collective-permute-start | bytes 1376264 | tf_op jit(solution)/shard_map/ppermute | solution.py:135
  144.2 17.5 %collective-permute-start.44 = (bf16[256,896]{1,0:T(8,128)(2,1)S(1)}, bf16[256,896]{1,0:T(8,128)(2,1)S(1)}, u32[]{:S(2)}, u32[]{:S(2)}) collective-permute-start(bf16[256,896]{1,0:T(8,128)(2,1)S(1)} %collective-permute-done.34.refs_3_), channel_id=1, source_target_pairs={{0,2},{2,0},{4,6},{6,4},{8,10},{10,8},{12,14},{14,12},{16,18},{18,... | collective-permute-start | bytes 1376264 | tf_op jit(solution)/shard_map/ppermute | solution.py:135
  151.5 14.2 %collective-permute-start.42 = (bf16[256,896]{1,0:T(8,128)(2,1)S(1)}, bf16[256,896]{1,0:T(8,128)(2,1)S(1)}, u32[]{:S(2)}, u32[]{:S(2)}) collective-permute-start(bf16[256,896]{1,0:T(8,128)(2,1)S(1)} %collective-permute-done.38.refs_3_), channel_id=1, source_target_pairs={{0,8},{2,6},{8,16},{10,2},{16,24},{18,10},{24,28},{26,18},{28,20},... | collective-permute-start | bytes 1376264 | tf_op jit(solution)/shard_map/ppermute | solution.py:135
  153.3 12.4 %collective-permute-start.48 = (bf16[256,896]{1,0:T(8,128)(2,1)S(1)}, bf16[256,896]{1,0:T(8,128)(2,1)S(1)}, u32[]{:S(2)}, u32[]{:S(2)}) collective-permute-start(bf16[256,896]{1,0:T(8,128)(2,1)S(1)} %collective-permute-done.46.refs_4_), channel_id=1, source_target_pairs={{0,8},{2,6},{8,16},{10,2},{16,24},{18,10},{24,28},{26,18},{28,20},... | collective-permute-start | bytes 1376264 | tf_op jit(solution)/shard_map/ppermute | solution.py:135
  154.0 10.4 %collective-permute-start.43 = (bf16[384,512]{1,0:T(8,128)(2,1)S(1)}, bf16[384,512]{1,0:T(8,128)(2,1)S(1)}, u32[]{:S(2)}, u32[]{:S(2)}) collective-permute-start(bf16[384,512]{1,0:T(8,128)(2,1)S(1)} %get-tuple-element.198), channel_id=1, source_target_pairs={{0,1},{1,0},{2,3},{3,2},{4,5},{5,4},{6,7},{7,6},{8,9},{9,8},{10,11... | collective-permute-start | bytes 1179656 | tf_op jit(solution)/shard_map/ppermute | solution.py:275
  (24 other events, 210.3 us)

commit v5 on v4

--- a/solution.py
+++ b/solution.py
@@ -318,12 +318,13 @@
     def result(self, kind):
         return jax.ShapeDtypeStruct((self.count, self.width), kind)
 
-    def multiply_keys(self, values, kind):
-        own, others, weights = self.specs()
+    def multiply_keys(self, values, kind, half=None):
+        steps = self.steps if half is None else self.steps // 2
+        own, others, weights = self.specs(steps * (half or 0))
         return self.call(
             keys_kernel, "keys", self.result(kind), ([own] if len(values) == 1 else others) + [weights],
             pl.BlockSpec((self.count, self.width), lambda i, where: (0, 0)),
-            [pltpu.VMEM((self.count, self.width), f32)], self.steps, *values, in_place(self.weight),
+            [pltpu.VMEM((self.count, self.width), f32)], steps, *values, in_place(self.weight),
         )
 
     def own_term(self, second):
@@ -370,12 +371,14 @@
 
         rows = pl.BlockSpec((self.count // 2, self.width), lambda i, where: (i, 0))
         self.keys = self.call(
-            kernel, "finish_keys", self.result(bf16), [rows] * (1 + len(self.came)), rows, [], 2, self.keys, *self.came
+            kernel, "finish_keys", self.result(bf16), [rows] * (2 + len(self.came)), rows, [], 2, self.keys, self.second_keys, *self.came
         )
 
     def late(self, k):
         if k == 1:
-            self.keys = self.multiply_keys([in_place(self.tokens)], f32)
+            self.keys = self.multiply_keys([in_place(self.tokens)], f32, 0)
+        if k == 3:
+            self.second_keys = self.multiply_keys([in_place(self.tokens)], f32, 1)
         if k == 2:
             others = [
                 self.multiply_keys([in_place(value) for value in pair], bf16) for pair in zip(self.first, self.second)

time: 171 us -> 170 us (level)
  waiting for transfers between devices: 38.5 us -> 34.1 us
  starting transfers between devices: 51.9 us -> 54.8 us
    ppermute x49, waiting for transfers between devices: 38.2 us -> 34.1 us  [send(): return lax.ppermute(x, 'replica', perm)]
    ppermute x49, starting transfers between devices: 44.5 us -> 47.4 us  [send(): return lax.ppermute(x, 'replica', perm)]
    pallas_call x18 -> x19, Pallas kernels: 50.5 us -> 51.7 us  [call(): pl.pallas_call(body, **params)]
  transfers between devices with their start and end apart: 52 -> 52, of which waited for: 22 -> 20; matrix products, arithmetic and copies ran while one was open for 15% -> 15% of each run, Pallas kernels for 29% -> 30%
where the time goes in v5:
time: 170 us
  starting transfers between devices  54.8 us (32%)
  Pallas kernels  51.7 us (30%)
  waiting for transfers between devices  34.1 us (20%)
  other arithmetic  25.2 us (15%)
  local copies, waits for them, and re-layouts  2.46 us (1%)
    pallas_call x19, Pallas kernels, call(): pl.pallas_call(body, **params)  51.7 us
    ppermute x49, starting transfers between devices, send(): return lax.ppermute(x, 'replica', perm)  47.4 us
    ppermute x49, waiting for transfers between devices, send(): return lax.ppermute(x, 'replica', perm)  34.1 us
    convert_element_type x14, other arithmetic, outer_step(): out = total.astype(bf16)  18.8 us
    ppermute x2, starting transfers between devices, shift(): return lax.ppermute(x, ('replica', 'fsdp'), pairs)  5.89 us
    convert_element_type x2, other arithmetic, outer_step(): (weights - outer_rate * (pseudo_grad + momentum_decay * momentum_new)).as...  4.88 us
  transfers between devices with their start and end apart: 52, of which 20 were waited for; matrix products, arithmetic and copies ran while one was open for 15% of the time, Pallas kernels for 30%

profile of v5, /device:TPU:0, one launch (start us, length us, event | category | flops | bytes accessed | tf_op | source)
XLA Modules:
  0.0 169.6 jit_solution(8079857050917820322)
XLA Ops:
  0.8 2.4 %dynamic-slice_bitcast_fusion = (bf16[256,896]{1,0:T(8,128)(2,1)S(1)}, bf16[256,896]{1,0:T(8,128)(2,1)S(1)}, bf16[256,896]{1,0:T(8,128)(2,1)}, bf16[256,896]{1,0:T(8,128)(2,1)S(1)}) fusion(bf16[2,8,2,256,896]{4,3,2,1,0:T(8,128)(2,1)} %bitcast.130, s32[]{:T(128)S(6)} %select_n.248, s32[]{:T(128)S(6)} %select_n.242, s32[]{:T(128)S(6)} %select_n.241), kind=kLoop, calls=%fused_computation.43 | loop fusion | bytes 3670028 | tf_op jit(solution)/shard_map/reshape | solution.py:146
  7.4 2.7 %collective-permute-start.5 = (bf16[256,896]{1,0:T(8,128)(2,1)S(1)}, bf16[256,896]{1,0:T(8,128)(2,1)S(1)}, u32[]{:S(2)}, u32[]{:S(2)}) collective-permute-start(bf16[256,896]{1,0:T(8,128)(2,1)S(1)} %fusion.7), channel_id=1, source_target_pairs={{0,8},{2,6},{8,16},{10,2},{16,24},{18,10},{24,28},{26,18},{28,20},... | collective-permute-start | bytes 1376264 | tf_op jit(solution)/shard_map/ppermute | solution.py:135
  12.9 3.8 %columns.1 = (f32[8,128]{1,0:T(8,128)S(1)}, bf16[384,4608]{1,0:T(8,128)(2,1)}) custom-call(s32[1]{0:T(128)} %bitcast.9.refs_0_, bf16[384,8192]{1,0:T(8,128)(2,1)} %refs_1_.9, bf16[384,512]{1,0:T(8,128)(2,1)} %refs_2_.5, bf16[256,896]{1,0:T(8,128)(2,1)S(1)} %fusion.2.refs_3_), custom_call_target="tpu_custom_call" | custom-call | tf_op jit(solution)/shard_map/columns/pallas_call | solution.py:73
  16.6 3.4 %collective-permute-start.16 = (bf16[384,4608]{1,0:T(8,128)(2,1)}, bf16[384,4608]{1,0:T(8,128)(2,1)}, u32[]{:S(2)}, u32[]{:S(2)}) collective-permute-start(bf16[384,4608]{1,0:T(8,128)(2,1)} %get-tuple-element.152), channel_id=1, source_target_pairs={{0,1},{1,0},{4,5},{5,4},{8,9},{9,8},{12,13},{13,12},{16,17},{17,16... | collective-permute-start | bytes 10616840 | tf_op jit(solution)/shard_map/ppermute | solution.py:281
  25.6 3.9 %collective-permute-done.4.refs_0_ = bf16[2,8,2,256,896]{4,3,2,1,0:T(8,128)(2,1)} collective-permute-done((bf16[2,8,2,256,896]{4,3,2,1,0:T(8,128)(2,1)}, bf16[2,8,2,256,896]{4,3,2,1,0:T(8,128)(2,1)}, u32[]{:S(2)}, u32[]{:S(2)}) %collective-permute-start.4) | collective-permute-done | bytes 14680096 | tf_op jit(solution)/shard_map/ppermute | solution.py:135
  31.1 2.7 %collective-permute-start.9 = (bf16[256,896]{1,0:T(8,128)(2,1)S(1)}, bf16[256,896]{1,0:T(8,128)(2,1)S(1)}, u32[]{:S(2)}, u32[]{:S(2)}) collective-permute-start(bf16[256,896]{1,0:T(8,128)(2,1)S(1)} %fusion.19), channel_id=1, source_target_pairs={{0,8},{2,6},{8,16},{10,2},{16,24},{18,10},{24,28},{26,18},{28,20},... | collective-permute-start | bytes 1376264 | tf_op jit(solution)/shard_map/ppermute | solution.py:135
  37.7 4.3 %own_term.2 = (f32[8,128]{1,0:T(8,128)S(1)}, bf16[2048,512]{1,0:T(8,128)(2,1)}) custom-call(s32[2]{0:T(128)S(1)} %pad_add_fusion.refs_0_, bf16[384,8192]{1,0:T(8,128)(2,1)} %refs_1_.9, bf16[384,512]{1,0:T(8,128)(2,1)} %refs_2_.5, bf16[256,896]{1,0:T(8,128)(2,1)S(1)} %fusion.18.refs_3_, f32[8,128]{1,0:T(8,128)S(1)} %get-tuple-element.133.refs_4_), custom_call_target="tpu_custom_call" | custom-call | tf_op jit(solution)/shard_map/own_term/pallas_call | solution.py:73
  46.7 2.1 %collective-permute-start.12 = (bf16[256,896]{1,0:T(8,128)(2,1)S(1)}, bf16[256,896]{1,0:T(8,128)(2,1)S(1)}, u32[]{:S(2)}, u32[]{:S(2)}) collective-permute-start(bf16[256,896]{1,0:T(8,128)(2,1)S(1)} %fusion.16), channel_id=1, source_target_pairs={{0,8},{2,6},{8,16},{10,2},{16,24},{18,10},{24,28},{26,18},{28,20},... | collective-permute-start | bytes 1376264 | tf_op jit(solution)/shard_map/ppermute | solution.py:135
  48.9 3.0 %collective-permute-done.11 = bf16[256,896]{1,0:T(8,128)(2,1)S(1)} collective-permute-done((bf16[256,896]{1,0:T(8,128)(2,1)S(1)}, bf16[256,896]{1,0:T(8,128)(2,1)S(1)}, u32[]{:S(2)}, u32[]{:S(2)}) %collective-permute-start.11) | collective-permute-done | bytes 458784 | tf_op jit(solution)/shard_map/ppermute | solution.py:135
  54.8 2.0 %collective-permute-done.12 = bf16[256,896]{1,0:T(8,128)(2,1)S(1)} collective-permute-done((bf16[256,896]{1,0:T(8,128)(2,1)S(1)}, bf16[256,896]{1,0:T(8,128)(2,1)S(1)}, u32[]{:S(2)}, u32[]{:S(2)}) %collective-permute-start.12) | collective-permute-done | bytes 458784 | tf_op jit(solution)/shard_map/ppermute | solution.py:135
  59.7 2.0 %collective-permute-done.13 = bf16[256,896]{1,0:T(8,128)(2,1)S(1)} collective-permute-done((bf16[256,896]{1,0:T(8,128)(2,1)S(1)}, bf16[256,896]{1,0:T(8,128)(2,1)S(1)}, u32[]{:S(2)}, u32[]{:S(2)}) %collective-permute-start.13) | collective-permute-done | bytes 458784 | tf_op jit(solution)/shard_map/ppermute | solution.py:135
  64.6 2.5 %collective-permute-start.33 = (bf16[384,4608]{1,0:T(8,128)(2,1)}, bf16[384,4608]{1,0:T(8,128)(2,1)}, u32[]{:S(2)}, u32[]{:S(2)}) collective-permute-start(bf16[384,4608]{1,0:T(8,128)(2,1)} %get-tuple-element.152), channel_id=1, source_target_pairs={{2,3},{3,2},{6,7},{7,6},{10,11},{11,10},{14,15},{15,14},{18,19},{1... | collective-permute-start | bytes 10616840 | tf_op jit(solution)/shard_map/ppermute | solution.py:281
  69.6 4.3 %own_term.3 = (f32[8,128]{1,0:T(8,128)S(1)}, bf16[2048,512]{1,0:T(8,128)(2,1)}) custom-call(s32[2]{0:T(128)S(1)} %pad_add_fusion.refs_0_, bf16[384,8192]{1,0:T(8,128)(2,1)} %refs_1_.9, bf16[384,512]{1,0:T(8,128)(2,1)} %refs_2_.5, bf16[256,896]{1,0:T(8,128)(2,1)S(1)} %fusion.12.refs_3_, f32[8,128]{1,0:T(8,128)S(1)} %get-tuple-element.148.refs_4_), custom_call_target="tpu_custom_call" | custom-call | tf_op jit(solution)/shard_map/own_term/pallas_call | solution.py:73
  77.0 2.1 %fusion.10 = bf16[256,896]{1,0:T(8,128)(2,1)} fusion(bf16[256,896]{1,0:T(8,128)(2,1)S(1)} %collective-permute-done.17, bf16[2,8,2,256,896]{4,3,2,1,0:T(8,128)(2,1)} %get-tuple-element.158, s32[]{:T(128)S(6)} %select_n.241, s32[]{:T(128)S(6)} %select_n.239, bf16[2,8,2,256,896]{4,3,2,1,0:T(8,128)(2,1)} %bitcast.145), kind=kLoop, calls=%fused_computation.24 | loop fusion | flops 1376256 | bytes 1835016 | tf_op jit(solution)/shard_map/convert_element_type | solution.py:163
  80.1 3.6 %collective-permute-done.18 = bf16[256,896]{1,0:T(8,128)(2,1)S(1)} collective-permute-done((bf16[256,896]{1,0:T(8,128)(2,1)S(1)}, bf16[256,896]{1,0:T(8,128)(2,1)S(1)}, u32[]{:S(2)}, u32[]{:S(2)}) %collective-permute-start.18) | collective-permute-done | bytes 458784 | tf_op jit(solution)/shard_map/ppermute | solution.py:135
  83.7 1.9 %fusion = (bf16[256,896]{1,0:T(8,128)(2,1)S(1)}, f32[256,896]{1,0:T(8,128)S(1)}) fusion(bf16[256,896]{1,0:T(8,128)(2,1)S(1)} %collective-permute-done.18, bf16[2,1,256,896]{3,2,1,0:T(8,128)(2,1)S(1)} %copy-done.3, bf16[2,8,2,256,896]{4,3,2,1,0:T(8,128)(2,1)} %get-tuple-element.158, s32[]{:T(128)S(6)} %select_n.268, s32[]{:T(128)S(6)} %select_n.239, ...), kind=kLoop, calls=%fused_computation.5 | loop fusion | flops 3440640 | bytes 4128776 | tf_op jit(solution)/shard_map/convert_element_type | solution.py:190
  86.8 1.8 %collective-permute-done.20 = bf16[256,896]{1,0:T(8,128)(2,1)S(1)} collective-permute-done((bf16[256,896]{1,0:T(8,128)(2,1)}, bf16[256,896]{1,0:T(8,128)(2,1)S(1)}, u32[]{:S(2)}, u32[]{:S(2)}) %collective-permute-start.20) | collective-permute-done | bytes 458784 | tf_op jit(solution)/shard_map/ppermute | solution.py:135
  88.6 3.0 %fusion.1 = (bf16[256,896]{1,0:T(8,128)(2,1)S(1)}, f32[256,896]{1,0:T(8,128)}) fusion(bf16[256,896]{1,0:T(8,128)(2,1)S(1)} %collective-permute-done.20, bf16[2,1,256,896]{3,2,1,0:T(8,128)(2,1)} %param.10, bf16[2,8,2,256,896]{4,3,2,1,0:T(8,128)(2,1)} %get-tuple-element.158, s32[]{:T(128)S(6)} %select_n.268, s32[]{:T(128)S(6)} %select_n.239, ...), kind=kLoop, calls=%fused_computation.6 | loop fusion | flops 3440640 | bytes 4128776 | tf_op jit(solution)/shard_map/convert_element_type | solution.py:190
  96.4 3.6 %collective-permute-done.24.refs_4_ = bf16[256,896]{1,0:T(8,128)(2,1)S(1)} collective-permute-done((bf16[256,896]{1,0:T(8,128)(2,1)S(1)}, bf16[256,896]{1,0:T(8,128)(2,1)S(1)}, u32[]{:S(2)}, u32[]{:S(2)}) %collective-permute-start.24) | collective-permute-done | bytes 458784 | tf_op jit(solution)/shard_map/ppermute | solution.py:135
  101.7 1.8 %place.10 = (f32[8,128]{1,0:T(8,128)S(1)}, bf16[2,16,256,896]{3,2,1,0:T(8,128)(2,1)}) custom-call(s32[16]{0:T(128)S(1)} %stack.88.refs_0_, bf16[256,896]{1,0:T(8,128)(2,1)S(1)} %collective-permute-done.22.refs_1_, bf16[256,896]{1,0:T(8,128)(2,1)S(1)} %collective-permute-done.23.refs_2_, ...), custom_call_target="tpu_custom_call", output_to_operand_aliasing={{1}: (5, {})} | custom-call | tf_op jit(solution)/shard_map/place/pallas_call | solution.py:73
  106.1 3.8 %collective-permute-done.28.refs_4_ = bf16[256,896]{1,0:T(8,128)(2,1)S(1)} collective-permute-done((bf16[256,896]{1,0:T(8,128)(2,1)S(1)}, bf16[256,896]{1,0:T(8,128)(2,1)S(1)}, u32[]{:S(2)}, u32[]{:S(2)}) %collective-permute-start.28) | collective-permute-done | bytes 458784 | tf_op jit(solution)/shard_map/ppermute | solution.py:135
  111.0 3.4 %keys.3 = (f32[8,128]{1,0:T(8,128)S(1)}, f32[384,512]{1,0:T(8,128)S(1)}) custom-call(s32[2]{0:T(128)S(1)} %pad_add_fusion.refs_0_, bf16[384,8192]{1,0:T(8,128)(2,1)} %refs_1_.9, bf16[4096,512]{1,0:T(8,128)(2,1)} %bitcast.127, f32[8,128]{1,0:T(8,128)S(1)} %get-tuple-element.173.refs_3_), custom_call_target="tpu_custom_call" | custom-call | tf_op jit(solution)/shard_map/keys/pallas_call | solution.py:73
  115.0 1.8 %place.11 = (f32[8,128]{1,0:T(8,128)S(1)}, bf16[2,16,256,896]{3,2,1,0:T(8,128)(2,1)}) custom-call(s32[16]{0:T(128)S(1)} %stack.88.refs_0_, bf16[256,896]{1,0:T(8,128)(2,1)S(1)} %collective-permute-done.26.refs_1_, bf16[256,896]{1,0:T(8,128)(2,1)S(1)} %collective-permute-done.27.refs_2_, ...), custom_call_target="tpu_custom_call", output_to_operand_aliasing={{1}: (5, {})} | custom-call | tf_op jit(solution)/shard_map/place/pallas_call | solution.py:73
  120.8 5.9 %keys.4 = (f32[8,128]{1,0:T(8,128)S(1)}, bf16[384,512]{1,0:T(8,128)(2,1)S(1)}) custom-call(s32[2]{0:T(128)S(1)} %pad_add_fusion.refs_0_, bf16[384,4608]{1,0:T(8,128)(2,1)} %collective-permute-done.16.refs_1_.refs_2_.refs_4_, bf16[384,4608]{1,0:T(8,128)(2,1)} %collective-permute-done.33.refs_2_.refs_3_.refs_5_, bf16[4096,512]{1,0:T(8,128)(2,1)} %bitcast.128, ...), custom_call_target="tpu_custom_call" | custom-call | tf_op jit(solution)/shard_map/keys/pallas_call | solution.py:73
  127.4 1.8 %place.12 = (f32[8,128]{1,0:T(8,128)S(1)}, bf16[2,16,256,896]{3,2,1,0:T(8,128)(2,1)}) custom-call(s32[16]{0:T(128)S(1)} %stack.88.refs_0_, bf16[256,896]{1,0:T(8,128)(2,1)S(1)} %collective-permute-done.30.refs_1_, bf16[256,896]{1,0:T(8,128)(2,1)S(1)} %collective-permute-done.31.refs_2_, ...), custom_call_target="tpu_custom_call", output_to_operand_aliasing={{1}: (5, {})} | custom-call | tf_op jit(solution)/shard_map/place/pallas_call | solution.py:73
  131.9 3.4 %keys.5 = (f32[8,128]{1,0:T(8,128)S(1)}, f32[384,512]{1,0:T(8,128)S(1)}) custom-call(s32[2]{0:T(128)S(1)} %pad_add_fusion.refs_0_, bf16[384,8192]{1,0:T(8,128)(2,1)} %refs_1_.9, bf16[4096,512]{1,0:T(8,128)(2,1)} %bitcast.129, f32[8,128]{1,0:T(8,128)S(1)} %get-tuple-element.188.refs_3_), custom_call_target="tpu_custom_call" | custom-call | tf_op jit(solution)/shard_map/keys/pallas_call | solution.py:73
  135.8 1.8 %place.13 = (f32[8,128]{1,0:T(8,128)S(1)}, bf16[2,16,256,896]{3,2,1,0:T(8,128)(2,1)}) custom-call(s32[16]{0:T(128)S(1)} %stack.88.refs_0_, bf16[256,896]{1,0:T(8,128)(2,1)S(1)} %collective-permute-done.35.refs_1_, bf16[256,896]{1,0:T(8,128)(2,1)S(1)} %collective-permute-done.36.refs_2_, ...), custom_call_target="tpu_custom_call", output_to_operand_aliasing={{1}: (5, {})} | custom-call | tf_op jit(solution)/shard_map/place/pallas_call | solution.py:73
  139.3 3.4 %collective-permute-done.41.refs_4_ = bf16[256,896]{1,0:T(8,128)(2,1)S(1)} collective-permute-done((bf16[256,896]{1,0:T(8,128)(2,1)S(1)}, bf16[256,896]{1,0:T(8,128)(2,1)S(1)}, u32[]{:S(2)}, u32[]{:S(2)}) %collective-permute-start.41) | collective-permute-done | bytes 458784 | tf_op jit(solution)/shard_map/ppermute | solution.py:135
  144.7 5.0 %grad.2 = (f32[8,128]{1,0:T(8,128)S(1)}, bf16[4096,512]{1,0:T(8,128)(2,1)}) custom-call(s32[2]{0:T(128)S(1)} %pad_add_fusion.refs_0_, bf16[2048,512]{1,0:T(8,128)(2,1)S(1)} %copy-done.1, bf16[384,4608]{1,0:T(8,128)(2,1)} %collective-permute-done.16.refs_1_.refs_2_.refs_4_, bf16[384,4608]{1,0:T(8,128)(2,1)} %collective-permute-done.33.refs_2_.refs_3_.refs_5_, ...), custom_call_target="tpu_custom_call" | custom-call | tf_op jit(solution)/shard_map/grad/pallas_call | solution.py:73
  149.7 1.8 %place.14 = (f32[8,128]{1,0:T(8,128)S(1)}, bf16[2,16,256,896]{3,2,1,0:T(8,128)(2,1)}) custom-call(s32[16]{0:T(128)S(1)} %stack.88.refs_0_, bf16[256,896]{1,0:T(8,128)(2,1)S(1)} %collective-permute-done.39.refs_1_, bf16[256,896]{1,0:T(8,128)(2,1)S(1)} %collective-permute-done.40.refs_2_, ...), custom_call_target="tpu_custom_call", output_to_operand_aliasing={{1}: (5, {})} | custom-call | tf_op jit(solution)/shard_map/place/pallas_call | solution.py:73
  157.0 4.8 %grad.3 = (f32[8,128]{1,0:T(8,128)S(1)}, bf16[4096,512]{1,0:T(8,128)(2,1)}) custom-call(s32[2]{0:T(128)S(1)} %pad_add_fusion.refs_0_, bf16[2048,512]{1,0:T(8,128)(2,1)S(1)} %copy-done, bf16[384,4608]{1,0:T(8,128)(2,1)} %collective-permute-done.16.refs_1_.refs_2_.refs_4_, ...), custom_call_target="tpu_custom_call", output_to_operand_aliasing={{1}: (6, {})} | custom-call | tf_op jit(solution)/shard_map/grad/pallas_call | solution.py:73
  166.0 1.8 %place.16 = (f32[8,128]{1,0:T(8,128)S(1)}, bf16[2,16,256,896]{3,2,1,0:T(8,128)(2,1)}) custom-call(s32[16]{0:T(128)S(1)} %stack.88.refs_0_, bf16[256,896]{1,0:T(8,128)(2,1)S(1)} %collective-permute-done.50.refs_1_, bf16[256,896]{1,0:T(8,128)(2,1)S(1)} %collective-permute-done.51.refs_2_, ...), custom_call_target="tpu_custom_call", output_to_operand_aliasing={{1}: (5, {})} | custom-call | tf_op jit(solution)/shard_map/place/pallas_call | solution.py:73
  (119 shorter events, 72.7 us)
Async XLA Ops:
  7.0 22.5 %collective-permute-start.4 = (bf16[2,8,2,256,896]{4,3,2,1,0:T(8,128)(2,1)}, bf16[2,8,2,256,896]{4,3,2,1,0:T(8,128)(2,1)}, u32[]{:S(2)}, u32[]{:S(2)}) collective-permute-start(bf16[2,8,2,256,896]{4,3,2,1,0:T(8,128)(2,1)} %bitcast.132), channel_id=1, source_target_pairs={{0,2},{2,0},{4,6},{6,4},{8,10},{10,8},{12,14},{14,12},{16,18},{18,... | collective-permute-start | bytes 44040200 | tf_op jit(solution)/shard_map/ppermute | solution.py:135
  7.4 12.6 %collective-permute-start.5 = (bf16[256,896]{1,0:T(8,128)(2,1)S(1)}, bf16[256,896]{1,0:T(8,128)(2,1)S(1)}, u32[]{:S(2)}, u32[]{:S(2)}) collective-permute-start(bf16[256,896]{1,0:T(8,128)(2,1)S(1)} %fusion.7), channel_id=1, source_target_pairs={{0,8},{2,6},{8,16},{10,2},{16,24},{18,10},{24,28},{26,18},{28,20},... | collective-permute-start | bytes 1376264 | tf_op jit(solution)/shard_map/ppermute | solution.py:135
  11.2 11.6 %collective-permute-start.6 = (bf16[256,896]{1,0:T(8,128)(2,1)S(1)}, bf16[256,896]{1,0:T(8,128)(2,1)S(1)}, u32[]{:S(2)}, u32[]{:S(2)}) collective-permute-start(bf16[256,896]{1,0:T(8,128)(2,1)S(1)} %fusion.2.refs_3_), channel_id=1, source_target_pairs={{0,8},{2,6},{8,16},{10,2},{16,24},{18,10},{24,28},{26,18},{28,20},... | collective-permute-start | bytes 1376264 | tf_op jit(solution)/shard_map/ppermute | solution.py:135
  16.6 57.2 %collective-permute-start.16 = (bf16[384,4608]{1,0:T(8,128)(2,1)}, bf16[384,4608]{1,0:T(8,128)(2,1)}, u32[]{:S(2)}, u32[]{:S(2)}) collective-permute-start(bf16[384,4608]{1,0:T(8,128)(2,1)} %get-tuple-element.152), channel_id=1, source_target_pairs={{0,1},{1,0},{4,5},{5,4},{8,9},{9,8},{12,13},{13,12},{16,17},{17,16... | collective-permute-start | bytes 10616840 | tf_op jit(solution)/shard_map/ppermute | solution.py:281
  24.1 10.6 %collective-permute-start.8 = (bf16[256,896]{1,0:T(8,128)(2,1)S(1)}, bf16[256,896]{1,0:T(8,128)(2,1)S(1)}, u32[]{:S(2)}, u32[]{:S(2)}) collective-permute-start(bf16[256,896]{1,0:T(8,128)(2,1)S(1)} %fusion.6.refs_1_), channel_id=1, source_target_pairs={{0,8},{2,6},{8,16},{10,2},{16,24},{18,10},{24,28},{26,18},{28,20},... | collective-permute-start | bytes 1376264 | tf_op jit(solution)/shard_map/ppermute | solution.py:135
  31.1 10.9 %collective-permute-start.9 = (bf16[256,896]{1,0:T(8,128)(2,1)S(1)}, bf16[256,896]{1,0:T(8,128)(2,1)S(1)}, u32[]{:S(2)}, u32[]{:S(2)}) collective-permute-start(bf16[256,896]{1,0:T(8,128)(2,1)S(1)} %fusion.19), channel_id=1, source_target_pairs={{0,8},{2,6},{8,16},{10,2},{16,24},{18,10},{24,28},{26,18},{28,20},... | collective-permute-start | bytes 1376264 | tf_op jit(solution)/shard_map/ppermute | solution.py:135
  36.0 9.2 %collective-permute-start.10 = (bf16[256,896]{1,0:T(8,128)(2,1)S(1)}, bf16[256,896]{1,0:T(8,128)(2,1)}, u32[]{:S(2)}, u32[]{:S(2)}) collective-permute-start(bf16[256,896]{1,0:T(8,128)(2,1)S(1)} %fusion.18.refs_3_), channel_id=1, source_target_pairs={{0,8},{2,6},{8,16},{10,2},{16,24},{18,10},{24,28},{26,18},{28,20},... | collective-permute-start | bytes 1376264 | tf_op jit(solution)/shard_map/ppermute | solution.py:135
  46.7 10.1 %collective-permute-start.12 = (bf16[256,896]{1,0:T(8,128)(2,1)S(1)}, bf16[256,896]{1,0:T(8,128)(2,1)S(1)}, u32[]{:S(2)}, u32[]{:S(2)}) collective-permute-start(bf16[256,896]{1,0:T(8,128)(2,1)S(1)} %fusion.16), channel_id=1, source_target_pairs={{0,8},{2,6},{8,16},{10,2},{16,24},{18,10},{24,28},{26,18},{28,20},... | collective-permute-start | bytes 1376264 | tf_op jit(solution)/shard_map/ppermute | solution.py:135
  58.1 9.0 %collective-permute-start.14 = (bf16[256,896]{1,0:T(8,128)(2,1)S(1)}, bf16[256,896]{1,0:T(8,128)(2,1)S(1)}, u32[]{:S(2)}, u32[]{:S(2)}) collective-permute-start(bf16[256,896]{1,0:T(8,128)(2,1)S(1)} %fusion.14), channel_id=1, source_target_pairs={{0,8},{2,6},{8,16},{10,2},{16,24},{18,10},{24,28},{26,18},{28,20},... | collective-permute-start | bytes 1376264 | tf_op jit(solution)/shard_map/ppermute | solution.py:135
  63.1 10.8 %collective-permute-start.15 = (bf16[256,896]{1,0:T(8,128)(2,1)S(1)}, bf16[256,896]{1,0:T(8,128)(2,1)S(1)}, u32[]{:S(2)}, u32[]{:S(2)}) collective-permute-start(bf16[256,896]{1,0:T(8,128)(2,1)S(1)} %fusion.13), channel_id=1, source_target_pairs={{0,8},{2,6},{8,16},{10,2},{16,24},{18,10},{24,28},{26,18},{28,20},... | collective-permute-start | bytes 1376264 | tf_op jit(solution)/shard_map/ppermute | solution.py:135
  64.6 56.2 %collective-permute-start.33 = (bf16[384,4608]{1,0:T(8,128)(2,1)}, bf16[384,4608]{1,0:T(8,128)(2,1)}, u32[]{:S(2)}, u32[]{:S(2)}) collective-permute-start(bf16[384,4608]{1,0:T(8,128)(2,1)} %get-tuple-element.152), channel_id=1, source_target_pairs={{2,3},{3,2},{6,7},{7,6},{10,11},{11,10},{14,15},{15,14},{18,19},{1... | collective-permute-start | bytes 10616840 | tf_op jit(solution)/shard_map/ppermute | solution.py:281
  79.1 9.5 %collective-permute-start.20 = (bf16[256,896]{1,0:T(8,128)(2,1)}, bf16[256,896]{1,0:T(8,128)(2,1)S(1)}, u32[]{:S(2)}, u32[]{:S(2)}) collective-permute-start(bf16[256,896]{1,0:T(8,128)(2,1)} %fusion.10), channel_id=1, source_target_pairs={{0,8},{2,6},{8,16},{10,2},{16,24},{18,10},{24,28},{26,18},{28,20},... | collective-permute-start | bytes 1376264 | tf_op jit(solution)/shard_map/ppermute | solution.py:135
  85.6 9.2 %collective-permute-start.19 = (bf16[256,896]{1,0:T(8,128)(2,1)S(1)}, bf16[256,896]{1,0:T(8,128)(2,1)S(1)}, u32[]{:S(2)}, u32[]{:S(2)}) collective-permute-start(bf16[256,896]{1,0:T(8,128)(2,1)S(1)} %get-tuple-element.157.refs_1_), channel_id=1, source_target_pairs={{0,8},{2,6},{8,16},{10,2},{16,24},{18,10},{24,28},{26,18},{28,20},... | collective-permute-start | bytes 1376264 | tf_op jit(solution)/shard_map/ppermute | solution.py:135
  94.9 10.1 %collective-permute-start.21 = (bf16[256,896]{1,0:T(8,128)(2,1)S(1)}, bf16[256,896]{1,0:T(8,128)(2,1)S(1)}, u32[]{:S(2)}, u32[]{:S(2)}) collective-permute-start(bf16[256,896]{1,0:T(8,128)(2,1)S(1)} %collective-permute-done.19.refs_3_), channel_id=1, source_target_pairs={{0,8},{2,6},{8,16},{10,2},{16,24},{18,10},{24,28},{26,18},{28,20},... | collective-permute-start | bytes 1376264 | tf_op jit(solution)/shard_map/ppermute | solution.py:135
  100.1 9.8 %collective-permute-start.28 = (bf16[256,896]{1,0:T(8,128)(2,1)S(1)}, bf16[256,896]{1,0:T(8,128)(2,1)S(1)}, u32[]{:S(2)}, u32[]{:S(2)}) collective-permute-start(bf16[256,896]{1,0:T(8,128)(2,1)S(1)} %collective-permute-done.24.refs_4_), channel_id=1, source_target_pairs={{0,8},{2,6},{8,16},{10,2},{16,24},{18,10},{24,28},{26,18},{28,20},... | collective-permute-start | bytes 1376264 | tf_op jit(solution)/shard_map/ppermute | solution.py:135
  101.2 13.2 %collective-permute-start.27 = (bf16[256,896]{1,0:T(8,128)(2,1)S(1)}, bf16[256,896]{1,0:T(8,128)(2,1)S(1)}, u32[]{:S(2)}, u32[]{:S(2)}) collective-permute-start(bf16[256,896]{1,0:T(8,128)(2,1)S(1)} %collective-permute-done.24.refs_4_), channel_id=1, source_target_pairs={{0,2},{2,0},{4,6},{6,4},{8,10},{10,8},{12,14},{14,12},{16,18},{18,... | collective-permute-start | bytes 1376264 | tf_op jit(solution)/shard_map/ppermute | solution.py:135
  101.2 13.3 %collective-permute-start.26 = (bf16[256,896]{1,0:T(8,128)(2,1)S(1)}, bf16[256,896]{1,0:T(8,128)(2,1)S(1)}, u32[]{:S(2)}, u32[]{:S(2)}) collective-permute-start(bf16[256,896]{1,0:T(8,128)(2,1)S(1)} %collective-permute-done.19.refs_3_), channel_id=1, source_target_pairs={{0,2},{2,0},{4,6},{6,4},{8,10},{10,8},{12,14},{14,12},{16,18},{18,... | collective-permute-start | bytes 1376264 | tf_op jit(solution)/shard_map/ppermute | solution.py:135
  105.0 11.8 %collective-permute-start.25 = (bf16[256,896]{1,0:T(8,128)(2,1)S(1)}, bf16[256,896]{1,0:T(8,128)(2,1)S(1)}, u32[]{:S(2)}, u32[]{:S(2)}) collective-permute-start(bf16[256,896]{1,0:T(8,128)(2,1)S(1)} %collective-permute-done.21.refs_3_), channel_id=1, source_target_pairs={{0,8},{2,6},{8,16},{10,2},{16,24},{18,10},{24,28},{26,18},{28,20},... | collective-permute-start | bytes 1376264 | tf_op jit(solution)/shard_map/ppermute | solution.py:135
  109.9 9.8 %collective-permute-start.32 = (bf16[256,896]{1,0:T(8,128)(2,1)S(1)}, bf16[256,896]{1,0:T(8,128)(2,1)S(1)}, u32[]{:S(2)}, u32[]{:S(2)}) collective-permute-start(bf16[256,896]{1,0:T(8,128)(2,1)S(1)} %collective-permute-done.28.refs_4_), channel_id=1, source_target_pairs={{0,8},{2,6},{8,16},{10,2},{16,24},{18,10},{24,28},{26,18},{28,20},... | collective-permute-start | bytes 1376264 | tf_op jit(solution)/shard_map/ppermute | solution.py:135
  114.4 12.5 %collective-permute-start.31 = (bf16[256,896]{1,0:T(8,128)(2,1)S(1)}, bf16[256,896]{1,0:T(8,128)(2,1)S(1)}, u32[]{:S(2)}, u32[]{:S(2)}) collective-permute-start(bf16[256,896]{1,0:T(8,128)(2,1)S(1)} %collective-permute-done.28.refs_4_), channel_id=1, source_target_pairs={{0,2},{2,0},{4,6},{6,4},{8,10},{10,8},{12,14},{14,12},{16,18},{18,... | collective-permute-start | bytes 1376264 | tf_op jit(solution)/shard_map/ppermute | solution.py:135
  114.5 12.9 %collective-permute-start.30 = (bf16[256,896]{1,0:T(8,128)(2,1)S(1)}, bf16[256,896]{1,0:T(8,128)(2,1)S(1)}, u32[]{:S(2)}, u32[]{:S(2)}) collective-permute-start(bf16[256,896]{1,0:T(8,128)(2,1)S(1)} %collective-permute-done.21.refs_3_), channel_id=1, source_target_pairs={{0,2},{2,0},{4,6},{6,4},{8,10},{10,8},{12,14},{14,12},{16,18},{18,... | collective-permute-start | bytes 1376264 | tf_op jit(solution)/shard_map/ppermute | solution.py:135
  116.8 12.4 %collective-permute-start.29 = (bf16[256,896]{1,0:T(8,128)(2,1)S(1)}, bf16[256,896]{1,0:T(8,128)(2,1)S(1)}, u32[]{:S(2)}, u32[]{:S(2)}) collective-permute-start(bf16[256,896]{1,0:T(8,128)(2,1)S(1)} %collective-permute-done.25.refs_3_), channel_id=1, source_target_pairs={{0,8},{2,6},{8,16},{10,2},{16,24},{18,10},{24,28},{26,18},{28,20},... | collective-permute-start | bytes 1376264 | tf_op jit(solution)/shard_map/ppermute | solution.py:135
  119.7 11.1 %collective-permute-start.37 = (bf16[256,896]{1,0:T(8,128)(2,1)S(1)}, bf16[256,896]{1,0:T(8,128)(2,1)S(1)}, u32[]{:S(2)}, u32[]{:S(2)}) collective-permute-start(bf16[256,896]{1,0:T(8,128)(2,1)S(1)} %collective-permute-done.32.refs_4_), channel_id=1, source_target_pairs={{0,8},{2,6},{8,16},{10,2},{16,24},{18,10},{24,28},{26,18},{28,20},... | collective-permute-start | bytes 1376264 | tf_op jit(solution)/shard_map/ppermute | solution.py:135
  130.8 11.9 %collective-permute-start.41 = (bf16[256,896]{1,0:T(8,128)(2,1)S(1)}, bf16[256,896]{1,0:T(8,128)(2,1)S(1)}, u32[]{:S(2)}, u32[]{:S(2)}) collective-permute-start(bf16[256,896]{1,0:T(8,128)(2,1)S(1)} %collective-permute-done.37.refs_4_), channel_id=1, source_target_pairs={{0,8},{2,6},{8,16},{10,2},{16,24},{18,10},{24,28},{26,18},{28,20},... | collective-permute-start | bytes 1376264 | tf_op jit(solution)/shard_map/ppermute | solution.py:135
  135.3 14.4 %collective-permute-start.39 = (bf16[256,896]{1,0:T(8,128)(2,1)S(1)}, bf16[256,896]{1,0:T(8,128)(2,1)S(1)}, u32[]{:S(2)}, u32[]{:S(2)}) collective-permute-start(bf16[256,896]{1,0:T(8,128)(2,1)S(1)} %collective-permute-done.29.refs_3_), channel_id=1, source_target_pairs={{0,2},{2,0},{4,6},{6,4},{8,10},{10,8},{12,14},{14,12},{16,18},{18,... | collective-permute-start | bytes 1376264 | tf_op jit(solution)/shard_map/ppermute | solution.py:135
  137.7 13.8 %collective-permute-start.38 = (bf16[256,896]{1,0:T(8,128)(2,1)S(1)}, bf16[256,896]{1,0:T(8,128)(2,1)S(1)}, u32[]{:S(2)}, u32[]{:S(2)}) collective-permute-start(bf16[256,896]{1,0:T(8,128)(2,1)S(1)} %collective-permute-done.34.refs_3_), channel_id=1, source_target_pairs={{0,8},{2,6},{8,16},{10,2},{16,24},{18,10},{24,28},{26,18},{28,20},... | collective-permute-start | bytes 1376264 | tf_op jit(solution)/shard_map/ppermute | solution.py:135
  142.7 10.0 %collective-permute-start.46 = (bf16[256,896]{1,0:T(8,128)(2,1)S(1)}, bf16[256,896]{1,0:T(8,128)(2,1)S(1)}, u32[]{:S(2)}, u32[]{:S(2)}) collective-permute-start(bf16[256,896]{1,0:T(8,128)(2,1)S(1)} %collective-permute-done.41.refs_4_), channel_id=1, source_target_pairs={{0,8},{2,6},{8,16},{10,2},{16,24},{18,10},{24,28},{26,18},{28,20},... | collective-permute-start | bytes 1376264 | tf_op jit(solution)/shard_map/ppermute | solution.py:135
  144.2 17.5 %collective-permute-start.45 = (bf16[256,896]{1,0:T(8,128)(2,1)S(1)}, bf16[256,896]{1,0:T(8,128)(2,1)S(1)}, u32[]{:S(2)}, u32[]{:S(2)}) collective-permute-start(bf16[256,896]{1,0:T(8,128)(2,1)S(1)} %collective-permute-done.41.refs_4_), channel_id=1, source_target_pairs={{0,2},{2,0},{4,6},{6,4},{8,10},{10,8},{12,14},{14,12},{16,18},{18,... | collective-permute-start | bytes 1376264 | tf_op jit(solution)/shard_map/ppermute | solution.py:135
  144.2 17.5 %collective-permute-start.44 = (bf16[256,896]{1,0:T(8,128)(2,1)S(1)}, bf16[256,896]{1,0:T(8,128)(2,1)S(1)}, u32[]{:S(2)}, u32[]{:S(2)}) collective-permute-start(bf16[256,896]{1,0:T(8,128)(2,1)S(1)} %collective-permute-done.34.refs_3_), channel_id=1, source_target_pairs={{0,2},{2,0},{4,6},{6,4},{8,10},{10,8},{12,14},{14,12},{16,18},{18,... | collective-permute-start | bytes 1376264 | tf_op jit(solution)/shard_map/ppermute | solution.py:135
  151.5 13.9 %collective-permute-start.42 = (bf16[256,896]{1,0:T(8,128)(2,1)S(1)}, bf16[256,896]{1,0:T(8,128)(2,1)S(1)}, u32[]{:S(2)}, u32[]{:S(2)}) collective-permute-start(bf16[256,896]{1,0:T(8,128)(2,1)S(1)} %collective-permute-done.38.refs_3_), channel_id=1, source_target_pairs={{0,8},{2,6},{8,16},{10,2},{16,24},{18,10},{24,28},{26,18},{28,20},... | collective-permute-start | bytes 1376264 | tf_op jit(solution)/shard_map/ppermute | solution.py:135
  152.7 12.7 %collective-permute-start.48 = (bf16[256,896]{1,0:T(8,128)(2,1)S(1)}, bf16[256,896]{1,0:T(8,128)(2,1)S(1)}, u32[]{:S(2)}, u32[]{:S(2)}) collective-permute-start(bf16[256,896]{1,0:T(8,128)(2,1)S(1)} %collective-permute-done.46.refs_4_), channel_id=1, source_target_pairs={{0,8},{2,6},{8,16},{10,2},{16,24},{18,10},{24,28},{26,18},{28,20},... | collective-permute-start | bytes 1376264 | tf_op jit(solution)/shard_map/ppermute | solution.py:135
  154.0 10.0 %collective-permute-start.43 = (bf16[384,512]{1,0:T(8,128)(2,1)S(1)}, bf16[384,512]{1,0:T(8,128)(2,1)S(1)}, u32[]{:S(2)}, u32[]{:S(2)}) collective-permute-start(bf16[384,512]{1,0:T(8,128)(2,1)S(1)} %get-tuple-element.202), channel_id=1, source_target_pairs={{0,1},{1,0},{2,3},{3,2},{4,5},{5,4},{6,7},{7,6},{8,9},{9,8},{10,11... | collective-permute-start | bytes 1179656 | tf_op jit(solution)/shard_map/ppermute | solution.py:275
  (24 other events, 212.8 us)
